TPU v7x, 32 devices: a whole 2x2x4 slice. The times are simulated.
32 devices in a mesh: ex: 8 (over z, y), ez: 4 (over x, core).
Axes of the slice: x: 2, y: 2, z: 4, core: 2. Of those that a mesh axis runs over, the one named last changes fastest.
Arguments:
- potential: float32 [64, 16, 32], P('ex', None, 'ez'), may hold values from -1.5 to 0.5
- basis_start: bfloat16 [8, 4, 2, 1728, 128], P('ex', 'ez'), may hold values from -6 to 6
Outputs:
- diagonal_blocks: float32 [8, 128, 4, 2, 128], P('ex', 'ez')
- coupling_blocks: float32 [8, 128, 4, 2, 3, 128], P('ex', 'ez')
All inputs are finite; a program needn't handle non-finite values.
Results may differ from a plain program's by a relative error of at most 0.0003.
Values sent between devices are 32-bit elements; how exact they have to be, the bound alone decides.
No kernel may reach another device: no remote copies, remote signals or barrier semaphores. Data moves between devices by JAX's collectives and lax.ppermute only.
A program may use at most 64 MiB of HBM per device.

v0:
```python
import jax
import jax.numpy as jnp
from jax import lax
from jax.sharding import PartitionSpec as P

G = 8
FILTER = 3


center = 6.5
halfwidth = 5.5
penalty = 1.0
highest = lax.Precision.HIGHEST


def padded_2(cells, sides, width):
    for axis, dim in sides:
        count = lax.axis_size(axis)
        head = lax.slice_in_dim(cells, 0, width, axis=dim)
        tail = lax.slice_in_dim(cells, cells.shape[dim] - width, cells.shape[dim], axis=dim)
        cells = jnp.concatenate(
            [
                lax.ppermute(tail, axis, [(i, (i + 1) % count) for i in range(count)]),
                cells,
                lax.ppermute(head, axis, [((i + 1) % count, i) for i in range(count)]),
            ],
            axis=dim,
        )
    return cells


def from_behind(block, axis, distance):
    devices = range(lax.axis_size(axis))
    route = [((i - distance) % len(devices), i) for i in devices]
    return lax.ppermute(block, axis, route)


def apply_hamiltonian(field, potential_box):
    padded = jnp.pad(field, ((1, 1), (1, 1), (1, 1), (0, 0)))
    beside = padded[2:, 1:-1, 1:-1] + padded[:-2, 1:-1, 1:-1]
    beside = beside + padded[1:-1, 2:, 1:-1] + padded[1:-1, :-2, 1:-1]
    beside = beside + padded[1:-1, 1:-1, 2:] + padded[1:-1, 1:-1, :-2]
    return 3.0 * field - 0.5 * beside + potential_box[:, :, :, None] * field


def local_basis(initial, potential_box):
    box_side = potential_box.shape[0]
    margin = (box_side - G) // 2
    columns = initial.shape[-1]
    previous = initial.astype(jnp.float32).reshape(box_side, box_side, box_side, columns)
    current = (apply_hamiltonian(previous, potential_box) - center * previous) / halfwidth
    for iteration in range(FILTER - 1):
        following = (
            2.0 / halfwidth * (apply_hamiltonian(current, potential_box) - center * current)
            - previous
        )
        previous, current = (current, following)
    flattened = current.reshape(box_side**3, columns)
    intersection = lax.dot_general(
        flattened,
        flattened,
        (((0,), (0,)), ((), ())),
        precision=highest,
        preferred_element_type=jnp.float32,
    )
    factor = jnp.linalg.cholesky(intersection)
    interior = current[margin : margin + G, margin : margin + G, margin : margin + G].reshape(
        G**3, columns
    )
    solved = jax.scipy.linalg.solve_triangular(factor, interior.T, lower=True)
    return solved.T.reshape(G, G, G, columns)


def forward_difference(basis, dimension):
    differences = jnp.diff(basis, axis=dimension)
    widths = [(0, 0)] * basis.ndim
    widths[dimension] = (0, 1)
    return jnp.pad(differences, widths)


def volume_terms(basis, inner_potential):
    gradients = [forward_difference(basis, dimension) for dimension in (1, 2, 3)]
    weighted = jnp.concatenate(
        [
            0.5 * gradients[0],
            0.5 * gradients[1],
            0.5 * gradients[2],
            inner_potential[..., None] * basis,
        ],
        axis=1,
    )
    plain_side = jnp.concatenate(gradients + [basis], axis=1)
    elements = basis.shape[0]
    columns = basis.shape[-1]
    weighted = weighted.reshape(elements, -1, columns)
    plain_side = plain_side.reshape(elements, -1, columns)
    return jnp.einsum("epi,epj->iej", weighted, plain_side, precision=highest)


def face_traces(basis):
    points = basis.shape[1]
    elements = basis.shape[0]
    columns = basis.shape[-1]
    plus_layers = []
    minus_layers = []
    for dimension in (1, 2, 3):
        outer_last = lax.index_in_dim(basis, points - 1, dimension, keepdims=False)
        inner_last = lax.index_in_dim(basis, points - 2, dimension, keepdims=False)
        outer_first = lax.index_in_dim(basis, 0, dimension, keepdims=False)
        inner_first = lax.index_in_dim(basis, 1, dimension, keepdims=False)
        plus_layers.append(jnp.stack([outer_last, outer_last - inner_last], axis=1))
        minus_layers.append(jnp.stack([outer_first, inner_first - outer_first], axis=1))
    plus_traces = jnp.stack(plus_layers, axis=1).reshape(elements, 3, 2, points * points, columns)
    minus_traces = jnp.stack(minus_layers, axis=1).reshape(elements, 3, 2, points * points, columns)
    return (plus_traces, minus_traces)


def face_diagonal(plus_traces, minus_traces):
    side_plus = -0.25 * plus_traces[:, :, 1] + 0.5 * penalty * plus_traces[:, :, 0]
    side_minus = 0.25 * minus_traces[:, :, 1] + 0.5 * penalty * minus_traces[:, :, 0]
    direct = jnp.einsum("ekpi,ekpj->iej", side_plus, plus_traces[:, :, 0], precision=highest)
    direct = direct + jnp.einsum(
        "ekpi,ekpj->iej", side_minus, minus_traces[:, :, 0], precision=highest
    )
    mirror = jnp.einsum("ekpi,ekpj->iej", plus_traces[:, :, 0], side_plus, precision=highest)
    mirror = mirror + jnp.einsum(
        "ekpi,ekpj->iej", minus_traces[:, :, 0], side_minus, precision=highest
    )
    return direct + mirror


def coupling(plus_traces, next_traces):
    weighted = 0.25 * plus_traces[:, :, 1] - penalty * plus_traces[:, :, 0]
    result = jnp.einsum("ekpi,ekpj->iekj", weighted, next_traces[:, :, 0], precision=highest)
    return result - 0.25 * jnp.einsum(
        "ekpi,ekpj->iekj", plus_traces[:, :, 0], next_traces[:, :, 1], precision=highest
    )


def local(potential, basis_start):
    y_elements = basis_start.shape[2]
    columns = basis_start.shape[-1]
    margin = G // 4
    box_side = G + 2 * margin
    extended = padded_2(potential, (("ex", 0), ("ez", 2)), margin)
    extended = jnp.concatenate([extended[:, -margin:], extended, extended[:, :margin]], axis=1)
    starts = basis_start.reshape(y_elements, box_side**3, columns)

    def one_element(element):
        initial = lax.dynamic_index_in_dim(starts, element, 0, keepdims=False)
        potential_box = lax.dynamic_slice_in_dim(extended, element * G, box_side, 1)
        return local_basis(initial, potential_box)

    basis = lax.map(one_element, jnp.arange(y_elements, dtype=jnp.int32))
    inner_potential = potential.reshape(G, y_elements, G, G).transpose(1, 0, 2, 3)
    plus_traces, minus_traces = face_traces(basis)
    diagonal = volume_terms(basis, inner_potential) + face_diagonal(plus_traces, minus_traces)
    diagonal = diagonal[None, :, None]
    from_x = from_behind(minus_traces[:, 0], "ex", -1)
    from_z = from_behind(minus_traces[:, 2], "ez", -1)
    from_y = jnp.roll(minus_traces[:, 1], -1, axis=0)
    next_traces = jnp.stack([from_x, from_y, from_z], axis=1)
    coupled = coupling(plus_traces, next_traces)[None, :, None]
    diagonal_rows, coupling_rows = (
        lax.all_to_all(diagonal, "ez", split_axis=1, concat_axis=2, tiled=True),
        lax.all_to_all(coupled, "ez", split_axis=1, concat_axis=2, tiled=True),
    )
    return (diagonal_rows, coupling_rows)


def solution(mesh):
    return jax.shard_map(
        local,
        mesh=mesh,
        in_specs=(P("ex", None, "ez"), P("ex", "ez", None, None, None)),
        out_specs=(P("ex", "ez", None, None, None), P("ex", "ez", None, None, None, None)),
        check_vma=False,
    )
```

profile of v0, /device:TPU:0, one launch (start us, length us, event | category | flops | bytes accessed | tf_op | source)
XLA Modules:
  0.0 115.4 jit_solution(8388356382391876310)
XLA Ops:
  0.6 0.8 copy.51
  1.5 3.0 %collective-permute-start = (f32[2,16,8]{2,1,0:T(8,128)S(1)}, f32[2,16,8]{2,1,0:T(8,128)S(1)}, u32[]{:S(2)}, u32[]{:S(2)}) collective-permute-start(f32[2,16,8]{2,1,0:T(8,128)S(1)} %get-tuple-element.114), channel_id=1, source_target_pairs={{0,4},{4,8},{8,12},{12,16},{16,20},{20,24},{24,28},{28,0},{1,5},{5... | collective-permute-start | bytes 3080 | tf_op jit(solution)/shard_map/ppermute | solution.py:23
  4.5 3.1 %collective-permute-start.1 = (f32[2,16,8]{2,1,0:T(8,128)S(1)}, f32[2,16,8]{2,1,0:T(8,128)S(1)}, u32[]{:S(2)}, u32[]{:S(2)}) collective-permute-start(f32[2,16,8]{2,1,0:T(8,128)S(1)} %get-tuple-element.115), channel_id=1, source_target_pairs={{4,0},{8,4},{12,8},{16,12},{20,16},{24,20},{28,24},{0,28},{5,1},{9... | collective-permute-start | bytes 3080 | tf_op jit(solution)/shard_map/ppermute | solution.py:25
  7.6 1.7 %collective-permute-done = f32[2,16,8]{2,1,0:T(8,128)S(1)} collective-permute-done((f32[2,16,8]{2,1,0:T(8,128)S(1)}, f32[2,16,8]{2,1,0:T(8,128)S(1)}, u32[]{:S(2)}, u32[]{:S(2)}) %collective-permute-start) | collective-permute-done | bytes 1056 | tf_op jit(solution)/shard_map/ppermute | solution.py:23
  9.3 0.0 collective-permute-done.1
  9.3 0.1 fusion.73
  9.4 0.1 collective-permute-start.2
  9.4 1.7 %collective-permute-start.3 = (f32[12,16,2]{2,1,0:T(8,128)S(1)}, f32[12,16,2]{2,1,0:T(8,128)S(1)}, u32[]{:S(2)}, u32[]{:S(2)}) collective-permute-start(f32[12,16,2]{2,1,0:T(8,128)S(1)} %get-tuple-element.113), channel_id=1, source_target_pairs={{1,0},{2,1},{3,2},{0,3},{5,4},{6,5},{7,6},{4,7},{9,8},{10,9},{11,1... | collective-permute-start | bytes 4616 | tf_op jit(solution)/shard_map/ppermute | solution.py:25
  11.2 0.9 reshape.199
  12.0 0.1 copy.54
  12.1 1.3 %collective-permute-done.2 = f32[12,16,2]{2,1,0:T(8,128)S(1)} collective-permute-done((f32[12,16,2]{2,1,0:T(8,128)S(1)}, f32[12,16,2]{2,1,0:T(8,128)S(1)}, u32[]{:S(2)}, u32[]{:S(2)}) %collective-permute-start.2) | collective-permute-done | bytes 1568 | tf_op jit(solution)/shard_map/ppermute | solution.py:23
  13.5 0.2 collective-permute-done.3
  13.7 0.2 fusion.47
  13.9 66.3 %while.12 = (s32[]{:T(128)}, f32[2,8,8,8,128]{4,3,2,1,0:T(8,128)S(1)}, s32[2]{0:T(128)S(1)}, bf16[2,1728,128]{2,1,0:T(8,128)(2,1)}, f32[12,20,12]{2,1,0:T(8,128)...) while((s32[]{:T(128)}, f32[2,8,8,8,128]{4,3,2,1,0:T(8,128)S(1)}, s32[2]{0:T(128)S(1)}, ...), condition=%wide.region_3.4_spmd, body=%wide.region_0.3_spmd.sunk | while | flops 450062144 | bytes 14051031 | solution.py:154
  13.9 0.6 dynamic_slice.26
  17.1 1.1 dynamic-slice_convert_fusion.2
  18.2 0.1 reshape.209
  18.3 1.0 broadcast_multiply_fusion.9
  19.3 1.2 fusion.95
  20.5 1.2 %fusion.96 = f32[12,12,12,128]{3,2,1,0:T(8,128)S(1)} fusion(f32[12,12,12,128]{3,2,1,0:T(8,128)S(1)} %fusion.95, f32[12,12,12,128]{3,2,1,0:T(8,128)S(1)} %get-tuple-element.158, f32[12,12,12]{2,1,0:T(8,128)S(1)} %get-tuple-element.156), kind=kLoop, calls=%fused_computation.48.clone.1 | loop fusion | flops 3317760 | bytes 2661120 | tf_op jit(solution)/shard_map/while/body/eval_jaxpr/sub | solution.py:54
  21.7 2.0 %convolution_bitcast_fusion.7 = f32[128,128]{1,0:T(8,128)S(1)} fusion(f32[12,12,12,128]{3,2,1,0:T(8,128)S(1)} %fusion.96), kind=kOutput, calls=%fused_computation.51.clone.1 | convolution fusion | flops 339738624 | bytes 950272 | tf_op jit(solution)/shard_map/while/body/eval_jaxpr/dot_general | solution.py:59
  23.7 0.1 copy.84
  23.8 11.7 %cholesky.58 = f32[128,128]{1,0:T(8,128)S(1)} custom-call(f32[128,128]{1,0:T(8,128)S(1)} %fusion.97), custom_call_target="Cholesky" | custom-call | tf_op jit(solution)/shard_map/while/body/eval_jaxpr/jit(cholesky)/cholesky | solution.py:66
  35.6 0.6 compare_reduce_fusion.2
  36.2 0.7 fusion.98
  36.9 9.8 %custom-call.15 = f32[1,128,128]{1,2,0:T(8,128)S(1)} custom-call(f32[1,128,128]{2,1,0:T(8,128)S(1)} %fusion.98), custom_call_target="InvertDiagBlocksLowerTriangular" | custom-call | tf_op jit(solution)/shard_map/while/body/eval_jaxpr/jit(_solve_triangular)/triangular_solve | solution.py:70
  46.7 0.4 fusion.99
  47.1 0.6 dynamic_slice.26
  50.3 1.1 dynamic-slice_convert_fusion.2
  51.4 0.1 reshape.209
  51.5 1.0 broadcast_multiply_fusion.9
  52.5 1.2 fusion.95
  53.7 1.2 %fusion.96 = f32[12,12,12,128]{3,2,1,0:T(8,128)S(1)} fusion(f32[12,12,12,128]{3,2,1,0:T(8,128)S(1)} %fusion.95, f32[12,12,12,128]{3,2,1,0:T(8,128)S(1)} %get-tuple-element.158, f32[12,12,12]{2,1,0:T(8,128)S(1)} %get-tuple-element.156), kind=kLoop, calls=%fused_computation.48.clone.1 | loop fusion | flops 3317760 | bytes 2661120 | tf_op jit(solution)/shard_map/while/body/eval_jaxpr/sub | solution.py:54
  54.8 2.0 %convolution_bitcast_fusion.7 = f32[128,128]{1,0:T(8,128)S(1)} fusion(f32[12,12,12,128]{3,2,1,0:T(8,128)S(1)} %fusion.96), kind=kOutput, calls=%fused_computation.51.clone.1 | convolution fusion | flops 339738624 | bytes 950272 | tf_op jit(solution)/shard_map/while/body/eval_jaxpr/dot_general | solution.py:59
  56.9 0.1 copy.84
  57.0 11.7 %cholesky.58 = f32[128,128]{1,0:T(8,128)S(1)} custom-call(f32[128,128]{1,0:T(8,128)S(1)} %fusion.97), custom_call_target="Cholesky" | custom-call | tf_op jit(solution)/shard_map/while/body/eval_jaxpr/jit(cholesky)/cholesky | solution.py:66
  68.7 0.6 compare_reduce_fusion.2
  69.4 0.7 fusion.98
  70.0 9.8 %custom-call.15 = f32[1,128,128]{1,2,0:T(8,128)S(1)} custom-call(f32[1,128,128]{2,1,0:T(8,128)S(1)} %fusion.98), custom_call_target="InvertDiagBlocksLowerTriangular" | custom-call | tf_op jit(solution)/shard_map/while/body/eval_jaxpr/jit(_solve_triangular)/triangular_solve | solution.py:70
  79.9 0.4 fusion.99
  80.3 0.2 fusion.72
  80.6 0.1 maximum_maximum_fusion
  80.7 0.7 convolution_bitcast_fusion.4
  81.4 0.7 convolution_bitcast_fusion.2
  82.1 0.1 slice_subtract_fusion
  82.2 2.0 %collective-permute-start.5 = (f32[2,2,64,128]{3,2,0,1:T(8,128)S(1)}, f32[2,2,64,128]{3,2,0,1:T(8,128)S(1)}, u32[]{:S(2)}, u32[]{:S(2)}) collective-permute-start(f32[2,2,64,128]{3,2,0,1:T(8,128)S(1)} %pad_maximum_fusion.13), channel_id=1, source_target_pairs={{1,0},{2,1},{3,2},{0,3},{5,4},{6,5},{7,6},{4,7},{9,8},{10,9},{11,1... | collective-permute-start | bytes 393224 | tf_op jit(solution)/shard_map/ppermute | solution.py:35
  84.2 4.7 %collective-permute-start.4 = (f32[2,2,64,128]{3,2,0,1:T(8,128)S(1)}, f32[2,2,64,128]{3,2,0,1:T(8,128)S(1)}, u32[]{:S(2)}, u32[]{:S(2)}) collective-permute-start(f32[2,2,64,128]{3,2,0,1:T(8,128)S(1)} %get-tuple-element.108), channel_id=1, source_target_pairs={{4,0},{8,4},{12,8},{16,12},{20,16},{24,20},{28,24},{0,28},{5,1},{9... | collective-permute-start | bytes 393224 | tf_op jit(solution)/shard_map/ppermute | solution.py:35
  88.9 0.7 fusion.40
  89.6 0.7 fusion.39
  90.3 0.2 broadcast_multiply_fusion.5
  90.5 0.2 broadcast_multiply_fusion.3
  90.8 0.2 pad_maximum_fusion
  91.0 0.2 pad_maximum_fusion.1
  91.2 3.5 %fusion.37 = f32[1,128,1,2,128]{1,4,3,2,0:T(8,128)S(1)} fusion(f32[2,128,128]{2,1,0:T(8,128)S(1)} %fusion.39, f32[2,2048,128]{2,1,0:T(8,128)S(1)} %bitcast.159, f32[2,2048,128]{2,1,0:T(8,128)S(1)} %bitcast.160), kind=kOutput, calls=%fused_computation.76 | convolution fusion | flops 805339136 | bytes 4456448 | tf_op jit(solution)/shard_map/epi,epj->iej/dot_general | solution.py:97
  94.7 0.8 copy.59
  95.5 3.3 %all-to-all-start = ((f32[1,128,1,2,128]{4,3,2,0,1:T(2,128)}), f32[1,128,1,2,128]{4,3,2,0,1:T(2,128)S(1)}, u32[]{:S(2)}, u32[]{:S(2)}) async-start(f32[1,128,1,2,128]{4,3,2,0,1:T(2,128)} %copy.59), calls=%async_computation | async-start | bytes 262144 | tf_op jit(solution)/shard_map/all_to_all | solution.py:165
  98.9 0.8 convolution_multiply_fusion
  99.7 0.8 fusion.36
  100.5 0.9 copy.62
  101.5 2.0 %all-to-all-done = f32[1,128,1,2,128]{4,3,2,0,1:T(2,128)S(1)} async-done(((f32[1,128,1,2,128]{4,3,2,0,1:T(2,128)}), f32[1,128,1,2,128]{4,3,2,0,1:T(2,128)S(1)}, u32[]{:S(2)}, u32[]{:S(2)}) %all-to-all-start) | async-done | bytes 131104 | tf_op jit(solution)/shard_map/all_to_all | solution.py:165
  103.4 3.5 %all-to-all-start.1 = ((f32[1,128,1,2,3,128]{5,3,4,2,0,1:T(2,128)}), f32[1,128,1,2,3,128]{5,3,4,2,0,1:T(2,128)S(1)}, u32[]{:S(2)}, u32[]{:S(2)}) async-start(f32[1,128,1,2,3,128]{5,3,4,2,0,1:T(2,128)} %copy.62), calls=%async_computation.1 | async-start | bytes 786432 | tf_op jit(solution)/shard_map/all_to_all | solution.py:166
  106.9 0.8 copy.64
  107.7 6.6 %all-to-all-done.1 = f32[1,128,1,2,3,128]{5,3,4,2,0,1:T(2,128)S(1)} async-done(((f32[1,128,1,2,3,128]{5,3,4,2,0,1:T(2,128)}), f32[1,128,1,2,3,128]{5,3,4,2,0,1:T(2,128)S(1)}, u32[]{:S(2)}, u32[]{:S(2)}) %all-to-all-start.1) | async-done | bytes 393248 | tf_op jit(solution)/shard_map/all_to_all | solution.py:166
  114.3 1.1 copy.65
  (30 shorter events, 0.5 us)
Async XLA Ops:
  1.5 7.8 %collective-permute-start = (f32[2,16,8]{2,1,0:T(8,128)S(1)}, f32[2,16,8]{2,1,0:T(8,128)S(1)}, u32[]{:S(2)}, u32[]{:S(2)}) collective-permute-start(f32[2,16,8]{2,1,0:T(8,128)S(1)} %get-tuple-element.114), channel_id=1, source_target_pairs={{0,4},{4,8},{8,12},{12,16},{16,20},{20,24},{24,28},{28,0},{1,5},{5... | collective-permute-start | bytes 3080 | tf_op jit(solution)/shard_map/ppermute | solution.py:23
  4.5 4.8 %collective-permute-start.1 = (f32[2,16,8]{2,1,0:T(8,128)S(1)}, f32[2,16,8]{2,1,0:T(8,128)S(1)}, u32[]{:S(2)}, u32[]{:S(2)}) collective-permute-start(f32[2,16,8]{2,1,0:T(8,128)S(1)} %get-tuple-element.115), channel_id=1, source_target_pairs={{4,0},{8,4},{12,8},{16,12},{20,16},{24,20},{28,24},{0,28},{5,1},{9... | collective-permute-start | bytes 3080 | tf_op jit(solution)/shard_map/ppermute | solution.py:25
  9.4 4.1 %collective-permute-start.2 = (f32[12,16,2]{2,1,0:T(8,128)S(1)}, f32[12,16,2]{2,1,0:T(8,128)S(1)}, u32[]{:S(2)}, u32[]{:S(2)}) collective-permute-start(f32[12,16,2]{2,1,0:T(8,128)S(1)} %get-tuple-element.112), channel_id=1, source_target_pairs={{0,1},{1,2},{2,3},{3,0},{4,5},{5,6},{6,7},{7,4},{8,9},{9,10},{10,1... | collective-permute-start | bytes 4616 | tf_op jit(solution)/shard_map/ppermute | solution.py:23
  9.4 4.3 %collective-permute-start.3 = (f32[12,16,2]{2,1,0:T(8,128)S(1)}, f32[12,16,2]{2,1,0:T(8,128)S(1)}, u32[]{:S(2)}, u32[]{:S(2)}) collective-permute-start(f32[12,16,2]{2,1,0:T(8,128)S(1)} %get-tuple-element.113), channel_id=1, source_target_pairs={{1,0},{2,1},{3,2},{0,3},{5,4},{6,5},{7,6},{4,7},{9,8},{10,9},{11,1... | collective-permute-start | bytes 4616 | tf_op jit(solution)/shard_map/ppermute | solution.py:25
  82.2 16.6 %collective-permute-start.5 = (f32[2,2,64,128]{3,2,0,1:T(8,128)S(1)}, f32[2,2,64,128]{3,2,0,1:T(8,128)S(1)}, u32[]{:S(2)}, u32[]{:S(2)}) collective-permute-start(f32[2,2,64,128]{3,2,0,1:T(8,128)S(1)} %pad_maximum_fusion.13), channel_id=1, source_target_pairs={{1,0},{2,1},{3,2},{0,3},{5,4},{6,5},{7,6},{4,7},{9,8},{10,9},{11,1... | collective-permute-start | bytes 393224 | tf_op jit(solution)/shard_map/ppermute | solution.py:35
  84.2 14.7 %collective-permute-start.4 = (f32[2,2,64,128]{3,2,0,1:T(8,128)S(1)}, f32[2,2,64,128]{3,2,0,1:T(8,128)S(1)}, u32[]{:S(2)}, u32[]{:S(2)}) collective-permute-start(f32[2,2,64,128]{3,2,0,1:T(8,128)S(1)} %get-tuple-element.108), channel_id=1, source_target_pairs={{4,0},{8,4},{12,8},{16,12},{20,16},{24,20},{28,24},{0,28},{5,1},{9... | collective-permute-start | bytes 393224 | tf_op jit(solution)/shard_map/ppermute | solution.py:35
  95.5 7.9 %all-to-all-start = ((f32[1,128,1,2,128]{4,3,2,0,1:T(2,128)}), f32[1,128,1,2,128]{4,3,2,0,1:T(2,128)S(1)}, u32[]{:S(2)}, u32[]{:S(2)}) async-start(f32[1,128,1,2,128]{4,3,2,0,1:T(2,128)} %copy.59), calls=%async_computation | async-start | bytes 262144 | tf_op jit(solution)/shard_map/all_to_all | solution.py:165
  103.4 10.9 %all-to-all-start.1 = ((f32[1,128,1,2,3,128]{5,3,4,2,0,1:T(2,128)}), f32[1,128,1,2,3,128]{5,3,4,2,0,1:T(2,128)S(1)}, u32[]{:S(2)}, u32[]{:S(2)}) async-start(f32[1,128,1,2,3,128]{5,3,4,2,0,1:T(2,128)} %copy.62), calls=%async_computation.1 | async-start | bytes 786432 | tf_op jit(solution)/shard_map/all_to_all | solution.py:166
where the time goes:
time: 116 us; the launch traced here: 115 us
  other arithmetic  56.1 us (48%)
  starting transfers between devices  21.4 us (18%)
  matrix products  12.6 us (11%)
  waiting for transfers between devices  11.8 us (10%)
  local copies, waits for them, and re-layouts  7.09 us (6%)
  loops' own time  5.39 us (5%)
    another operation x6, other arithmetic, local_basis(): factor = jnp.linalg.cholesky(intersection)  24.8 us
    another operation x4, other arithmetic, local_basis(): solved = jax.scipy.linalg.solve_triangular(factor, interior.T, lower=True)  20.9 us
    ppermute x2, starting transfers between devices, from_behind(): return lax.ppermute(block, axis, route)  6.68 us
    all_to_all x1, waiting for transfers between devices, local(): lax.all_to_all(coupled, 'ez', split_axis=1, concat_axis=2, tiled=True)  6.63 us
    another operation x1, loops' own time, local(): basis = lax.map(one_element, jnp.arange(y_elements, dtype=jnp.int32))  5.39 us
    ppermute x2, starting transfers between devices, padded_2(): lax.ppermute(head, axis, [((i + 1) % count, i) for i in range(count)])  4.84 us
    sub x4, other arithmetic, local_basis(): 2.0 / halfwidth  4.64 us
    dot_general x2, matrix products, local_basis(): lax.dot_general(flattened, flattened, (((0,), (0,)), ((), ())), precision...  4.06 us
  transfers between devices with their start and end apart: 8, of which 5 were waited for; matrix products, arithmetic and copies ran while one was open for 9% of the time, Pallas kernels for 0%

commit v1 on v0

v1 whole, which is shorter than its diff:
```python
import functools

import jax
import jax.numpy as jnp
from jax import lax
from jax.experimental import pallas as pl
from jax.experimental.pallas import tpu as pltpu
from jax.sharding import PartitionSpec as P

G = 8
FILTER = 3

center = 6.5
halfwidth = 5.5

f32 = jnp.float32
bf16 = jnp.bfloat16

LEAD = 8
COL = 16
BLOCK = 8


def split(value):
    high = value.astype(bf16)
    return high, (value - high.astype(f32)).astype(bf16)


def product(a, b, dims):
    dims = (dims, ((), ()))
    dot = functools.partial(lax.dot_general, dimension_numbers=dims, preferred_element_type=f32)
    return dot(a[0], b[0]) + (dot(a[0], b[1]) + dot(a[1], b[0]))


NN = ((1,), (0,))
NT = ((1,), (1,))
TN = ((0,), (0,))


def bcast_row(value, k):
    return jnp.broadcast_to(value[k : k + 1, :], value.shape)


def bcast_lane(value, k, lanes):
    return jnp.broadcast_to(value[:, k : k + 1], (value.shape[0], lanes))


def inverse_factors(matrix_ref, inverse_ref):
    count, size, width = matrix_ref.shape
    row = lax.broadcasted_iota(jnp.int32, (BLOCK, size), 0)
    for start in range(0, size, BLOCK):
        rows = slice(start, start + BLOCK)
        solved = []
        for e in range(count):
            panel = [matrix_ref[e, rows, :size], matrix_ref[e, rows, size:]]
            columns = [bcast_lane(panel[0], start + j, size) for j in range(BLOCK)]
            kept = jnp.zeros_like(panel[1])
            pivots = jnp.ones_like(panel[1])
            for k in range(BLOCK):
                here = row == k
                pivot = bcast_row(columns[k], k)
                reciprocal = 1.0 / pivot
                kept = jnp.where(here, panel[1], kept)
                pivots = jnp.where(here, pivot, pivots)
                for j in range(k + 1, BLOCK):
                    scaled = bcast_row(columns[j], k) * reciprocal
                    columns[j] = jnp.where(here, scaled, columns[j] - columns[k] * scaled)
                for part in range(2):
                    scaled = bcast_row(panel[part], k) * reciprocal
                    panel[part] = jnp.where(here, scaled, panel[part] - columns[k] * scaled)
            inverse_ref[e, rows, :] = kept * lax.rsqrt(pivots)
            solved.append(panel)
        for below in range(start + BLOCK, size, BLOCK):
            for e in range(count):
                left = matrix_ref[e, below : below + BLOCK, :size]
                right = matrix_ref[e, below : below + BLOCK, size:]
                factors = [bcast_lane(left, start + k, size) for k in range(BLOCK)]
                for k in range(BLOCK):
                    left = left - factors[k] * bcast_row(solved[e][0], k)
                    right = right - factors[k] * bcast_row(solved[e][1], k)
                matrix_ref[e, below : below + BLOCK, :size] = left
                matrix_ref[e, below : below + BLOCK, size:] = right


def basis_kernel(
    elements,
    side,
    own_ref,
    x_before_ref,
    x_after_ref,
    z_before_ref,
    z_after_ref,
    start_ref,
    minus_x_ref,
    minus_z_ref,
    plus_ref,
    near_ref,
    box_ref,
    scaled_ref,
    flat_ref,
    field_a,
    field_b,
    pair_ref,
    inner_ref,
    applied_ref,
    matrix_ref,
    inverse_ref,
):
    margin = (side - G) // 2
    columns = start_ref.shape[-1]
    y_points = own_ref.shape[-1]
    slab = side * side

    box_ref[...] = jnp.zeros_like(box_ref)
    inner = slice(margin, margin + G)
    box_ref[inner, inner, :y_points] = own_ref[...]
    box_ref[:margin, inner, :y_points] = x_before_ref[...]
    box_ref[margin + G :, inner, :y_points] = x_after_ref[...]
    box_ref[:, :margin, :y_points] = z_before_ref[...]
    box_ref[:, margin + G : side, :y_points] = z_after_ref[...]

    for ref in (field_a, field_b):
        for e in range(elements):
            ref[e, 0] = jnp.zeros(ref.shape[2:], f32)
            ref[e, side + 1] = jnp.zeros(ref.shape[2:], f32)
    inside = lax.broadcasted_iota(jnp.int32, (COL, columns), 0) < side
    zero_rows = jnp.zeros((LEAD, columns), f32)

    def prepare(x, carry):
        rows = box_ref[x]
        for y in range(y_points):
            scaled_ref[x, y] = (bcast_lane(rows, y, columns) + (3.0 - center)) * (1.0 / halfwidth)
        for e in range(elements):
            flat_ref[:slab] = start_ref[e, pl.ds(pl.multiple_of(x * slab, 16), slab), :].astype(f32)
            for y in range(side):
                value = jnp.where(inside, flat_ref[side * y : side * y + COL], 0.0)
                field_a[e, x + 1, LEAD + COL * y : LEAD + COL * (y + 1)] = value
            for ref in (field_a, field_b):
                ref[e, x + 1, :LEAD] = zero_rows
                ref[e, x + 1, LEAD + COL * side :] = zero_rows
        return carry

    lax.fori_loop(0, side, prepare, 0)

    def sweep(source, target, first, last):
        def at_x(x, carry):
            for e in range(elements):

                def column(y):
                    return source[e, x + 1, LEAD + COL * y : LEAD + COL * (y + 1)]

                before, here = None, column(0)
                for y in range(side):
                    low = LEAD + COL * y
                    after = column(y + 1) if y + 1 < side else None
                    beside = source[e, x, low : low + COL] + source[e, x + 2, low : low + COL]
                    beside = beside + (
                        source[e, x + 1, low - 1 : low - 1 + COL]
                        + source[e, x + 1, low + 1 : low + 1 + COL]
                    )
                    if before is not None:
                        beside = beside + before
                    if after is not None:
                        beside = beside + after
                    y_point = (e * G - margin + y) % y_points
                    value = scaled_ref[x, y_point] * here - (0.5 / halfwidth) * beside
                    if not first:
                        value = (value + value) - target[e, x + 1, low : low + COL]
                    value = jnp.where(inside, value, 0.0)
                    target[e, x + 1, low : low + COL] = value
                    if last:
                        high, rest = split(value)
                        at = pl.multiple_of(x * (side * COL), COL) + COL * y
                        pair_ref[e, pl.ds(at, COL), :columns] = high
                        pair_ref[e, pl.ds(at, COL), columns:] = rest
                    before, here = here, after
            return carry

        lax.fori_loop(0, side, at_x, 0)

    fields = (field_a, field_b)
    for step in range(FILTER):
        sweep(fields[step % 2], fields[(step + 1) % 2], step == 0, step == FILTER - 1)
    field = fields[FILTER % 2]

    identity = (
        lax.broadcasted_iota(jnp.int32, (columns, columns), 0)
        == lax.broadcasted_iota(jnp.int32, (columns, columns), 1)
    ).astype(f32)
    for e in range(elements):
        both = lax.dot_general(
            pair_ref[e, :, :columns], pair_ref[e], (TN, ((), ())), preferred_element_type=f32
        )
        cross = both[:, columns:]
        matrix_ref[e, :, :columns] = both[:, :columns] + (cross + cross.T)
        matrix_ref[e, :, columns:] = identity

    inverse_factors(matrix_ref, inverse_ref)

    z = lax.broadcasted_iota(jnp.int32, (G, columns), 0)
    edge = (z == 1) | (z == G - 1)
    weight_down = jnp.where(z == 0, 0.0, jnp.where(edge, 0.25, 0.5))
    edge = (z == 0) | (z == G - 2)
    weight_up = jnp.where(z == G - 1, 0.0, jnp.where(edge, 0.25, 0.5))

    def link(i):
        return 0.25 if i in (0, G - 2) else 0.5

    def point_rows(e, x, y):
        low = LEAD + COL * (margin + y) + margin
        return field[e, margin + x + 1, low : low + G]

    for e in range(elements):
        for x in range(G):
            for y in range(0, G, 2):
                inner_pair, applied_pair = [], []
                for yy in (y, y + 1):
                    here = point_rows(e, x, yy)
                    potential = scaled_ref[margin + x, (e * G + yy) % y_points, margin : margin + G]
                    value = (halfwidth * potential + center) * here
                    value = value - weight_down * pltpu.roll(here, 1, 0)
                    value = value - weight_up * pltpu.roll(here, G - 1, 0)
                    if x > 0:
                        value = value - link(x - 1) * point_rows(e, x - 1, yy)
                    if x < G - 1:
                        value = value - link(x) * point_rows(e, x + 1, yy)
                    if yy > 0:
                        value = value - link(yy - 1) * point_rows(e, x, yy - 1)
                    if yy < G - 1:
                        value = value - link(yy) * point_rows(e, x, yy + 1)
                    inner_pair.append(here)
                    applied_pair.append(value)
                at = slice((x * G + y) * G, (x * G + y + 2) * G)
                for ref, pair in ((inner_ref, inner_pair), (applied_ref, applied_pair)):
                    high, rest = split(jnp.concatenate(pair, axis=0))
                    ref[e, at, :columns] = high
                    ref[e, at, columns:] = rest

    def layer(e, d, i):
        if d == 0:
            return [point_rows(e, i, y) for y in range(G)]
        if d == 1:
            return [point_rows(e, x, i) for x in range(G)]
        low = LEAD + COL * margin + margin + i
        return [field[e, margin + x + 1, pl.ds(low, G, stride=COL)] for x in range(G)]

    minus, plus, inverse = [], [], []
    for e in range(elements):
        inverse.append(split(inverse_ref[e]))
        minus_rows, plus_rows = [], []
        for d in range(3):
            minus_rows += layer(e, d, 0) + layer(e, d, 1)
            last, inside_last = layer(e, d, G - 1), layer(e, d, G - 2)
            plus_rows += [-(0.5 * a + 0.25 * b) for a, b in zip(last, inside_last)]
            plus_rows += [-0.25 * a for a in last]
        minus.append(product(split(jnp.concatenate(minus_rows, 0)), inverse[e], NT))
        plus.append(product(inverse[e], split(jnp.concatenate(plus_rows, 0)), NT))

    face = 2 * G * G
    for e in range(elements):
        minus_x_ref[e] = minus[e][:face]
        minus_z_ref[e] = minus[e][2 * face :]
        plus_ref[e, 0] = plus[e][:, :face]
        plus_ref[e, 1] = plus[e][:, 2 * face :]
        both = lax.dot_general(
            inner_ref[e, :, :columns], applied_ref[e], (TN, ((), ())), preferred_element_type=f32
        )
        raw = both[:, :columns] + both[:, columns:]
        raw = raw + lax.dot_general(
            inner_ref[e, :, columns:],
            applied_ref[e, :, :columns],
            (TN, ((), ())),
            preferred_element_type=f32,
        )
        half = product(inverse[e], split(raw), NN)
        near_ref[0, e] = product(split(half), inverse[e], NT)
        following = minus[(e + 1) % elements][face : 2 * face]
        near_ref[1, e] = product(split(plus[e][:, face : 2 * face]), split(following), NN)


def coupling_kernel(count, plus_ref, next_x_ref, next_z_ref, near_ref, *rest):
    out_refs, far_ref = rest[:-1], rest[-1]
    elements = plus_ref.shape[0]
    rows = plus_ref.shape[2] // count
    me = lax.axis_index("ez")
    for e in range(elements):
        for d, ref in ((0, next_x_ref), (1, next_z_ref)):
            far_ref[d, e] = product(split(plus_ref[e, d]), split(ref[e]), NN)
    for step in range(count):
        at = pl.ds(pl.multiple_of(lax.rem(me + step, count) * rows, rows), rows)
        for e in range(elements):
            for slot, (ref, d) in enumerate(
                ((near_ref, 0), (far_ref, 0), (near_ref, 1), (far_ref, 1))
            ):
                out_refs[step][:, elements * slot + e, :] = ref[d, e, at, :]


def assemble_kernel(count, *refs):
    in_refs, diagonal_ref, coupling_ref = refs[:count], refs[count], refs[count + 1]
    elements = diagonal_ref.shape[2]
    me = lax.axis_index("ez")
    for step in range(count):
        z = lax.rem(me + (count - step), count)
        diagonal_ref[:, z] = in_refs[step][:, :elements]
        coupling_ref[:, z] = in_refs[step][:, elements:]


def vmem(count):
    return [pl.BlockSpec(memory_space=pltpu.VMEM)] * count


def shift(block, axis, distance):
    count = lax.axis_size(axis)
    return lax.ppermute(block, axis, [(i, (i + distance) % count) for i in range(count)])


def local(potential, basis_start):
    elements, points, columns = basis_start.shape[2:]
    side = round(points ** (1 / 3))
    margin = (side - G) // 2
    y_points = potential.shape[1]
    count = lax.axis_size("ez")
    starts = basis_start.reshape(elements, points, columns)
    own = potential.transpose(0, 2, 1)
    x_before = shift(own[G - margin :], "ex", 1)
    x_after = shift(own[:margin], "ex", -1)
    tall = jnp.concatenate([x_before, own, x_after], axis=0)
    z_before = shift(tall[:, G - margin :], "ez", 1)
    z_after = shift(tall[:, :margin], "ez", -1)

    face = 2 * G * G
    shape = jax.ShapeDtypeStruct
    minus_x, minus_z, plus, near = pl.pallas_call(
        functools.partial(basis_kernel, elements, side),
        out_shape=[
            shape((elements, face, columns), f32),
            shape((elements, face, columns), f32),
            shape((elements, 2, columns, face), f32),
            shape((2, elements, columns, columns), f32),
        ],
        in_specs=vmem(6),
        out_specs=vmem(4),
        scratch_shapes=[
            pltpu.VMEM((side, COL, 128), f32),
            pltpu.VMEM((side, y_points, COL, columns), f32),
            pltpu.VMEM((side * side + COL, columns), f32),
            pltpu.VMEM((elements, side + 2, LEAD + COL * side + LEAD, columns), f32),
            pltpu.VMEM((elements, side + 2, LEAD + COL * side + LEAD, columns), f32),
            pltpu.VMEM((elements, side * side * COL, 2 * columns), bf16),
            pltpu.VMEM((elements, G**3, 2 * columns), bf16),
            pltpu.VMEM((elements, G**3, 2 * columns), bf16),
            pltpu.VMEM((elements, columns, 2 * columns), f32),
            pltpu.VMEM((elements, columns, columns), f32),
        ],
        compiler_params=pltpu.CompilerParams(vmem_limit_bytes=32 * 2**20),
        name="basis",
    )(own, x_before, x_after, z_before, z_after, starts)

    next_x = shift(minus_x, "ex", -1)
    next_z = shift(minus_z, "ez", -1)
    rows = columns // count
    blocks = pl.pallas_call(
        functools.partial(coupling_kernel, count),
        out_shape=[shape((rows, 4 * elements, columns), f32)] * count,
        in_specs=vmem(4),
        out_specs=vmem(count),
        scratch_shapes=[pltpu.VMEM((2, elements, columns, columns), f32)],
        compiler_params=pltpu.CompilerParams(vmem_limit_bytes=16 * 2**20),
        name="coupling",
    )(plus, next_x, next_z, near)
    arrived = [blocks[0]] + [shift(blocks[step], "ez", step) for step in range(1, count)]
    diagonal, coupled = pl.pallas_call(
        functools.partial(assemble_kernel, count),
        out_shape=[
            shape((rows, count, elements, columns), f32),
            shape((rows, count, 3 * elements, columns), f32),
        ],
        in_specs=vmem(count),
        out_specs=vmem(2),
        compiler_params=pltpu.CompilerParams(vmem_limit_bytes=16 * 2**20),
        name="assemble",
    )(*arrived)
    coupled = coupled.reshape(rows, count, 3, elements, columns).transpose(0, 1, 3, 2, 4)
    return (diagonal[None], coupled[None])


def solution(mesh):
    return jax.shard_map(
        local,
        mesh=mesh,
        in_specs=(P("ex", None, "ez"), P("ex", "ez", None, None, None)),
        out_specs=(P("ex", "ez", None, None, None), P("ex", "ez", None, None, None, None)),
        check_vma=False,
    )
```

time: 116 us -> 47.9 us (0.41)
  the two profiles are of different devices: /device:TPU:0 before, /device:TPU:1 now
where the time goes in v1:
time: 47.9 us; the launch traced here: 47.6 us
  waiting for transfers between devices  17.8 us (37%)
  Pallas kernels  14.5 us (30%)
  starting transfers between devices  11.5 us (24%)
  local copies, waits for them, and re-layouts  3.22 us (7%)
  between operations  0.68 us (1%)
    ppermute x9, waiting for transfers between devices, shift(): lax.ppermute(block, axis, [(i, (i + distance) % count) for i in range(cou...  17.8 us
    pallas_call x1, Pallas kernels, local(): pl.pallas_call(functools.partial(basis_kernel, elements, side), out_shape...  13.3 us
    ppermute x9, starting transfers between devices, shift(): lax.ppermute(block, axis, [(i, (i + distance) % count) for i in range(cou...  11.5 us
    unnamed x5, local copies, waits for them, and re-layouts  2.22 us
  transfers between devices with their start and end apart: 9, of which 8 were waited for; matrix products, arithmetic and copies ran while one was open for 0% of the time, Pallas kernels for 0%

profile of v1, /device:TPU:1, one launch (start us, length us, event | category | flops | bytes accessed | tf_op | source)
XLA Modules:
  0.0 47.6 jit_solution(10539777943980184047)
XLA Ops:
  0.6 0.0 copy-start.1
  0.6 0.8 %fusion = (f32[2,8,16]{2,1,0:T(8,128)S(1)}, f32[2,8,16]{2,1,0:T(8,128)S(1)}) fusion(f32[8,8,16]{2,1,0:T(8,128)} %bitcast.9), kind=kLoop, calls=%fused_computation.3 | loop fusion | bytes 4096 | tf_op jit(solution)/shard_map/slice | solution.py:326
  1.4 5.1 %collective-permute-start.1 = (f32[2,8,16]{2,1,0:T(8,128)S(1)}, f32[2,8,16]{2,1,0:T(8,128)S(1)}, u32[]{:S(2)}, u32[]{:S(2)}) collective-permute-start(f32[2,8,16]{2,1,0:T(8,128)S(1)} %get-tuple-element.26), channel_id=1, source_target_pairs={{0,28},{4,0},{8,4},{12,8},{16,12},{20,16},{24,20},{28,24},{1,29},{... | collective-permute-start | bytes 3080 | tf_op jit(solution)/shard_map/ppermute | solution.py:314
  6.5 0.0 collective-permute-start
  6.5 0.8 %collective-permute-done.1.x_after_ref = f32[2,8,16]{2,1,0:T(8,128)S(1)} collective-permute-done((f32[2,8,16]{2,1,0:T(8,128)S(1)}, f32[2,8,16]{2,1,0:T(8,128)S(1)}, u32[]{:S(2)}, u32[]{:S(2)}) %collective-permute-start.1) | collective-permute-done | bytes 1056 | tf_op jit(solution)/shard_map/ppermute | solution.py:314
  7.3 4.4 %collective-permute-done.x_before_ref = f32[2,8,16]{2,1,0:T(8,128)S(1)} collective-permute-done((f32[2,8,16]{2,1,0:T(8,128)S(1)}, f32[2,8,16]{2,1,0:T(8,128)S(1)}, u32[]{:S(2)}, u32[]{:S(2)}) %collective-permute-start) | collective-permute-done | bytes 1056 | tf_op jit(solution)/shard_map/ppermute | solution.py:314
  11.7 0.0 copy-done.1
  11.7 2.2 %collective-permute-start.3 = (f32[12,2,16]{2,1,0:T(2,128)S(1)}, f32[12,2,16]{2,1,0:T(2,128)S(1)}, u32[]{:S(2)}, u32[]{:S(2)}) collective-permute-start(f32[12,2,16]{2,1,0:T(2,128)S(1)} %get-tuple-element.24), channel_id=1, source_target_pairs={{0,3},{1,0},{2,1},{3,2},{4,7},{5,4},{6,5},{7,6},{8,11},{9,8},{10,9... | collective-permute-start | bytes 4616 | tf_op jit(solution)/shard_map/ppermute | solution.py:314
  13.9 1.2 %collective-permute-start.2 = (f32[12,2,16]{2,1,0:T(2,128)S(1)}, f32[12,2,16]{2,1,0:T(2,128)S(1)}, u32[]{:S(2)}, u32[]{:S(2)}) collective-permute-start(f32[12,2,16]{2,1,0:T(2,128)S(1)} %get-tuple-element.25), channel_id=1, source_target_pairs={{0,1},{1,2},{2,3},{3,0},{4,5},{5,6},{6,7},{7,4},{8,9},{9,10},{10,1... | collective-permute-start | bytes 4616 | tf_op jit(solution)/shard_map/ppermute | solution.py:314
  15.0 1.7 %collective-permute-done.3.z_after_ref = f32[12,2,16]{2,1,0:T(2,128)S(1)} collective-permute-done((f32[12,2,16]{2,1,0:T(2,128)S(1)}, f32[12,2,16]{2,1,0:T(2,128)S(1)}, u32[]{:S(2)}, u32[]{:S(2)}) %collective-permute-start.3) | collective-permute-done | bytes 1568 | tf_op jit(solution)/shard_map/ppermute | solution.py:314
  16.8 0.0 collective-permute-done.2.z_before_ref
  16.8 0.0 copy-start
  16.8 1.2 %copy-done = bf16[1,1,2,1728,128]{4,3,2,1,0:T(8,128)(2,1)S(1)} copy-done((bf16[1,1,2,1728,128]{4,3,2,1,0:T(8,128)(2,1)S(1)}, bf16[1,1,2,1728,128]{4,3,2,1,0:T(8,128)(2,1)}, u32[]{:S(2)}) %copy-start) | copy-done | bytes 884760
  17.9 13.3 %basis.1 = (f32[2,128,128]{2,1,0:T(8,128)S(1)}, f32[2,128,128]{2,1,0:T(8,128)S(1)}, f32[2,2,128,128]{3,2,1,0:T(8,128)S(1)}, f32[2,2,128,128]{3,2,1,0:T(8,128)S(1)}) custom-call(f32[8,8,16]{2,1,0:T(8,128)S(1)} %bitcast.11, f32[2,8,16]{2,1,0:T(8,128)S(1)} %collective-permute-done.x_before_ref, f32[2,8,16]{2,1,0:T(8,128)S(1)} %collective-permute-done.1.x_after_ref, ...), custom_call_target="tpu_custom_call" | custom-call | tf_op jit(solution)/shard_map/basis/pallas_call | solution.py:333
  31.2 0.1 collective-permute-start.4
  31.3 0.5 collective-permute-start.5
  31.8 4.2 %collective-permute-done.4.next_x_ref = f32[2,128,128]{2,1,0:T(8,128)S(1)} collective-permute-done((f32[2,128,128]{2,1,0:T(8,128)S(1)}, f32[2,128,128]{2,1,0:T(8,128)S(1)}, u32[]{:S(2)}, u32[]{:S(2)}) %collective-permute-start.4) | collective-permute-done | bytes 131104 | tf_op jit(solution)/shard_map/ppermute | solution.py:314
  35.9 0.1 collective-permute-done.5.next_z_ref
  36.0 0.4 coupling.1
  36.5 1.7 %collective-permute-start.6 = (f32[32,8,128]{2,1,0:T(8,128)S(1)}, f32[32,8,128]{2,1,0:T(8,128)S(1)}, u32[]{:S(2)}, u32[]{:S(2)}) collective-permute-start(f32[32,8,128]{2,1,0:T(8,128)S(1)} %get-tuple-element.17), channel_id=1, source_target_pairs={{0,1},{1,2},{2,3},{3,0},{4,5},{5,6},{6,7},{7,4},{8,9},{9,10},{10,1... | collective-permute-start | bytes 393224 | tf_op jit(solution)/shard_map/ppermute | solution.py:314
  38.1 0.9 %collective-permute-start.7 = (f32[32,8,128]{2,1,0:T(8,128)S(1)}, f32[32,8,128]{2,1,0:T(8,128)S(1)}, u32[]{:S(2)}, u32[]{:S(2)}) collective-permute-start(f32[32,8,128]{2,1,0:T(8,128)S(1)} %get-tuple-element.18), channel_id=1, source_target_pairs={{0,2},{1,3},{2,0},{3,1},{4,6},{5,7},{6,4},{7,5},{8,10},{9,11},{10,... | collective-permute-start | bytes 393224 | tf_op jit(solution)/shard_map/ppermute | solution.py:314
  39.1 0.0 collective-permute-start.8
  39.1 1.8 %collective-permute-done.6.refs_1_ = f32[32,8,128]{2,1,0:T(8,128)S(1)} collective-permute-done((f32[32,8,128]{2,1,0:T(8,128)S(1)}, f32[32,8,128]{2,1,0:T(8,128)S(1)}, u32[]{:S(2)}, u32[]{:S(2)}) %collective-permute-start.6) | collective-permute-done | bytes 131104 | tf_op jit(solution)/shard_map/ppermute | solution.py:314
  40.9 4.1 %collective-permute-done.7.refs_2_ = f32[32,8,128]{2,1,0:T(8,128)S(1)} collective-permute-done((f32[32,8,128]{2,1,0:T(8,128)S(1)}, f32[32,8,128]{2,1,0:T(8,128)S(1)}, u32[]{:S(2)}, u32[]{:S(2)}) %collective-permute-start.7) | collective-permute-done | bytes 131104 | tf_op jit(solution)/shard_map/ppermute | solution.py:314
  45.0 0.6 %collective-permute-done.8.refs_3_ = f32[32,8,128]{2,1,0:T(8,128)S(1)} collective-permute-done((f32[32,8,128]{2,1,0:T(8,128)S(1)}, f32[32,8,128]{2,1,0:T(8,128)S(1)}, u32[]{:S(2)}, u32[]{:S(2)}) %collective-permute-start.8) | collective-permute-done | bytes 131104 | tf_op jit(solution)/shard_map/ppermute | solution.py:314
  45.6 0.7 %assemble.1 = (f32[32,4,2,128]{3,2,1,0:T(2,128)}, f32[32,4,6,128]{3,2,1,0:T(8,128)S(1)}) custom-call(f32[32,8,128]{2,1,0:T(8,128)S(1)} %get-tuple-element.16.refs_0_, f32[32,8,128]{2,1,0:T(8,128)S(1)} %collective-permute-done.6.refs_1_, f32[32,8,128]{2,1,0:T(8,128)S(1)} %collective-permute-done.7.refs_2_, f32[32,8,128]{2,1,0:T(8,128)S(1)} %collective-permute-done.8.refs_3_), custom_call_target="tpu_custom_call" | custom-call | tf_op jit(solution)/shard_map/assemble/pallas_call | solution.py:372
  46.4 0.2 copy.4
  46.6 1.1 %copy.5 = f32[1,32,4,2,3,128]{5,3,4,2,1,0:T(2,128)} copy(f32[1,32,4,2,3,128]{5,1,3,4,2,0:T(8,128)S(1)} %bitcast.12) | data formatting | bytes 786432
  (1 shorter events, 0.0 us)
Async XLA Ops:
  0.6 11.1 %copy-start.1 = (f32[8,16,8]{1,2,0:T(8,128)S(1)}, f32[8,16,8]{1,2,0:T(8,128)}, u32[]{:S(2)}) copy-start(f32[8,16,8]{1,2,0:T(8,128)} %param.2) | copy-start | bytes 12292
  1.4 5.9 %collective-permute-start.1 = (f32[2,8,16]{2,1,0:T(8,128)S(1)}, f32[2,8,16]{2,1,0:T(8,128)S(1)}, u32[]{:S(2)}, u32[]{:S(2)}) collective-permute-start(f32[2,8,16]{2,1,0:T(8,128)S(1)} %get-tuple-element.26), channel_id=1, source_target_pairs={{0,28},{4,0},{8,4},{12,8},{16,12},{20,16},{24,20},{28,24},{1,29},{... | collective-permute-start | bytes 3080 | tf_op jit(solution)/shard_map/ppermute | solution.py:314
  6.5 5.2 %collective-permute-start = (f32[2,8,16]{2,1,0:T(8,128)S(1)}, f32[2,8,16]{2,1,0:T(8,128)S(1)}, u32[]{:S(2)}, u32[]{:S(2)}) collective-permute-start(f32[2,8,16]{2,1,0:T(8,128)S(1)} %get-tuple-element.27), channel_id=1, source_target_pairs={{0,4},{4,8},{8,12},{12,16},{16,20},{20,24},{24,28},{28,0},{1,5},{5... | collective-permute-start | bytes 3080 | tf_op jit(solution)/shard_map/ppermute | solution.py:314
  11.7 5.0 %collective-permute-start.3 = (f32[12,2,16]{2,1,0:T(2,128)S(1)}, f32[12,2,16]{2,1,0:T(2,128)S(1)}, u32[]{:S(2)}, u32[]{:S(2)}) collective-permute-start(f32[12,2,16]{2,1,0:T(2,128)S(1)} %get-tuple-element.24), channel_id=1, source_target_pairs={{0,3},{1,0},{2,1},{3,2},{4,7},{5,4},{6,5},{7,6},{8,11},{9,8},{10,9... | collective-permute-start | bytes 4616 | tf_op jit(solution)/shard_map/ppermute | solution.py:314
  13.9 2.9 %collective-permute-start.2 = (f32[12,2,16]{2,1,0:T(2,128)S(1)}, f32[12,2,16]{2,1,0:T(2,128)S(1)}, u32[]{:S(2)}, u32[]{:S(2)}) collective-permute-start(f32[12,2,16]{2,1,0:T(2,128)S(1)} %get-tuple-element.25), channel_id=1, source_target_pairs={{0,1},{1,2},{2,3},{3,0},{4,5},{5,6},{6,7},{7,4},{8,9},{9,10},{10,1... | collective-permute-start | bytes 4616 | tf_op jit(solution)/shard_map/ppermute | solution.py:314
  16.8 1.2 %copy-start = (bf16[1,1,2,1728,128]{4,3,2,1,0:T(8,128)(2,1)S(1)}, bf16[1,1,2,1728,128]{4,3,2,1,0:T(8,128)(2,1)}, u32[]{:S(2)}) copy-start(bf16[1,1,2,1728,128]{4,3,2,1,0:T(8,128)(2,1)} %param.3) | copy-start | bytes 2654212
  31.2 4.7 %collective-permute-start.4 = (f32[2,128,128]{2,1,0:T(8,128)S(1)}, f32[2,128,128]{2,1,0:T(8,128)S(1)}, u32[]{:S(2)}, u32[]{:S(2)}) collective-permute-start(f32[2,128,128]{2,1,0:T(8,128)S(1)} %get-tuple-element.13), channel_id=1, source_target_pairs={{0,28},{4,0},{8,4},{12,8},{16,12},{20,16},{24,20},{28,24},{1,29},{... | collective-permute-start | bytes 393224 | tf_op jit(solution)/shard_map/ppermute | solution.py:314
  31.3 4.7 %collective-permute-start.5 = (f32[2,128,128]{2,1,0:T(8,128)S(1)}, f32[2,128,128]{2,1,0:T(8,128)S(1)}, u32[]{:S(2)}, u32[]{:S(2)}) collective-permute-start(f32[2,128,128]{2,1,0:T(8,128)S(1)} %get-tuple-element.14), channel_id=1, source_target_pairs={{0,3},{1,0},{2,1},{3,2},{4,7},{5,4},{6,5},{7,6},{8,11},{9,8},{10,9... | collective-permute-start | bytes 393224 | tf_op jit(solution)/shard_map/ppermute | solution.py:314
  36.5 4.4 %collective-permute-start.6 = (f32[32,8,128]{2,1,0:T(8,128)S(1)}, f32[32,8,128]{2,1,0:T(8,128)S(1)}, u32[]{:S(2)}, u32[]{:S(2)}) collective-permute-start(f32[32,8,128]{2,1,0:T(8,128)S(1)} %get-tuple-element.17), channel_id=1, source_target_pairs={{0,1},{1,2},{2,3},{3,0},{4,5},{5,6},{6,7},{7,4},{8,9},{9,10},{10,1... | collective-permute-start | bytes 393224 | tf_op jit(solution)/shard_map/ppermute | solution.py:314
  38.1 6.9 %collective-permute-start.7 = (f32[32,8,128]{2,1,0:T(8,128)S(1)}, f32[32,8,128]{2,1,0:T(8,128)S(1)}, u32[]{:S(2)}, u32[]{:S(2)}) collective-permute-start(f32[32,8,128]{2,1,0:T(8,128)S(1)} %get-tuple-element.18), channel_id=1, source_target_pairs={{0,2},{1,3},{2,0},{3,1},{4,6},{5,7},{6,4},{7,5},{8,10},{9,11},{10,... | collective-permute-start | bytes 393224 | tf_op jit(solution)/shard_map/ppermute | solution.py:314
  39.1 6.6 %collective-permute-start.8 = (f32[32,8,128]{2,1,0:T(8,128)S(1)}, f32[32,8,128]{2,1,0:T(8,128)S(1)}, u32[]{:S(2)}, u32[]{:S(2)}) collective-permute-start(f32[32,8,128]{2,1,0:T(8,128)S(1)} %get-tuple-element.19), channel_id=1, source_target_pairs={{0,3},{1,0},{2,1},{3,2},{4,7},{5,4},{6,5},{7,6},{8,11},{9,8},{10,9... | collective-permute-start | bytes 393224 | tf_op jit(solution)/shard_map/ppermute | solution.py:314

commit v2 on v1

v2 whole, which is shorter than its diff:
```python
import functools

import jax
import jax.numpy as jnp
from jax import lax
from jax.experimental import pallas as pl
from jax.experimental.pallas import tpu as pltpu
from jax.sharding import PartitionSpec as P

G = 8
FILTER = 3

center = 6.5
halfwidth = 5.5

f32 = jnp.float32
bf16 = jnp.bfloat16

LEAD = 8
COL = 16
BLOCK = 8
PANEL = 32


def split(value):
    high = value.astype(bf16)
    return high, (value - high.astype(f32)).astype(bf16)


def weights(pair, transposed):
    high, low = pair
    empty = jnp.zeros_like(low)
    if transposed:
        upper = jnp.concatenate([high, high], axis=1)
        lower = jnp.concatenate([low, empty], axis=1)
        return jnp.concatenate([upper, lower], axis=0)
    upper = jnp.concatenate([high, low], axis=1)
    lower = jnp.concatenate([high, empty], axis=1)
    return jnp.concatenate([upper, lower], axis=0)


def product(value, held, transposed):
    pair = jnp.concatenate(split(value), axis=1)
    dims = (((1,), (1 if transposed else 0,)), ((), ()))
    both = lax.dot_general(pair, held, dims, preferred_element_type=f32)
    half = both.shape[1] // 2
    return both[:, :half] + both[:, half:]


def bcast_row(value, k):
    return jnp.broadcast_to(value[k : k + 1, :], value.shape)


def bcast_lane(value, k, lanes):
    return jnp.broadcast_to(value[:, k : k + 1], (value.shape[0], lanes))


def triple(value):
    high, rest = split(value)
    low = (value - high.astype(f32) - rest.astype(f32)).astype(bf16)
    return high, rest, low


def inverse_factors(matrix_ref, inverse_ref):
    count, size, width = matrix_ref.shape
    row = lax.broadcasted_iota(jnp.int32, (BLOCK, size), 0)
    for top in range(0, size, PANEL):
        bottom = top + PANEL
        kept = [[] for _ in range(count)]
        for start in range(top, bottom, BLOCK):
            rows = slice(start, start + BLOCK)
            for e in range(count):
                panel = [matrix_ref[e, rows, :size], matrix_ref[e, rows, size:]]
                columns = [bcast_lane(panel[0], start + j, size) for j in range(BLOCK)]
                pivot_rows = list(panel)
                pivots = None
                pivot = bcast_row(columns[0], 0)
                for k in range(BLOCK):
                    here = row == k
                    reciprocal = 1.0 / pivot
                    pivots = pivot if pivots is None else jnp.where(row >= k, pivot, pivots)
                    if k > 0:
                        pivot_rows = [
                            jnp.where(here, new, old) for new, old in zip(panel, pivot_rows)
                        ]
                    if k + 1 < BLOCK:
                        beside = bcast_row(columns[k + 1], k)
                        pivot = bcast_row(columns[k + 1], k + 1) - (beside * beside) * reciprocal
                    for j in range(k + 1, BLOCK):
                        scaled = bcast_row(columns[j], k) * reciprocal
                        columns[j] = jnp.where(here, scaled, columns[j] - columns[k] * scaled)
                    for part in range(2):
                        scaled = bcast_row(panel[part], k) * reciprocal
                        panel[part] = jnp.where(here, scaled, panel[part] - columns[k] * scaled)
                scale = lax.rsqrt(pivots)
                kept[e].append([part * scale for part in pivot_rows])
                inverse_ref[e, rows, :] = kept[e][-1][1]
                for below in range(start + BLOCK, bottom, BLOCK):
                    at = slice(below, below + BLOCK)
                    left, right = matrix_ref[e, at, :size], matrix_ref[e, at, size:]
                    terms = [[], []]
                    for k in range(BLOCK):
                        factor = bcast_lane(left, start + k, size)
                        for part in range(2):
                            terms[part].append(factor * bcast_row(panel[part], k))
                    for part in range(2):
                        while len(terms[part]) > 1:
                            pairs = zip(terms[part][::2], terms[part][1::2])
                            terms[part] = [x + y for x, y in pairs]
                    matrix_ref[e, at, :size] = left - terms[0][0]
                    matrix_ref[e, at, size:] = right - terms[1][0]
        if bottom == size:
            break
        for e in range(count):
            parts = [jnp.concatenate([b[i] for b in kept[e]], axis=0) for i in range(2)]
            left = triple(parts[0])
            both = [jnp.concatenate(p, axis=1) for p in zip(left, triple(parts[1]))]
            order = ((0, 0), (0, 1), (1, 0), (0, 2), (2, 0), (1, 1))
            taken = lax.dot_general(
                jnp.concatenate([left[i] for i, _ in order], axis=0),
                jnp.concatenate([both[j] for _, j in order], axis=0),
                (((0,), (0,)), ((), ())),
                preferred_element_type=f32,
            )
            matrix_ref[e, bottom:, :] = matrix_ref[e, bottom:, :] - taken[bottom:]


def is_inside(side, columns):
    return lax.broadcasted_iota(jnp.int32, (COL, columns), 0) < side


def zero_ends(ref, elements, side):
    for e in range(elements):
        ref[e, 0] = jnp.zeros(ref.shape[2:], f32)
        ref[e, side + 1] = jnp.zeros(ref.shape[2:], f32)
        for x in range(side):
            ref[e, x + 1, :LEAD] = jnp.zeros((LEAD, ref.shape[-1]), f32)
            ref[e, x + 1, LEAD + COL * side :] = jnp.zeros((LEAD, ref.shape[-1]), f32)


def sweep(source, scaled_ref, previous, target, pair_ref, margin):
    elements, side = source.shape[0], source.shape[1] - 2
    columns = source.shape[-1]
    y_points = scaled_ref.shape[1]
    inside = is_inside(side, columns)

    def at_x(x, carry):
        for e in range(elements):

            def column(y):
                return source[e, x + 1, LEAD + COL * y : LEAD + COL * (y + 1)]

            before, here = None, column(0)
            for y in range(side):
                low = LEAD + COL * y
                after = column(y + 1) if y + 1 < side else None
                beside = source[e, x, low : low + COL] + source[e, x + 2, low : low + COL]
                beside = beside + (
                    source[e, x + 1, low - 1 : low - 1 + COL]
                    + source[e, x + 1, low + 1 : low + 1 + COL]
                )
                if before is not None:
                    beside = beside + before
                if after is not None:
                    beside = beside + after
                y_point = (e * G - margin + y) % y_points
                value = scaled_ref[x, y_point] * here - (0.5 / halfwidth) * beside
                if previous is not None:
                    value = (value + value) - previous[e, x + 1, low : low + COL]
                value = jnp.where(inside, value, 0.0)
                target[e, x + 1, low : low + COL] = value
                if pair_ref is not None:
                    high, rest = split(value)
                    at = pl.multiple_of(x * (side * COL), COL) + COL * y
                    pair_ref[e, pl.ds(at, COL), :columns] = high
                    pair_ref[e, pl.ds(at, COL), columns:] = rest
                before, here = here, after
        return carry

    lax.fori_loop(0, side, at_x, 0)


def first_kernel(
    margin,
    own_ref,
    start_ref,
    held_ref,
    field_ref,
    first_ref,
    scaled_ref,
    box_ref,
    copy_ref,
    flat_ref,
    own_arrived,
    arrived,
):
    elements, columns = start_ref.shape[0], start_ref.shape[-1]
    side, y_points = scaled_ref.shape[:2]
    slab = side * side

    def part(e, x):
        at = pl.ds(pl.multiple_of(x * slab, 16), slab)
        return pltpu.make_async_copy(start_ref.at[e, at], copy_ref.at[e, at], arrived.at[e, x])

    own = pltpu.make_async_copy(own_ref, held_ref, own_arrived)
    own.start()
    for x in range(side):
        for e in range(elements):
            part(e, x).start()
    zero_ends(field_ref, elements, side)
    zero_ends(first_ref, elements, side)
    inside = is_inside(side, columns)
    box_ref[...] = jnp.zeros_like(box_ref)
    own.wait()
    box_ref[margin : margin + G, margin : margin + G, :y_points] = held_ref[...]

    def prepare(x, carry):
        rows = (box_ref[x] + (3.0 - center)) * (1.0 / halfwidth)
        for y in range(y_points):
            scaled_ref[x, y] = bcast_lane(rows, y, columns)
        for e in range(elements):
            part(e, x).wait()
            flat_ref[e, :slab] = copy_ref[e, pl.ds(pl.multiple_of(x * slab, 16), slab), :].astype(f32)
            for y in range(side):
                value = jnp.where(inside, flat_ref[e, side * y : side * y + COL], 0.0)
                field_ref[e, x + 1, LEAD + COL * y : LEAD + COL * (y + 1)] = value
        return carry

    lax.fori_loop(0, side, prepare, 0)
    sweep(field_ref, scaled_ref, None, first_ref, None, margin)


def point_rows(field, margin, e, x, y):
    low = LEAD + COL * (margin + y) + margin
    return field[e, margin + x + 1, low : low + G]


def layer(field, margin, e, d, i):
    if d == 0:
        return [point_rows(field, margin, e, i, y) for y in range(G)]
    if d == 1:
        return [point_rows(field, margin, e, x, i) for x in range(G)]
    low = LEAD + COL * margin + margin + i
    return [field[e, margin + x + 1, pl.ds(low, G, stride=COL)] for x in range(G)]


def basis_kernel(
    margin,
    x_before_ref,
    x_after_ref,
    z_before_ref,
    z_after_ref,
    start_in,
    first_in,
    scaled_in,
    minus_x_ref,
    minus_z_ref,
    inverse_ref,
    start_ref,
    first_ref,
    scaled_ref,
    box_ref,
    pair_ref,
    matrix_ref,
):
    elements, columns = start_ref.shape[0], start_ref.shape[-1]
    side, y_points = scaled_ref.shape[:2]
    box_ref[...] = jnp.zeros_like(box_ref)
    box_ref[:margin, margin : margin + G, :y_points] = x_before_ref[...]
    box_ref[margin + G :, margin : margin + G, :y_points] = x_after_ref[...]
    box_ref[:, :margin, :y_points] = z_before_ref[...]
    box_ref[:, margin + G : side, :y_points] = z_after_ref[...]

    def complete(x, carry):
        rows = box_ref[x] * (1.0 / halfwidth)
        for y in range(y_points):
            added = bcast_lane(rows, y, columns)
            scaled_ref[x, y] = scaled_in[x, y] + added
            for e in range(elements):
                box_y = (y - e * G + margin) % y_points
                if box_y < side:
                    at = slice(LEAD + COL * box_y, LEAD + COL * (box_y + 1))
                    first_ref[e, x + 1, at] = first_in[e, x + 1, at] + added * start_in[e, x + 1, at]
        return carry

    lax.fori_loop(0, side, complete, 0, unroll=3)
    source, field = first_ref, start_ref
    for step in range(1, FILTER):
        last = step == FILTER - 1
        sweep(source, scaled_ref, field, field, pair_ref if last else None, margin)
        source, field = field, source
    field = source

    identity = (
        lax.broadcasted_iota(jnp.int32, (columns, columns), 0)
        == lax.broadcasted_iota(jnp.int32, (columns, columns), 1)
    ).astype(f32)
    for e in range(elements):
        both = lax.dot_general(
            pair_ref[e, :, :columns],
            pair_ref[e],
            (((0,), (0,)), ((), ())),
            preferred_element_type=f32,
        )
        cross = both[:, columns:]
        matrix_ref[e, :, :columns] = both[:, :columns] + (cross + cross.T)
        matrix_ref[e, :, columns:] = identity

    inverse_factors(matrix_ref, inverse_ref)

    for e in range(elements):
        held = weights(split(inverse_ref[e]), True)
        for d, ref in ((0, minus_x_ref), (2, minus_z_ref)):
            rows = layer(field, margin, e, d, 0) + layer(field, margin, e, d, 1)
            ref[e] = product(jnp.concatenate(rows, 0), held, True)


def near_kernel(
    count,
    margin,
    inverse_ref,
    field,
    scaled_ref,
    plus_ref,
    *rest,
):
    out_refs = rest[:count]
    inner_ref, applied_ref, near_ref = rest[count:]
    elements, columns = inverse_ref.shape[0], inverse_ref.shape[-1]
    y_points = scaled_ref.shape[1]

    z = lax.broadcasted_iota(jnp.int32, (G, columns), 0)
    edge = (z == 1) | (z == G - 1)
    weight_down = jnp.where(z == 0, 0.0, jnp.where(edge, 0.25, 0.5))
    edge = (z == 0) | (z == G - 2)
    weight_up = jnp.where(z == G - 1, 0.0, jnp.where(edge, 0.25, 0.5))

    def link(i):
        return 0.25 if i in (0, G - 2) else 0.5

    for e in range(elements):
        for x in range(G):
            for y in range(0, G, 2):
                inner_pair, applied_pair = [], []
                for yy in (y, y + 1):
                    here = point_rows(field, margin, e, x, yy)
                    potential = scaled_ref[margin + x, (e * G + yy) % y_points, margin : margin + G]
                    value = (halfwidth * potential + center) * here
                    value = value - weight_down * pltpu.roll(here, 1, 0)
                    value = value - weight_up * pltpu.roll(here, G - 1, 0)
                    if x > 0:
                        value = value - link(x - 1) * point_rows(field, margin, e, x - 1, yy)
                    if x < G - 1:
                        value = value - link(x) * point_rows(field, margin, e, x + 1, yy)
                    if yy > 0:
                        value = value - link(yy - 1) * point_rows(field, margin, e, x, yy - 1)
                    if yy < G - 1:
                        value = value - link(yy) * point_rows(field, margin, e, x, yy + 1)
                    inner_pair.append(here)
                    applied_pair.append(value)
                at = slice((x * G + y) * G, (x * G + y + 2) * G)
                for ref, pair in ((inner_ref, inner_pair), (applied_ref, applied_pair)):
                    high, low = split(jnp.concatenate(pair, axis=0))
                    ref[e, at, :columns] = high
                    ref[e, at, columns:] = low

    face = 2 * G * G
    minus, plus, held = [], [], []
    for e in range(elements):
        held.append(weights(split(inverse_ref[e]), True))
        rows = layer(field, margin, e, 1, 0) + layer(field, margin, e, 1, 1)
        for d in range(3):
            last = layer(field, margin, e, d, G - 1)
            before = layer(field, margin, e, d, G - 2)
            rows += [-(0.5 * a + 0.25 * b) for a, b in zip(last, before)]
            rows += [-0.25 * a for a in last]
        faces = product(jnp.concatenate(rows, 0), held[e], True)
        minus.append(faces[:face])
        plus.append(faces[face : 2 * face].T)
        plus_ref[e, 0] = plus[e]
        plus[e] = faces[2 * face : 3 * face].T
        plus_ref[e, 1] = faces[3 * face :].T

    for e in range(elements):
        both = lax.dot_general(
            inner_ref[e, :, :columns],
            applied_ref[e],
            (((0,), (0,)), ((), ())),
            preferred_element_type=f32,
        )
        raw = both[:, :columns] + both[:, columns:]
        raw = raw + lax.dot_general(
            inner_ref[e, :, columns:],
            applied_ref[e, :, :columns],
            (((0,), (0,)), ((), ())),
            preferred_element_type=f32,
        )
        half = product(inverse_ref[e], weights(split(raw), False), False)
        near_ref[0, e] = product(half, held[e], True)
        following = weights(split(minus[(e + 1) % elements]), False)
        near_ref[1, e] = product(plus[e], following, False)
    send_rows(count, near_ref, out_refs)


def send_rows(count, blocks_ref, out_refs):
    kinds, elements, size = blocks_ref.shape[:3]
    rows = size // count
    me = lax.axis_index("ez")
    for step in range(count):
        at = pl.ds(pl.multiple_of(lax.rem(me + step, count) * rows, rows), rows)
        for kind in range(kinds):
            for e in range(elements):
                out_refs[step][:, elements * kind + e, :] = blocks_ref[kind, e, at, :]


def far_kernel(count, plus_ref, next_x_ref, next_z_ref, *rest):
    out_refs, far_ref = rest[:-1], rest[-1]
    for e in range(plus_ref.shape[0]):
        for d, ref in ((0, next_x_ref), (1, next_z_ref)):
            far_ref[d, e] = product(plus_ref[e, d], weights(split(ref[e]), False), False)
    send_rows(count, far_ref, out_refs)


def assemble_kernel(count, *refs):
    near_refs, far_refs = refs[:count], refs[count : 2 * count]
    diagonal_ref, coupling_ref = refs[2 * count :]
    elements = diagonal_ref.shape[2]
    me = lax.axis_index("ez")
    for step in range(count):
        z = lax.rem(me + (count - step), count)
        diagonal_ref[:, z] = near_refs[step][:, :elements]
        coupling_ref[:, z, 1] = near_refs[step][:, elements:]
        coupling_ref[:, z, 0] = far_refs[step][:, :elements]
        coupling_ref[:, z, 2] = far_refs[step][:, elements:]


def vmem(count):
    return [pl.BlockSpec(memory_space=pltpu.VMEM)] * count


def shift(block, axis, distance):
    count = lax.axis_size(axis)
    return lax.ppermute(block, axis, [(i, (i + distance) % count) for i in range(count)])


def local(potential, basis_start):
    elements, points, columns = basis_start.shape[2:]
    side = round(points ** (1 / 3))
    margin = (side - G) // 2
    y_points = potential.shape[1]
    count = lax.axis_size("ez")
    starts = basis_start.reshape(elements, points, columns)
    own = potential.transpose(0, 2, 1)
    x_before = shift(own, "ex", 1)[G - margin :]
    x_after = shift(own[:margin], "ex", -1)

    shape = jax.ShapeDtypeStruct
    field = shape((elements, side + 2, LEAD + COL * side + LEAD, columns), f32)
    scaled = shape((side, y_points, COL, columns), f32)
    held, start, first, own_scaled = pl.pallas_call(
        functools.partial(first_kernel, margin),
        out_shape=[shape(own.shape, f32), field, field, scaled],
        in_specs=[pl.BlockSpec(memory_space=pltpu.HBM)] * 2,
        out_specs=vmem(4),
        scratch_shapes=[
            pltpu.VMEM((side, COL, 128), f32),
            pltpu.VMEM(starts.shape, bf16),
            pltpu.VMEM((elements, side * side + COL, columns), f32),
            pltpu.SemaphoreType.DMA,
            pltpu.SemaphoreType.DMA((elements, side)),
        ],
        compiler_params=pltpu.CompilerParams(vmem_limit_bytes=24 * 2**20),
        cost_estimate=pl.CostEstimate(flops=10**8, bytes_accessed=10**7, transcendentals=0),
        name="first",
    )(own, starts)
    tall = jnp.concatenate([x_before, held, x_after], axis=0)
    z_before = shift(tall[:, G - margin :], "ez", 1)
    z_after = shift(tall[:, :margin], "ez", -1)

    face = shape((elements, 2 * G * G, columns), f32)
    square = shape((elements, columns, columns), f32)
    minus_x, minus_z, inverse, _, filtered, whole_scaled = pl.pallas_call(
        functools.partial(basis_kernel, margin),
        out_shape=[face, face, square, field, field, scaled],
        in_specs=vmem(7),
        out_specs=vmem(6),
        input_output_aliases={4: 3, 5: 4, 6: 5},
        scratch_shapes=[
            pltpu.VMEM((side, COL, 128), f32),
            pltpu.VMEM((elements, side * side * COL, 2 * columns), bf16),
            pltpu.VMEM((elements, columns, 2 * columns), f32),
        ],
        compiler_params=pltpu.CompilerParams(vmem_limit_bytes=32 * 2**20),
        name="basis",
    )(x_before, x_after, z_before, z_after, start, first, own_scaled)

    next_x = shift(minus_x, "ex", -1)
    next_z = shift(minus_z, "ez", -1)
    block = shape((columns // count, 2 * elements, columns), f32)
    plus, *near = pl.pallas_call(
        functools.partial(near_kernel, count, margin),
        out_shape=[shape((elements, 2, columns, 2 * G * G), f32)] + [block] * count,
        in_specs=vmem(3),
        out_specs=vmem(1 + count),
        scratch_shapes=[
            pltpu.VMEM((elements, G**3, 2 * columns), bf16),
            pltpu.VMEM((elements, G**3, 2 * columns), bf16),
            pltpu.VMEM((2, elements, columns, columns), f32),
        ],
        compiler_params=pltpu.CompilerParams(vmem_limit_bytes=24 * 2**20),
        cost_estimate=pl.CostEstimate(flops=10**8, bytes_accessed=10**7, transcendentals=0),
        name="near",
    )(inverse, filtered, whole_scaled)
    near = list(near[:1]) + [shift(near[step], "ez", step) for step in range(1, count)]

    far = pl.pallas_call(
        functools.partial(far_kernel, count),
        out_shape=[block] * count,
        in_specs=vmem(3),
        out_specs=vmem(count),
        scratch_shapes=[pltpu.VMEM((2, elements, columns, columns), f32)],
        compiler_params=pltpu.CompilerParams(vmem_limit_bytes=16 * 2**20),
        name="far",
    )(plus, next_x, next_z)
    far = list(far[:1]) + [shift(far[step], "ez", step) for step in range(1, count)]

    rows = columns // count
    diagonal, coupled = pl.pallas_call(
        functools.partial(assemble_kernel, count),
        out_shape=[
            shape((rows, count, elements, columns), f32),
            shape((rows, count, 3, elements, columns), f32),
        ],
        in_specs=vmem(2 * count),
        out_specs=vmem(2),
        compiler_params=pltpu.CompilerParams(vmem_limit_bytes=16 * 2**20),
        name="assemble",
    )(*near, *far)
    return (diagonal[None], coupled.transpose(0, 1, 3, 2, 4)[None])


def solution(mesh):
    return jax.shard_map(
        local,
        mesh=mesh,
        in_specs=(P("ex", None, "ez"), P("ex", "ez", None, None, None)),
        out_specs=(P("ex", "ez", None, None, None), P("ex", "ez", None, None, None, None)),
        check_vma=False,
    )
```

time: 47.9 us -> 38.7 us (0.81)
  the two profiles are of different devices: /device:TPU:1 before, /device:TPU:0 now
where the time goes in v2:
time: 38.7 us; the launch traced here: 38.3 us
  Pallas kernels  15.5 us (40%)
  starting transfers between devices  13.6 us (35%)
  waiting for transfers between devices  5.82 us (15%)
  local copies, waits for them, and re-layouts  2.66 us (7%)
  between operations  0.71 us (2%)
    ppermute x12, starting transfers between devices, shift(): lax.ppermute(block, axis, [(i, (i + distance) % count) for i in range(cou...  13.6 us
    pallas_call x1, Pallas kernels, local(): pl.pallas_call(functools.partial(basis_kernel, margin), out_shape=[face,...  8.56 us
    ppermute x12, waiting for transfers between devices, shift(): lax.ppermute(block, axis, [(i, (i + distance) % count) for i in range(cou...  5.82 us
    pallas_call x1, Pallas kernels, local(): pl.pallas_call(functools.partial(first_kernel, margin), out_shape=[shape(...  4.15 us
    unnamed x4, local copies, waits for them, and re-layouts  1.92 us
    pallas_call x1, Pallas kernels, local(): pl.pallas_call(functools.partial(near_kernel, count, margin), out_shape=[...  1.4 us
    pallas_call x1, Pallas kernels, local(): pl.pallas_call(functools.partial(assemble_kernel, count), out_shape=[shap...  0.97 us
  transfers between devices with their start and end apart: 12, of which 4 were waited for; matrix products, arithmetic and copies ran while one was open for 2% of the time, Pallas kernels for 15%

profile of v2, /device:TPU:0, one launch (start us, length us, event | category | flops | bytes accessed | tf_op | source)
XLA Modules:
  0.0 38.3 jit_solution(2174602763751246469)
XLA Ops:
  0.6 3.0 %collective-permute-start = (f32[8,8,16]{2,1,0:T(8,128)}, f32[8,8,16]{2,1,0:T(8,128)S(1)}, u32[]{:S(2)}, u32[]{:S(2)}) collective-permute-start(f32[8,8,16]{2,1,0:T(8,128)} %bitcast.7), channel_id=1, source_target_pairs={{0,4},{4,8},{8,12},{12,16},{16,20},{20,24},{24,28},{28,0},{1,5},{5... | collective-permute-start | bytes 12296 | tf_op jit(solution)/shard_map/ppermute | solution.py:443
  3.6 0.7 %slice.17 = f32[2,8,16]{2,1,0:T(8,128)S(1)} slice(f32[8,8,16]{2,1,0:T(8,128)} %bitcast.8), slice={[0:2], [0:8], [0:16]} | slice | bytes 2048 | tf_op jit(solution)/shard_map/slice | solution.py:455
  4.4 3.0 %collective-permute-start.1 = (f32[2,8,16]{2,1,0:T(8,128)S(1)}, f32[2,8,16]{2,1,0:T(8,128)S(1)}, u32[]{:S(2)}, u32[]{:S(2)}) collective-permute-start(f32[2,8,16]{2,1,0:T(8,128)S(1)} %slice.17), channel_id=1, source_target_pairs={{0,28},{4,0},{8,4},{12,8},{16,12},{20,16},{24,20},{28,24},{1,29},{... | collective-permute-start | bytes 3080 | tf_op jit(solution)/shard_map/ppermute | solution.py:443
  7.4 0.0 copy-start
  7.4 1.2 %copy-done = bf16[1,1,2,1728,128]{4,3,2,1,0:T(8,128)(2,1)S(1)} copy-done((bf16[1,1,2,1728,128]{4,3,2,1,0:T(8,128)(2,1)S(1)}, bf16[1,1,2,1728,128]{4,3,2,1,0:T(8,128)(2,1)}, u32[]{:S(2)}) %copy-start) | copy-done | bytes 884760
  8.6 0.0 copy-start.1
  8.6 0.8 %copy-done.1 = f32[8,16,8]{1,2,0:T(8,128)S(1)} copy-done((f32[8,16,8]{1,2,0:T(8,128)S(1)}, f32[8,16,8]{1,2,0:T(8,128)}, u32[]{:S(2)}) %copy-start.1) | copy-done | bytes 4120
  9.4 4.1 %first.1 = (f32[8,8,16]{2,1,0:T(8,128)S(1)}, f32[2,14,208,128]{3,2,1,0:T(8,128)S(1)}, f32[2,14,208,128]{3,2,1,0:T(8,128)S(1)}, f32[12,16,16,128]{3,2,1,0:T(8,128)S(1)}) custom-call(f32[8,8,16]{2,1,0:T(8,128)S(1)} %bitcast.9, bf16[2,1728,128]{2,1,0:T(8,128)(2,1)S(1)} %bitcast.6), custom_call_target="tpu_custom_call" | custom-call | flops 100000000 | bytes 10000000 | tf_op jit(solution)/shard_map/first/pallas_call | solution.py:460
  13.5 0.0 collective-permute-done
  13.5 0.0 collective-permute-done.1.x_after_ref
  13.6 0.7 %collective-permute-start.3 = (f32[12,2,16]{2,1,0:T(2,128)S(1)}, f32[12,2,16]{2,1,0:T(2,128)S(1)}, u32[]{:S(2)}, u32[]{:S(2)}) collective-permute-start(f32[12,2,16]{2,1,0:T(2,128)S(1)} %get-tuple-element.42), channel_id=1, source_target_pairs={{0,3},{1,0},{2,1},{3,2},{4,7},{5,4},{6,5},{7,6},{8,11},{9,8},{10,9... | collective-permute-start | bytes 4616 | tf_op jit(solution)/shard_map/ppermute | solution.py:443
  14.3 0.0 collective-permute-start.2
  14.3 1.4 %collective-permute-done.3.z_after_ref = f32[12,2,16]{2,1,0:T(2,128)S(1)} collective-permute-done((f32[12,2,16]{2,1,0:T(2,128)S(1)}, f32[12,2,16]{2,1,0:T(2,128)S(1)}, u32[]{:S(2)}, u32[]{:S(2)}) %collective-permute-start.3) | collective-permute-done | bytes 1568 | tf_op jit(solution)/shard_map/ppermute | solution.py:443
  15.7 1.7 %collective-permute-done.2.z_before_ref = f32[12,2,16]{2,1,0:T(2,128)S(1)} collective-permute-done((f32[12,2,16]{2,1,0:T(2,128)S(1)}, f32[12,2,16]{2,1,0:T(2,128)S(1)}, u32[]{:S(2)}, u32[]{:S(2)}) %collective-permute-start.2) | collective-permute-done | bytes 1568 | tf_op jit(solution)/shard_map/ppermute | solution.py:443
  17.4 8.6 %basis.1 = (f32[2,128,128]{2,1,0:T(8,128)S(1)}, f32[2,128,128]{2,1,0:T(8,128)S(1)}, f32[2,128,128]{2,1,0:T(8,128)S(1)}, f32[2,14,208,128]{3,2,1,0:T(8,128)S(1)},...) custom-call(f32[2,8,16]{2,1,0:T(8,128)S(1)} %slice.16.x_before_ref, ...), custom_call_target="tpu_custom_call", output_to_operand_aliasing={{3}: (4, {}), {4}: (5, {}), {5}: (6, {})} | custom-call | tf_op jit(solution)/shard_map/basis/pallas_call | solution.py:482
  26.0 1.8 %collective-permute-start.7 = (f32[2,128,128]{2,1,0:T(8,128)S(1)}, f32[2,128,128]{2,1,0:T(8,128)S(1)}, u32[]{:S(2)}, u32[]{:S(2)}) collective-permute-start(f32[2,128,128]{2,1,0:T(8,128)S(1)} %get-tuple-element.34), channel_id=1, source_target_pairs={{0,28},{4,0},{8,4},{12,8},{16,12},{20,16},{24,20},{28,24},{1,29},{... | collective-permute-start | bytes 393224 | tf_op jit(solution)/shard_map/ppermute | solution.py:443
  27.8 0.0 collective-permute-start.8
  27.8 1.4 %near.1 = (f32[2,2,128,128]{3,2,1,0:T(8,128)S(1)}, f32[32,4,128]{2,1,0:T(4,128)S(1)}, f32[32,4,128]{2,1,0:T(4,128)S(1)}, f32[32,4,128]{2,1,0:T(4,128)S(1)}, f32[32,4,128]{2,1,0:T(4,128)S(1)}) custom-call(f32[2,128,128]{2,1,0:T(8,128)S(1)} %get-tuple-element.26.inverse_ref, f32[2,14,208,128]{3,2,1,0:T(8,128)S(1)} %get-tuple-element.27.field, ...), custom_call_target="tpu_custom_call" | custom-call | flops 100000000 | bytes 10000000 | tf_op jit(solution)/shard_map/near/pallas_call | solution.py:500
  29.2 0.6 %collective-permute-start.4 = (f32[32,4,128]{2,1,0:T(4,128)S(1)}, f32[32,4,128]{2,1,0:T(4,128)S(1)}, u32[]{:S(2)}, u32[]{:S(2)}) collective-permute-start(f32[32,4,128]{2,1,0:T(4,128)S(1)} %get-tuple-element.30), channel_id=1, source_target_pairs={{0,1},{1,2},{2,3},{3,0},{4,5},{5,6},{6,7},{7,4},{8,9},{9,10},{10,1... | collective-permute-start | bytes 196616 | tf_op jit(solution)/shard_map/ppermute | solution.py:443
  29.7 1.2 %collective-permute-start.5 = (f32[32,4,128]{2,1,0:T(4,128)S(1)}, f32[32,4,128]{2,1,0:T(4,128)S(1)}, u32[]{:S(2)}, u32[]{:S(2)}) collective-permute-start(f32[32,4,128]{2,1,0:T(4,128)S(1)} %get-tuple-element.31), channel_id=1, source_target_pairs={{0,2},{1,3},{2,0},{3,1},{4,6},{5,7},{6,4},{7,5},{8,10},{9,11},{10,... | collective-permute-start | bytes 196616 | tf_op jit(solution)/shard_map/ppermute | solution.py:443
  30.9 1.0 %collective-permute-start.6 = (f32[32,4,128]{2,1,0:T(4,128)S(1)}, f32[32,4,128]{2,1,0:T(4,128)S(1)}, u32[]{:S(2)}, u32[]{:S(2)}) collective-permute-start(f32[32,4,128]{2,1,0:T(4,128)S(1)} %get-tuple-element.32), channel_id=1, source_target_pairs={{0,3},{1,0},{2,1},{3,2},{4,7},{5,4},{6,5},{7,6},{8,11},{9,8},{10,9... | collective-permute-start | bytes 196616 | tf_op jit(solution)/shard_map/ppermute | solution.py:443
  31.9 0.0 collective-permute-done.7.next_x_ref
  31.9 0.0 collective-permute-done.8.next_z_ref
  31.9 0.4 far.1
  32.2 0.1 collective-permute-start.9
  32.3 0.9 %collective-permute-start.10 = (f32[32,4,128]{2,1,0:T(4,128)S(1)}, f32[32,4,128]{2,1,0:T(4,128)S(1)}, u32[]{:S(2)}, u32[]{:S(2)}) collective-permute-start(f32[32,4,128]{2,1,0:T(4,128)S(1)} %get-tuple-element.38), channel_id=1, source_target_pairs={{0,2},{1,3},{2,0},{3,1},{4,6},{5,7},{6,4},{7,5},{8,10},{9,11},{10,... | collective-permute-start | bytes 196616 | tf_op jit(solution)/shard_map/ppermute | solution.py:443
  33.2 0.0 collective-permute-done.4.refs_1_
  33.2 1.4 %collective-permute-start.11 = (f32[32,4,128]{2,1,0:T(4,128)S(1)}, f32[32,4,128]{2,1,0:T(4,128)S(1)}, u32[]{:S(2)}, u32[]{:S(2)}) collective-permute-start(f32[32,4,128]{2,1,0:T(4,128)S(1)} %get-tuple-element.39), channel_id=1, source_target_pairs={{0,3},{1,0},{2,1},{3,2},{4,7},{5,4},{6,5},{7,6},{8,11},{9,8},{10,9... | collective-permute-start | bytes 196616 | tf_op jit(solution)/shard_map/ppermute | solution.py:443
  34.6 0.0 collective-permute-done.5.refs_2_
  34.6 0.0 collective-permute-done.6.refs_3_
  34.6 1.5 %collective-permute-done.9.refs_5_ = f32[32,4,128]{2,1,0:T(4,128)S(1)} collective-permute-done((f32[32,4,128]{2,1,0:T(4,128)S(1)}, f32[32,4,128]{2,1,0:T(4,128)S(1)}, u32[]{:S(2)}, u32[]{:S(2)}) %collective-permute-start.9) | collective-permute-done | bytes 65568 | tf_op jit(solution)/shard_map/ppermute | solution.py:443
  36.1 1.2 %collective-permute-done.10.refs_6_ = f32[32,4,128]{2,1,0:T(4,128)S(1)} collective-permute-done((f32[32,4,128]{2,1,0:T(4,128)S(1)}, f32[32,4,128]{2,1,0:T(4,128)S(1)}, u32[]{:S(2)}, u32[]{:S(2)}) %collective-permute-start.10) | collective-permute-done | bytes 65568 | tf_op jit(solution)/shard_map/ppermute | solution.py:443
  37.3 0.0 collective-permute-done.11.refs_7_
  37.3 1.0 %assemble.1 = (f32[32,4,2,128]{3,2,1,0:T(2,128)}, f32[32,4,3,2,128]{4,3,2,1,0:T(2,128)}) custom-call(f32[32,4,128]{2,1,0:T(4,128)S(1)} %get-tuple-element.29.refs_0_, f32[32,4,128]{2,1,0:T(4,128)S(1)} %collective-permute-done.4.refs_1_, f32[32,4,128]{2,1,0:T(4,128)S(1)} %collective-permute-done.5.refs_2_, f32[32,4,128]{2,1,0:T(4,128)S(1)} %collective-permute-done.6.refs_3_, ...), custom_call_target="tpu_custom_call" | custom-call | tf_op jit(solution)/shard_map/assemble/pallas_call | solution.py:528
  (2 shorter events, 0.0 us)
Async XLA Ops:
  0.6 12.9 %collective-permute-start = (f32[8,8,16]{2,1,0:T(8,128)}, f32[8,8,16]{2,1,0:T(8,128)S(1)}, u32[]{:S(2)}, u32[]{:S(2)}) collective-permute-start(f32[8,8,16]{2,1,0:T(8,128)} %bitcast.7), channel_id=1, source_target_pairs={{0,4},{4,8},{8,12},{12,16},{16,20},{20,24},{24,28},{28,0},{1,5},{5... | collective-permute-start | bytes 12296 | tf_op jit(solution)/shard_map/ppermute | solution.py:443
  4.4 9.2 %collective-permute-start.1 = (f32[2,8,16]{2,1,0:T(8,128)S(1)}, f32[2,8,16]{2,1,0:T(8,128)S(1)}, u32[]{:S(2)}, u32[]{:S(2)}) collective-permute-start(f32[2,8,16]{2,1,0:T(8,128)S(1)} %slice.17), channel_id=1, source_target_pairs={{0,28},{4,0},{8,4},{12,8},{16,12},{20,16},{24,20},{28,24},{1,29},{... | collective-permute-start | bytes 3080 | tf_op jit(solution)/shard_map/ppermute | solution.py:443
  7.4 1.2 %copy-start = (bf16[1,1,2,1728,128]{4,3,2,1,0:T(8,128)(2,1)S(1)}, bf16[1,1,2,1728,128]{4,3,2,1,0:T(8,128)(2,1)}, u32[]{:S(2)}) copy-start(bf16[1,1,2,1728,128]{4,3,2,1,0:T(8,128)(2,1)} %param.3) | copy-start | bytes 2654212
  8.6 0.8 %copy-start.1 = (f32[8,16,8]{1,2,0:T(8,128)S(1)}, f32[8,16,8]{1,2,0:T(8,128)}, u32[]{:S(2)}) copy-start(f32[8,16,8]{1,2,0:T(8,128)} %param.2) | copy-start | bytes 12292
  13.6 2.1 %collective-permute-start.3 = (f32[12,2,16]{2,1,0:T(2,128)S(1)}, f32[12,2,16]{2,1,0:T(2,128)S(1)}, u32[]{:S(2)}, u32[]{:S(2)}) collective-permute-start(f32[12,2,16]{2,1,0:T(2,128)S(1)} %get-tuple-element.42), channel_id=1, source_target_pairs={{0,3},{1,0},{2,1},{3,2},{4,7},{5,4},{6,5},{7,6},{8,11},{9,8},{10,9... | collective-permute-start | bytes 4616 | tf_op jit(solution)/shard_map/ppermute | solution.py:443
  14.3 3.1 %collective-permute-start.2 = (f32[12,2,16]{2,1,0:T(2,128)S(1)}, f32[12,2,16]{2,1,0:T(2,128)S(1)}, u32[]{:S(2)}, u32[]{:S(2)}) collective-permute-start(f32[12,2,16]{2,1,0:T(2,128)S(1)} %get-tuple-element.43), channel_id=1, source_target_pairs={{0,1},{1,2},{2,3},{3,0},{4,5},{5,6},{6,7},{7,4},{8,9},{9,10},{10,1... | collective-permute-start | bytes 4616 | tf_op jit(solution)/shard_map/ppermute | solution.py:443
  26.0 5.9 %collective-permute-start.7 = (f32[2,128,128]{2,1,0:T(8,128)S(1)}, f32[2,128,128]{2,1,0:T(8,128)S(1)}, u32[]{:S(2)}, u32[]{:S(2)}) collective-permute-start(f32[2,128,128]{2,1,0:T(8,128)S(1)} %get-tuple-element.34), channel_id=1, source_target_pairs={{0,28},{4,0},{8,4},{12,8},{16,12},{20,16},{24,20},{28,24},{1,29},{... | collective-permute-start | bytes 393224 | tf_op jit(solution)/shard_map/ppermute | solution.py:443
  27.8 4.1 %collective-permute-start.8 = (f32[2,128,128]{2,1,0:T(8,128)S(1)}, f32[2,128,128]{2,1,0:T(8,128)S(1)}, u32[]{:S(2)}, u32[]{:S(2)}) collective-permute-start(f32[2,128,128]{2,1,0:T(8,128)S(1)} %get-tuple-element.35), channel_id=1, source_target_pairs={{0,3},{1,0},{2,1},{3,2},{4,7},{5,4},{6,5},{7,6},{8,11},{9,8},{10,9... | collective-permute-start | bytes 393224 | tf_op jit(solution)/shard_map/ppermute | solution.py:443
  29.2 4.1 %collective-permute-start.4 = (f32[32,4,128]{2,1,0:T(4,128)S(1)}, f32[32,4,128]{2,1,0:T(4,128)S(1)}, u32[]{:S(2)}, u32[]{:S(2)}) collective-permute-start(f32[32,4,128]{2,1,0:T(4,128)S(1)} %get-tuple-element.30), channel_id=1, source_target_pairs={{0,1},{1,2},{2,3},{3,0},{4,5},{5,6},{6,7},{7,4},{8,9},{9,10},{10,1... | collective-permute-start | bytes 196616 | tf_op jit(solution)/shard_map/ppermute | solution.py:443
  29.7 4.9 %collective-permute-start.5 = (f32[32,4,128]{2,1,0:T(4,128)S(1)}, f32[32,4,128]{2,1,0:T(4,128)S(1)}, u32[]{:S(2)}, u32[]{:S(2)}) collective-permute-start(f32[32,4,128]{2,1,0:T(4,128)S(1)} %get-tuple-element.31), channel_id=1, source_target_pairs={{0,2},{1,3},{2,0},{3,1},{4,6},{5,7},{6,4},{7,5},{8,10},{9,11},{10,... | collective-permute-start | bytes 196616 | tf_op jit(solution)/shard_map/ppermute | solution.py:443
  30.9 3.7 %collective-permute-start.6 = (f32[32,4,128]{2,1,0:T(4,128)S(1)}, f32[32,4,128]{2,1,0:T(4,128)S(1)}, u32[]{:S(2)}, u32[]{:S(2)}) collective-permute-start(f32[32,4,128]{2,1,0:T(4,128)S(1)} %get-tuple-element.32), channel_id=1, source_target_pairs={{0,3},{1,0},{2,1},{3,2},{4,7},{5,4},{6,5},{7,6},{8,11},{9,8},{10,9... | collective-permute-start | bytes 196616 | tf_op jit(solution)/shard_map/ppermute | solution.py:443
  32.2 3.8 %collective-permute-start.9 = (f32[32,4,128]{2,1,0:T(4,128)S(1)}, f32[32,4,128]{2,1,0:T(4,128)S(1)}, u32[]{:S(2)}, u32[]{:S(2)}) collective-permute-start(f32[32,4,128]{2,1,0:T(4,128)S(1)} %get-tuple-element.37), channel_id=1, source_target_pairs={{0,1},{1,2},{2,3},{3,0},{4,5},{5,6},{6,7},{7,4},{8,9},{9,10},{10,1... | collective-permute-start | bytes 196616 | tf_op jit(solution)/shard_map/ppermute | solution.py:443
  32.3 5.0 %collective-permute-start.10 = (f32[32,4,128]{2,1,0:T(4,128)S(1)}, f32[32,4,128]{2,1,0:T(4,128)S(1)}, u32[]{:S(2)}, u32[]{:S(2)}) collective-permute-start(f32[32,4,128]{2,1,0:T(4,128)S(1)} %get-tuple-element.38), channel_id=1, source_target_pairs={{0,2},{1,3},{2,0},{3,1},{4,6},{5,7},{6,4},{7,5},{8,10},{9,11},{10,... | collective-permute-start | bytes 196616 | tf_op jit(solution)/shard_map/ppermute | solution.py:443
  33.2 4.1 %collective-permute-start.11 = (f32[32,4,128]{2,1,0:T(4,128)S(1)}, f32[32,4,128]{2,1,0:T(4,128)S(1)}, u32[]{:S(2)}, u32[]{:S(2)}) collective-permute-start(f32[32,4,128]{2,1,0:T(4,128)S(1)} %get-tuple-element.39), channel_id=1, source_target_pairs={{0,3},{1,0},{2,1},{3,2},{4,7},{5,4},{6,5},{7,6},{8,11},{9,8},{10,9... | collective-permute-start | bytes 196616 | tf_op jit(solution)/shard_map/ppermute | solution.py:443

commit v3 on v2

v3 whole, which is shorter than its diff:
```python
import functools

import jax
import jax.numpy as jnp
from jax import lax
from jax.experimental import pallas as pl
from jax.experimental.pallas import tpu as pltpu
from jax.sharding import PartitionSpec as P

G = 8
FILTER = 3

center = 6.5
halfwidth = 5.5

f32 = jnp.float32
bf16 = jnp.bfloat16

LEAD = 8
COL = 16
BLOCK = 16


def split(value):
    high = value.astype(bf16)
    return high, (value - high.astype(f32)).astype(bf16)


def weights(pair, transposed):
    high, low = pair
    empty = jnp.zeros_like(low)
    if transposed:
        upper = jnp.concatenate([high, high], axis=1)
        lower = jnp.concatenate([low, empty], axis=1)
        return jnp.concatenate([upper, lower], axis=0)
    upper = jnp.concatenate([high, low], axis=1)
    lower = jnp.concatenate([high, empty], axis=1)
    return jnp.concatenate([upper, lower], axis=0)


def product(value, held, transposed):
    pair = jnp.concatenate(split(value), axis=1)
    dims = (((1,), (1 if transposed else 0,)), ((), ()))
    both = lax.dot_general(pair, held, dims, preferred_element_type=f32)
    half = both.shape[1] // 2
    return both[:, :half] + both[:, half:]


def bcast_row(value, k):
    return jnp.broadcast_to(value[k : k + 1, :], value.shape)


def bcast_lane(value, k, lanes):
    return jnp.broadcast_to(value[:, k : k + 1], (value.shape[0], lanes))


def triple(value):
    high, rest = split(value)
    low = (value - high.astype(f32) - rest.astype(f32)).astype(bf16)
    return high, rest, low


def pack(values):
    first, second = values
    half = first.shape[1] // 2
    left = lax.broadcasted_iota(jnp.int32, first.shape, 1) < half
    return (
        jnp.where(left, first, pltpu.roll(second, half, 1)),
        jnp.where(left, pltpu.roll(first, half, 1), second),
    )


def tree_sum(terms):
    while len(terms) > 1:
        terms = [a + b for a, b in zip(terms[::2], terms[1::2])] + terms[len(terms) & ~1 :]
    return terms[0]


def inverse_factors(matrix_ref, inverse_ref):
    size = matrix_ref.shape[1]
    half = size // 2
    row = lax.broadcasted_iota(jnp.int32, (BLOCK, size), 0)
    lane = lax.broadcasted_iota(jnp.int32, (BLOCK, size), 1)
    other = jnp.where(lane < half, 0, half)

    def columns_of(value, at):
        return jnp.take_along_axis(value, other + at, axis=1)

    for top in (0, half):
        parts = (0, 1, 2) if top == 0 else (1, 2, 3)
        pivot_part = 0 if top == 0 else 1
        kept = []
        for start in range(top, top + half, BLOCK):
            rows = slice(start, start + BLOCK)
            panel = [matrix_ref[part, rows, :] for part in parts]
            at = start - top
            columns = [columns_of(panel[0], at + j) for j in range(BLOCK)]
            pivot_rows = list(panel)
            pivot = bcast_row(columns[0], 0)
            pivots = pivot
            for k in range(BLOCK):
                reciprocal = 1.0 / pivot
                if k > 0:
                    pivots = jnp.where(row >= k, pivot, pivots)
                    pivot_rows = [
                        jnp.where(row >= k, new, old) for new, old in zip(panel, pivot_rows)
                    ]
                if k + 1 < BLOCK:
                    beside = bcast_row(columns[k + 1], k)
                    pivot = bcast_row(columns[k + 1], k + 1) - (beside * beside) * reciprocal
                factor = jnp.where(row == k, 0.0, columns[k]) * reciprocal
                for j in range(k + 1, BLOCK):
                    columns[j] = columns[j] - factor * bcast_row(columns[j], k)
                panel = [value - factor * bcast_row(value, k) for value in panel]
            reciprocals = 1.0 / pivots
            solved = [value * reciprocals for value in panel]
            scale = lax.rsqrt(pivots)
            kept.append([value * scale for value in pivot_rows])
            inverse_ref[0, rows, :] = kept[-1][parts.index(2)]
            if 3 in parts:
                inverse_ref[1, rows, :] = kept[-1][parts.index(3)]
            else:
                inverse_ref[1, rows, :] = jnp.zeros((BLOCK, size), f32)
            for below in range(start + BLOCK, top + half, BLOCK):
                rows = slice(below, below + BLOCK)
                values = [matrix_ref[part, rows, :] for part in parts]
                factors = [columns_of(values[0], at + k) for k in range(BLOCK)]
                for part, value, taken in zip(parts, values, solved):
                    terms = [factors[k] * bcast_row(taken, k) for k in range(BLOCK)]
                    matrix_ref[part, rows, :] = value - tree_sum(terms)
        if top == 0:
            right = [jnp.concatenate([k[i] for k in kept], axis=0) for i in (1, 2)]
            left = triple(right[0])
            both = [jnp.concatenate(p, axis=1) for p in zip(left, triple(right[1]))]
            order = ((0, 0), (0, 1), (1, 0), (0, 2), (2, 0), (1, 1))
            taken = lax.dot_general(
                jnp.concatenate([left[i] for i, _ in order], axis=0),
                jnp.concatenate([both[j] for _, j in order], axis=0),
                (((0,), (0,)), ((), ())),
                preferred_element_type=f32,
            )
            is_left = lax.broadcasted_iota(jnp.int32, (half, size), 1) < half
            for i, part in enumerate((1, 2)):
                at = slice(size * i, size * (i + 1))
                mine = jnp.where(is_left, taken[:half, at], taken[half:, at])
                matrix_ref[part, half:, :] = matrix_ref[part, half:, :] - mine


def zero_ends(ref, elements, side):
    for e in range(elements):
        ref[e, 0] = jnp.zeros(ref.shape[2:], f32)
        ref[e, side + 1] = jnp.zeros(ref.shape[2:], f32)
        for x in range(side):
            ref[e, x + 1, :LEAD] = jnp.zeros((LEAD, ref.shape[-1]), f32)
            ref[e, x + 1, LEAD + COL * side :] = jnp.zeros((LEAD, ref.shape[-1]), f32)


def beside_weight(side, columns):
    inside = lax.broadcasted_iota(jnp.int32, (COL, columns), 0) < side
    return jnp.where(inside, 1.0 / halfwidth, 0.0)


def slab_step(x, source, scaled_ref, previous, target, pair_ref, margin):
    elements, side = source.shape[0], source.shape[1] - 2
    columns = source.shape[-1]
    weight = beside_weight(side, columns)
    if previous is None:
        weight = 0.5 * weight
    for e in range(elements):

        def column(y):
            return source[e, x + 1, LEAD + COL * y : LEAD + COL * (y + 1)]

        before, here = None, column(0)
        for y in range(side):
            low = LEAD + COL * y
            after = column(y + 1) if y + 1 < side else None
            beside = source[e, x, low : low + COL] + source[e, x + 2, low : low + COL]
            beside = beside + (
                source[e, x + 1, low - 1 : low - 1 + COL]
                + source[e, x + 1, low + 1 : low + 1 + COL]
            )
            if before is not None:
                beside = beside + before
            if after is not None:
                beside = beside + after
            if previous is None:
                value = -weight * beside
            else:
                scaled = scaled_ref[x, (e * G - margin + y) % scaled_ref.shape[1]]
                value = scaled * here - weight * beside - previous[e, x + 1, low : low + COL]
            target[e, x + 1, low : low + COL] = value
            if pair_ref is not None:
                high, rest = split(value)
                at = pl.multiple_of(x * (side * COL), COL) + COL * y
                pair_ref[e, pl.ds(at, COL), :columns] = high
                pair_ref[e, pl.ds(at, COL), columns:] = rest
            before, here = here, after


def first_kernel(start_ref, field_ref, first_ref, flat_ref):
    elements, columns = start_ref.shape[0], start_ref.shape[-1]
    side = field_ref.shape[1] - 2
    slab = side * side
    zero_ends(field_ref, elements, side)
    zero_ends(first_ref, elements, side)
    inside = lax.broadcasted_iota(jnp.int32, (COL, columns), 0) < side

    def prepare(x, carry):
        for e in range(elements):
            flat_ref[e, :slab] = start_ref[e, pl.ds(pl.multiple_of(x * slab, 16), slab), :].astype(f32)
            for y in range(side):
                value = jnp.where(inside, flat_ref[e, side * y : side * y + COL], 0.0)
                field_ref[e, x + 1, LEAD + COL * y : LEAD + COL * (y + 1)] = value
        return carry

    lax.fori_loop(0, side, prepare, 0)

    def step(x, carry):
        slab_step(x, field_ref, None, None, first_ref, None, 0)
        return carry

    lax.fori_loop(0, side, step, 0)


def point_rows(field, margin, e, x, y):
    low = LEAD + COL * (margin + y) + margin
    return field[e, margin + x + 1, low : low + G]


def layer(field, margin, e, d, i):
    if d == 0:
        return [point_rows(field, margin, e, i, y) for y in range(G)]
    if d == 1:
        return [point_rows(field, margin, e, x, i) for x in range(G)]
    low = LEAD + COL * margin + margin + i
    return [field[e, margin + x + 1, pl.ds(low, G, stride=COL)] for x in range(G)]


def potential_part(x, box_ref, margin, scaled_ref, first_in, start_in, first_ref):
    elements, columns = start_in.shape[0], start_in.shape[-1]
    side, y_points = scaled_ref.shape[:2]
    rows = box_ref[x]
    for y in range(y_points):
        scaled = bcast_lane(rows, y, columns)
        scaled_ref[x, y] = scaled
        scaled = 0.5 * scaled
        for e in range(elements):
            box_y = (y - e * G + margin) % y_points
            if box_y < side:
                at = slice(LEAD + COL * box_y, LEAD + COL * (box_y + 1))
                first_ref[e, x + 1, at] = first_in[e, x + 1, at] + scaled * start_in[e, x + 1, at]


def steps(ranges, first_ref, start_ref, scaled_ref, pair_ref, margin):
    fields = (first_ref, start_ref)
    for index in range(1, FILTER):
        source, target = fields
        pair = pair_ref if index == FILTER - 1 else None

        def next_step(x, carry):
            slab_step(x, source, scaled_ref, target, target, pair, margin)
            return carry

        lax.fori_loop(*ranges(index), next_step, 0)
        fields = fields[::-1]
    return fields[0]


def overlaps(pair_ref, low, high):
    columns = pair_ref.shape[-1] // 2
    return [
        lax.dot_general(
            pair_ref[e, low:high, :columns],
            pair_ref[e, low:high],
            (((0,), (0,)), ((), ())),
            preferred_element_type=f32,
        )
        for e in range(pair_ref.shape[0])
    ]


def middle_kernel(
    margin,
    low_ref,
    z_before_ref,
    z_after_ref,
    start_in,
    first_in,
    start_ref,
    first_ref,
    scaled_ref,
    pair_ref,
    overlap_ref,
    box_ref,
):
    side, y_points = scaled_ref.shape[:2]
    end = side - margin
    box_ref[...] = jnp.zeros_like(box_ref)
    box_ref[:end, margin : margin + G, :y_points] = low_ref[...]
    box_ref[:end, :margin, :y_points] = z_before_ref[...]
    box_ref[:end, margin + G : side, :y_points] = z_after_ref[...]

    def complete(x, carry):
        potential_part(x, box_ref, margin, scaled_ref, first_in, start_in, first_ref)
        return carry

    lax.fori_loop(0, end, complete, 0, unroll=2)
    steps(lambda i: (0, end - i), first_ref, start_ref, scaled_ref, pair_ref, margin)
    for e, value in enumerate(overlaps(pair_ref, 0, (end - FILTER + 1) * side * COL)):
        overlap_ref[e] = value


def basis_kernel(
    margin,
    x_after_ref,
    z_before_ref,
    z_after_ref,
    start_in,
    first_in,
    scaled_in,
    pair_in,
    overlap_ref,
    minus_x_ref,
    minus_z_ref,
    inverse_ref,
    start_ref,
    first_ref,
    scaled_ref,
    pair_ref,
    box_ref,
    matrix_ref,
    packed_ref,
):
    elements, columns = start_ref.shape[0], start_ref.shape[-1]
    side, y_points = scaled_ref.shape[:2]
    end = side - margin
    box_ref[...] = jnp.zeros_like(box_ref)
    box_ref[end:, margin : margin + G, :y_points] = x_after_ref[...]
    box_ref[end:, :margin, :y_points] = z_before_ref[...]
    box_ref[end:, margin + G : side, :y_points] = z_after_ref[...]
    for x in range(end, side):
        potential_part(x, box_ref, margin, scaled_ref, first_in, start_in, first_ref)
    field = steps(
        lambda i: (end - i, side), first_ref, start_ref, scaled_ref, pair_ref, margin
    )
    rest = overlaps(pair_ref, (end - FILTER + 1) * side * COL, side * side * COL)

    identity = (
        lax.broadcasted_iota(jnp.int32, (columns, columns), 0)
        == lax.broadcasted_iota(jnp.int32, (columns, columns), 1)
    ).astype(f32)
    grams = []
    for e in range(elements):
        products = overlap_ref[e] + rest[e]
        cross = products[:, columns:]
        grams.append(products[:, :columns] + (cross + cross.T))
    for e in range(0, elements, 2):
        pairs = [grams[e], grams[min(e + 1, elements - 1)]]
        for i, value in enumerate(pack(pairs) + pack([identity, identity])):
            matrix_ref[i] = value
        inverse_factors(matrix_ref, packed_ref)
        solved = pack([packed_ref[0], packed_ref[1]])
        for i in range(min(2, elements - e)):
            inverse_ref[e + i] = solved[i]

    for e in range(elements):
        held = weights(split(inverse_ref[e]), True)
        for d, ref in ((0, minus_x_ref), (2, minus_z_ref)):
            rows = layer(field, margin, e, d, 0) + layer(field, margin, e, d, 1)
            ref[e] = product(jnp.concatenate(rows, 0), held, True)


def near_kernel(
    count,
    margin,
    inverse_ref,
    field,
    scaled_ref,
    plus_ref,
    *rest,
):
    out_refs = rest[:count]
    inner_ref, applied_ref, near_ref = rest[count:]
    elements, columns = inverse_ref.shape[0], inverse_ref.shape[-1]
    y_points = scaled_ref.shape[1]

    z = lax.broadcasted_iota(jnp.int32, (G, columns), 0)
    edge = (z == 1) | (z == G - 1)
    weight_down = jnp.where(z == 0, 0.0, jnp.where(edge, 0.25, 0.5))
    edge = (z == 0) | (z == G - 2)
    weight_up = jnp.where(z == G - 1, 0.0, jnp.where(edge, 0.25, 0.5))

    def link(i):
        return 0.25 if i in (0, G - 2) else 0.5

    for e in range(elements):
        for x in range(G):
            for y in range(0, G, 2):
                inner_pair, applied_pair = [], []
                for yy in (y, y + 1):
                    here = point_rows(field, margin, e, x, yy)
                    potential = scaled_ref[margin + x, (e * G + yy) % y_points, margin : margin + G]
                    value = (0.5 * halfwidth * potential + center) * here
                    value = value - weight_down * pltpu.roll(here, 1, 0)
                    value = value - weight_up * pltpu.roll(here, G - 1, 0)
                    if x > 0:
                        value = value - link(x - 1) * point_rows(field, margin, e, x - 1, yy)
                    if x < G - 1:
                        value = value - link(x) * point_rows(field, margin, e, x + 1, yy)
                    if yy > 0:
                        value = value - link(yy - 1) * point_rows(field, margin, e, x, yy - 1)
                    if yy < G - 1:
                        value = value - link(yy) * point_rows(field, margin, e, x, yy + 1)
                    inner_pair.append(here)
                    applied_pair.append(value)
                at = slice((x * G + y) * G, (x * G + y + 2) * G)
                for ref, pair in ((inner_ref, inner_pair), (applied_ref, applied_pair)):
                    high, low = split(jnp.concatenate(pair, axis=0))
                    ref[e, at, :columns] = high
                    ref[e, at, columns:] = low

    face = 2 * G * G
    minus, plus, held = [], [], []
    for e in range(elements):
        held.append(weights(split(inverse_ref[e]), True))
        rows = layer(field, margin, e, 1, 0) + layer(field, margin, e, 1, 1)
        for d in range(3):
            last = layer(field, margin, e, d, G - 1)
            before = layer(field, margin, e, d, G - 2)
            rows += [-(0.5 * a + 0.25 * b) for a, b in zip(last, before)]
            rows += [-0.25 * a for a in last]
        faces = product(jnp.concatenate(rows, 0), held[e], True)
        minus.append(faces[:face])
        plus.append(faces[face : 2 * face].T)
        plus_ref[e, 0] = plus[e]
        plus[e] = faces[2 * face : 3 * face].T
        plus_ref[e, 1] = faces[3 * face :].T

    for e in range(elements):
        both = lax.dot_general(
            inner_ref[e, :, :columns],
            applied_ref[e],
            (((0,), (0,)), ((), ())),
            preferred_element_type=f32,
        )
        raw = both[:, :columns] + both[:, columns:]
        raw = raw + lax.dot_general(
            inner_ref[e, :, columns:],
            applied_ref[e, :, :columns],
            (((0,), (0,)), ((), ())),
            preferred_element_type=f32,
        )
        half = product(inverse_ref[e], weights(split(raw), False), False)
        near_ref[0, e] = product(half, held[e], True)
        following = weights(split(minus[(e + 1) % elements]), False)
        near_ref[1, e] = product(plus[e], following, False)
    send_rows(count, near_ref, out_refs)


def send_rows(count, blocks_ref, out_refs):
    kinds, elements, size = blocks_ref.shape[:3]
    rows = size // count
    me = lax.axis_index("ez")
    for step in range(count):
        at = pl.ds(pl.multiple_of(lax.rem(me + step, count) * rows, rows), rows)
        for kind in range(kinds):
            for e in range(elements):
                out_refs[step][:, elements * kind + e, :] = blocks_ref[kind, e, at, :]


def far_kernel(count, plus_ref, next_x_ref, next_z_ref, *rest):
    out_refs, far_ref = rest[:-1], rest[-1]
    for e in range(plus_ref.shape[0]):
        for d, ref in ((0, next_x_ref), (1, next_z_ref)):
            far_ref[d, e] = product(plus_ref[e, d], weights(split(ref[e]), False), False)
    send_rows(count, far_ref, out_refs)


def assemble_kernel(count, *refs):
    near_refs, far_refs = refs[:count], refs[count : 2 * count]
    diagonal_ref, coupling_ref = refs[2 * count :]
    elements = diagonal_ref.shape[2]
    me = lax.axis_index("ez")
    for step in range(count):
        z = lax.rem(me + (count - step), count)
        diagonal_ref[:, z] = near_refs[step][:, :elements]
        coupling_ref[:, z, 1] = near_refs[step][:, elements:]
        coupling_ref[:, z, 0] = far_refs[step][:, :elements]
        coupling_ref[:, z, 2] = far_refs[step][:, elements:]


def vmem(count):
    return [pl.BlockSpec(memory_space=pltpu.VMEM)] * count


def shift(block, axis, distance):
    count = lax.axis_size(axis)
    return lax.ppermute(block, axis, [(i, (i + distance) % count) for i in range(count)])


def local(potential, basis_start):
    elements, points, columns = basis_start.shape[2:]
    side = round(points ** (1 / 3))
    margin = (side - G) // 2
    y_points = potential.shape[1]
    count = lax.axis_size("ez")
    starts = basis_start.reshape(elements, points, columns)
    own = potential.transpose(0, 2, 1)
    own_scaled = lax.optimization_barrier((own + (3.0 - center)) * (2.0 / halfwidth))
    x_before = (shift(own, "ex", 1)[G - margin :] + (3.0 - center)) * (2.0 / halfwidth)
    x_after = shift(own_scaled[:margin], "ex", -1)

    shape = jax.ShapeDtypeStruct
    field = shape((elements, side + 2, LEAD + COL * side + LEAD, columns), f32)
    scaled = shape((side, y_points, COL, columns), f32)
    start, first = pl.pallas_call(
        first_kernel,
        out_shape=[field, field],
        in_specs=vmem(1),
        out_specs=vmem(2),
        scratch_shapes=[pltpu.VMEM((elements, side * side + COL, columns), f32)],
        compiler_params=pltpu.CompilerParams(vmem_limit_bytes=24 * 2**20),
        cost_estimate=pl.CostEstimate(flops=10**5, bytes_accessed=10**4, transcendentals=0),
        name="first",
    )(starts)
    low = lax.optimization_barrier(jnp.concatenate([x_before, own_scaled], axis=0))
    z_before = shift(low[:, G - margin :], "ez", 1)
    z_after = shift(low[:, :margin], "ez", -1)
    edge_before = shift(x_after[:, G - margin :], "ez", 1)
    edge_after = shift(x_after[:, :margin], "ez", -1)
    pair = shape((elements, side * side * COL, 2 * columns), bf16)
    overlap = shape((elements, columns, 2 * columns), f32)
    box = pltpu.VMEM((side, COL, 128), f32)
    start, first, most_scaled, pairs, overlapped = pl.pallas_call(
        functools.partial(middle_kernel, margin),
        out_shape=[field, field, scaled, pair, overlap],
        in_specs=vmem(5),
        out_specs=vmem(5),
        input_output_aliases={3: 0, 4: 1},
        scratch_shapes=[box],
        compiler_params=pltpu.CompilerParams(vmem_limit_bytes=32 * 2**20),
        cost_estimate=pl.CostEstimate(flops=10**8, bytes_accessed=10**7, transcendentals=0),
        name="middle",
    )(low, z_before, z_after, start, first)

    face = shape((elements, 2 * G * G, columns), f32)
    square = shape((elements, columns, columns), f32)
    minus_x, minus_z, inverse, _, filtered, whole_scaled, _ = pl.pallas_call(
        functools.partial(basis_kernel, margin),
        out_shape=[face, face, square, field, field, scaled, pair],
        in_specs=vmem(8),
        out_specs=vmem(7),
        input_output_aliases={3: 3, 4: 4, 5: 5, 6: 6},
        scratch_shapes=[
            box,
            pltpu.VMEM((4, columns, columns), f32),
            pltpu.VMEM((2, columns, columns), f32),
        ],
        compiler_params=pltpu.CompilerParams(vmem_limit_bytes=32 * 2**20),
        name="basis",
    )(x_after, edge_before, edge_after, start, first, most_scaled, pairs, overlapped)

    next_x = shift(minus_x, "ex", -1)
    next_z = shift(minus_z, "ez", -1)
    block = shape((columns // count, 2 * elements, columns), f32)
    plus, *near = pl.pallas_call(
        functools.partial(near_kernel, count, margin),
        out_shape=[shape((elements, 2, columns, 2 * G * G), f32)] + [block] * count,
        in_specs=vmem(3),
        out_specs=vmem(1 + count),
        scratch_shapes=[
            pltpu.VMEM((elements, G**3, 2 * columns), bf16),
            pltpu.VMEM((elements, G**3, 2 * columns), bf16),
            pltpu.VMEM((2, elements, columns, columns), f32),
        ],
        compiler_params=pltpu.CompilerParams(vmem_limit_bytes=24 * 2**20),
        cost_estimate=pl.CostEstimate(flops=10**8, bytes_accessed=10**7, transcendentals=0),
        name="near",
    )(inverse, filtered, whole_scaled)
    near = list(near[:1]) + [shift(near[step], "ez", step) for step in range(1, count)]

    far = pl.pallas_call(
        functools.partial(far_kernel, count),
        out_shape=[block] * count,
        in_specs=vmem(3),
        out_specs=vmem(count),
        scratch_shapes=[pltpu.VMEM((2, elements, columns, columns), f32)],
        compiler_params=pltpu.CompilerParams(vmem_limit_bytes=16 * 2**20),
        name="far",
    )(plus, next_x, next_z)
    far = list(far[:1]) + [shift(far[step], "ez", step) for step in range(1, count)]

    rows = columns // count
    diagonal, coupled = pl.pallas_call(
        functools.partial(assemble_kernel, count),
        out_shape=[
            shape((rows, count, elements, columns), f32),
            shape((rows, count, 3, elements, columns), f32),
        ],
        in_specs=vmem(2 * count),
        out_specs=vmem(2),
        compiler_params=pltpu.CompilerParams(vmem_limit_bytes=16 * 2**20),
        name="assemble",
    )(*near, *far)
    return (diagonal[None], coupled.transpose(0, 1, 3, 2, 4)[None])


def solution(mesh):
    return jax.shard_map(
        local,
        mesh=mesh,
        in_specs=(P("ex", None, "ez"), P("ex", "ez", None, None, None)),
        out_specs=(P("ex", "ez", None, None, None), P("ex", "ez", None, None, None, None)),
        check_vma=False,
    )
```

time: 38.7 us -> 34.7 us (0.90)
  Pallas kernels: 15.5 us -> 11.7 us
  starting transfers between devices: 13.6 us -> 15.5 us
  local copies, waits for them, and re-layouts: 2.66 us -> 1.18 us
  waiting for transfers between devices: 5.82 us -> 4.4 us
  other arithmetic: 0.01 us -> 0.81 us
    pallas_call x1, Pallas kernels: 8.56 us -> 4.92 us  [local(): pl.pallas_call(functools.partial(basis_kernel, margin), out_shape=[face,...]
    ppermute x12 -> x14, starting transfers between devices: 13.6 us -> 15.5 us  [shift(): lax.ppermute(block, axis, [(i, (i + distance) % count) for i in range(cou...]
    ppermute x12 -> x14, waiting for transfers between devices: 5.82 us -> 4.4 us  [shift(): lax.ppermute(block, axis, [(i, (i + distance) % count) for i in range(cou...]
    mul x0 -> x2, other arithmetic: none -> 0.8 us  [the longest x1 0.8 us: local(): (own + (3.0 - center)) * (2.0 / halfwidth)]
    unnamed x4 -> x2, local copies, waits for them, and re-layouts: 1.92 us -> 1.17 us
    slice x2 -> x3, local copies, waits for them, and re-layouts: 0.73 us -> 0.02 us  [the longest x1 0.01 us: local(): z_after = shift(low[:, :margin], 'ez', -1)]
    pallas_call x1 -> x2, Pallas kernels: 4.15 us -> 4.04 us  [the longest x1 3.01 us: local(): pl.pallas_call(functools.partial(middle_kernel, margin), out_shape=[field...]
  transfers between devices with their start and end apart: 12 -> 14, of which waited for: 4 -> 3; matrix products, arithmetic and copies ran while one was open for 2% -> 2% of each run, Pallas kernels for 15% -> 17%
where the time goes in v3:
time: 34.7 us; the launch traced here: 34.3 us
  starting transfers between devices  15.5 us (45%)
  Pallas kernels  11.7 us (34%)
  waiting for transfers between devices  4.4 us (13%)
  local copies, waits for them, and re-layouts  1.18 us (3%)
  other arithmetic  0.81 us (2%)
  between operations  0.74 us (2%)
    ppermute x14, starting transfers between devices, shift(): lax.ppermute(block, axis, [(i, (i + distance) % count) for i in range(cou...  15.5 us
    pallas_call x1, Pallas kernels, local(): pl.pallas_call(functools.partial(basis_kernel, margin), out_shape=[face,...  4.92 us
    ppermute x14, waiting for transfers between devices, shift(): lax.ppermute(block, axis, [(i, (i + distance) % count) for i in range(cou...  4.4 us
    pallas_call x1, Pallas kernels, local(): pl.pallas_call(functools.partial(middle_kernel, margin), out_shape=[field...  3.01 us
    pallas_call x1, Pallas kernels, local(): pl.pallas_call(functools.partial(near_kernel, count, margin), out_shape=[...  1.4 us
    unnamed x2, local copies, waits for them, and re-layouts  1.17 us
    pallas_call x1, Pallas kernels, local(): pl.pallas_call(first_kernel, out_shape=[field, field], in_specs=vmem(1),...  1.04 us
    pallas_call x1, Pallas kernels, local(): pl.pallas_call(functools.partial(assemble_kernel, count), out_shape=[shap...  0.97 us
  transfers between devices with their start and end apart: 14, of which 3 were waited for; matrix products, arithmetic and copies ran while one was open for 2% of the time, Pallas kernels for 17%

profile of v3, /device:TPU:0, one launch (start us, length us, event | category | flops | bytes accessed | tf_op | source)
XLA Modules:
  0.0 34.3 jit_solution(5620113346774605710)
XLA Ops:
  0.6 3.0 %collective-permute-start.3 = (f32[8,8,16]{2,1,0:T(8,128)}, f32[8,8,16]{2,1,0:T(8,128)S(1)}, u32[]{:S(2)}, u32[]{:S(2)}) collective-permute-start(f32[8,8,16]{2,1,0:T(8,128)} %bitcast.8), channel_id=1, source_target_pairs={{0,4},{4,8},{8,12},{12,16},{16,20},{20,24},{24,28},{28,0},{1,5},{5... | collective-permute-start | bytes 12296 | tf_op jit(solution)/shard_map/ppermute | solution.py:499
  3.6 0.8 %add_multiply_fusion = f32[8,8,16]{2,1,0:T(8,128)S(1)} fusion(f32[8,16,8]{1,2,0:T(8,128)} %param.2), kind=kLoop, calls=%fused_computation.1 | loop fusion | flops 2048 | bytes 8192 | tf_op jit(solution)/shard_map/mul | solution.py:510
  4.4 3.0 %collective-permute-start = (f32[2,8,16]{2,1,0:T(8,128)S(1)}, f32[2,8,16]{2,1,0:T(8,128)S(1)}, u32[]{:S(2)}, u32[]{:S(2)}) collective-permute-start(f32[2,8,16]{2,1,0:T(8,128)S(1)} %slice.24), channel_id=1, source_target_pairs={{0,28},{4,0},{8,4},{12,8},{16,12},{20,16},{24,20},{28,24},{1,29},{... | collective-permute-start | bytes 3080 | tf_op jit(solution)/shard_map/ppermute | solution.py:499
  7.5 0.0 copy-start
  7.5 1.2 %copy-done = bf16[1,1,2,1728,128]{4,3,2,1,0:T(8,128)(2,1)S(1)} copy-done((bf16[1,1,2,1728,128]{4,3,2,1,0:T(8,128)(2,1)S(1)}, bf16[1,1,2,1728,128]{4,3,2,1,0:T(8,128)(2,1)}, u32[]{:S(2)}) %copy-start) | copy-done | bytes 884760
  8.7 1.0 %first.1 = (f32[2,14,208,128]{3,2,1,0:T(8,128)S(1)}, f32[2,14,208,128]{3,2,1,0:T(8,128)S(1)}) custom-call(bf16[2,1728,128]{2,1,0:T(8,128)(2,1)S(1)} %bitcast.7), custom_call_target="tpu_custom_call" | custom-call | flops 100000 | bytes 10000 | tf_op jit(solution)/shard_map/first/pallas_call | solution.py:517
  9.7 0.0 collective-permute-done.3
  9.8 0.7 %collective-permute-start.5 = (f32[10,2,16]{2,1,0:T(2,128)S(1)}, f32[10,2,16]{2,1,0:T(2,128)S(1)}, u32[]{:S(2)}, u32[]{:S(2)}) collective-permute-start(f32[10,2,16]{2,1,0:T(2,128)S(1)} %get-tuple-element.48), channel_id=1, source_target_pairs={{0,3},{1,0},{2,1},{3,2},{4,7},{5,4},{6,5},{7,6},{8,11},{9,8},{10,9... | collective-permute-start | bytes 3848 | tf_op jit(solution)/shard_map/ppermute | solution.py:499
  10.5 0.0 collective-permute-start.4
  10.5 0.0 collective-permute-done.x_after_ref
  10.5 1.7 %collective-permute-start.2 = (f32[2,2,16]{2,1,0:T(2,128)S(1)}, f32[2,2,16]{2,1,0:T(2,128)S(1)}, u32[]{:S(2)}, u32[]{:S(2)}) collective-permute-start(f32[2,2,16]{2,1,0:T(2,128)S(1)} %get-tuple-element.50), channel_id=1, source_target_pairs={{0,3},{1,0},{2,1},{3,2},{4,7},{5,4},{6,5},{7,6},{8,11},{9,8},{10,9... | collective-permute-start | bytes 776 | tf_op jit(solution)/shard_map/ppermute | solution.py:499
  12.2 0.0 collective-permute-start.1
  12.2 0.0 collective-permute-done.5.z_after_ref
  12.2 1.3 %collective-permute-done.4.z_before_ref = f32[10,2,16]{2,1,0:T(2,128)S(1)} collective-permute-done((f32[10,2,16]{2,1,0:T(2,128)S(1)}, f32[10,2,16]{2,1,0:T(2,128)S(1)}, u32[]{:S(2)}, u32[]{:S(2)}) %collective-permute-start.4) | collective-permute-done | bytes 1312 | tf_op jit(solution)/shard_map/ppermute | solution.py:499
  13.6 3.0 %middle.1 = (f32[2,14,208,128]{3,2,1,0:T(8,128)S(1)}, f32[2,14,208,128]{3,2,1,0:T(8,128)S(1)}, f32[12,16,16,128]{3,2,1,0:T(8,128)S(1)}, bf16[2,2304,256]{2,1,0:T(8,128)(2,1)S(1)}, f32[2,128,256]{2,1,0:T(8,128)S(1)}) custom-call(f32[10,8,16]{2,1,0:T(8,128)S(1)} %pad_maximum_fusion.low_ref, ...), custom_call_target="tpu_custom_call", output_to_operand_aliasing={{0}: (3, {}), {1}: (4, {})} | custom-call | flops 100000000 | bytes 10000000 | tf_op jit(solution)/shard_map/middle/pallas_call | solution.py:535
  16.6 0.0 collective-permute-done.2.z_after_ref
  16.6 0.0 collective-permute-done.1.z_before_ref
  16.6 4.9 %basis.1 = (f32[2,128,128]{2,1,0:T(8,128)S(1)}, f32[2,128,128]{2,1,0:T(8,128)S(1)}, f32[2,128,128]{2,1,0:T(8,128)S(1)}, f32[2,14,208,128]{3,2,1,0:T(8,128)S(1)},...) custom-call(f32[2,8,16]{2,1,0:T(8,128)S(1)} %collective-permute-done, ...), custom_call_target="tpu_custom_call", output_to_operand_aliasing={{3}: (3, {}), {4}: (4, {}), {5}: (5, {}), {6}: (6, {})} | custom-call | tf_op jit(solution)/shard_map/basis/pallas_call | solution.py:549
  21.5 1.8 %collective-permute-start.9 = (f32[2,128,128]{2,1,0:T(8,128)S(1)}, f32[2,128,128]{2,1,0:T(8,128)S(1)}, u32[]{:S(2)}, u32[]{:S(2)}) collective-permute-start(f32[2,128,128]{2,1,0:T(8,128)S(1)} %get-tuple-element.40), channel_id=1, source_target_pairs={{0,28},{4,0},{8,4},{12,8},{16,12},{20,16},{24,20},{28,24},{1,29},{... | collective-permute-start | bytes 393224 | tf_op jit(solution)/shard_map/ppermute | solution.py:499
  23.3 0.1 collective-permute-start.10
  23.4 1.4 %near.1 = (f32[2,2,128,128]{3,2,1,0:T(8,128)S(1)}, f32[32,4,128]{2,1,0:T(4,128)S(1)}, f32[32,4,128]{2,1,0:T(4,128)S(1)}, f32[32,4,128]{2,1,0:T(4,128)S(1)}, f32[32,4,128]{2,1,0:T(4,128)S(1)}) custom-call(f32[2,128,128]{2,1,0:T(8,128)S(1)} %get-tuple-element.32.inverse_ref, f32[2,14,208,128]{3,2,1,0:T(8,128)S(1)} %get-tuple-element.33.field, ...), custom_call_target="tpu_custom_call" | custom-call | flops 100000000 | bytes 10000000 | tf_op jit(solution)/shard_map/near/pallas_call | solution.py:567
  24.9 0.4 %collective-permute-start.6 = (f32[32,4,128]{2,1,0:T(4,128)S(1)}, f32[32,4,128]{2,1,0:T(4,128)S(1)}, u32[]{:S(2)}, u32[]{:S(2)}) collective-permute-start(f32[32,4,128]{2,1,0:T(4,128)S(1)} %get-tuple-element.36), channel_id=1, source_target_pairs={{0,1},{1,2},{2,3},{3,0},{4,5},{5,6},{6,7},{7,4},{8,9},{9,10},{10,1... | collective-permute-start | bytes 196616 | tf_op jit(solution)/shard_map/ppermute | solution.py:499
  25.3 1.2 %collective-permute-start.7 = (f32[32,4,128]{2,1,0:T(4,128)S(1)}, f32[32,4,128]{2,1,0:T(4,128)S(1)}, u32[]{:S(2)}, u32[]{:S(2)}) collective-permute-start(f32[32,4,128]{2,1,0:T(4,128)S(1)} %get-tuple-element.37), channel_id=1, source_target_pairs={{0,2},{1,3},{2,0},{3,1},{4,6},{5,7},{6,4},{7,5},{8,10},{9,11},{10,... | collective-permute-start | bytes 196616 | tf_op jit(solution)/shard_map/ppermute | solution.py:499
  26.5 1.4 %collective-permute-start.8 = (f32[32,4,128]{2,1,0:T(4,128)S(1)}, f32[32,4,128]{2,1,0:T(4,128)S(1)}, u32[]{:S(2)}, u32[]{:S(2)}) collective-permute-start(f32[32,4,128]{2,1,0:T(4,128)S(1)} %get-tuple-element.38), channel_id=1, source_target_pairs={{0,3},{1,0},{2,1},{3,2},{4,7},{5,4},{6,5},{7,6},{8,11},{9,8},{10,9... | collective-permute-start | bytes 196616 | tf_op jit(solution)/shard_map/ppermute | solution.py:499
  27.9 0.0 collective-permute-done.9.next_x_ref
  27.9 0.0 collective-permute-done.10.next_z_ref
  27.9 0.4 %far.1 = (f32[32,4,128]{2,1,0:T(4,128)S(1)}, f32[32,4,128]{2,1,0:T(4,128)S(1)}, f32[32,4,128]{2,1,0:T(4,128)S(1)}, f32[32,4,128]{2,1,0:T(4,128)S(1)}) custom-call(f32[2,2,128,128]{3,2,1,0:T(8,128)S(1)} %get-tuple-element.39.plus_ref, f32[2,128,128]{2,1,0:T(8,128)S(1)} %collective-permute-done.9.next_x_ref, f32[2,128,128]{2,1,0:T(8,128)S(1)} %collective-permute-done.10.next_z_ref), custom_call_target="tpu_custom_call" | custom-call | tf_op jit(solution)/shard_map/far/pallas_call | solution.py:583
  28.3 0.1 collective-permute-start.11
  28.4 0.6 %collective-permute-start.12 = (f32[32,4,128]{2,1,0:T(4,128)S(1)}, f32[32,4,128]{2,1,0:T(4,128)S(1)}, u32[]{:S(2)}, u32[]{:S(2)}) collective-permute-start(f32[32,4,128]{2,1,0:T(4,128)S(1)} %get-tuple-element.44), channel_id=1, source_target_pairs={{0,2},{1,3},{2,0},{3,1},{4,6},{5,7},{6,4},{7,5},{8,10},{9,11},{10,... | collective-permute-start | bytes 196616 | tf_op jit(solution)/shard_map/ppermute | solution.py:499
  28.9 0.0 collective-permute-done.6.refs_1_
  28.9 1.4 %collective-permute-start.13 = (f32[32,4,128]{2,1,0:T(4,128)S(1)}, f32[32,4,128]{2,1,0:T(4,128)S(1)}, u32[]{:S(2)}, u32[]{:S(2)}) collective-permute-start(f32[32,4,128]{2,1,0:T(4,128)S(1)} %get-tuple-element.45), channel_id=1, source_target_pairs={{0,3},{1,0},{2,1},{3,2},{4,7},{5,4},{6,5},{7,6},{8,11},{9,8},{10,9... | collective-permute-start | bytes 196616 | tf_op jit(solution)/shard_map/ppermute | solution.py:499
  30.3 0.0 collective-permute-done.7.refs_2_
  30.3 0.0 collective-permute-done.8.refs_3_
  30.3 1.8 %collective-permute-done.11.refs_5_ = f32[32,4,128]{2,1,0:T(4,128)S(1)} collective-permute-done((f32[32,4,128]{2,1,0:T(4,128)S(1)}, f32[32,4,128]{2,1,0:T(4,128)S(1)}, u32[]{:S(2)}, u32[]{:S(2)}) %collective-permute-start.11) | collective-permute-done | bytes 65568 | tf_op jit(solution)/shard_map/ppermute | solution.py:499
  32.1 1.2 %collective-permute-done.12.refs_6_ = f32[32,4,128]{2,1,0:T(4,128)S(1)} collective-permute-done((f32[32,4,128]{2,1,0:T(4,128)S(1)}, f32[32,4,128]{2,1,0:T(4,128)S(1)}, u32[]{:S(2)}, u32[]{:S(2)}) %collective-permute-start.12) | collective-permute-done | bytes 65568 | tf_op jit(solution)/shard_map/ppermute | solution.py:499
  33.3 0.0 collective-permute-done.13.refs_7_
  33.3 1.0 %assemble.1 = (f32[32,4,2,128]{3,2,1,0:T(2,128)}, f32[32,4,3,2,128]{4,3,2,1,0:T(2,128)}) custom-call(f32[32,4,128]{2,1,0:T(4,128)S(1)} %get-tuple-element.35.refs_0_, f32[32,4,128]{2,1,0:T(4,128)S(1)} %collective-permute-done.6.refs_1_, f32[32,4,128]{2,1,0:T(4,128)S(1)} %collective-permute-done.7.refs_2_, f32[32,4,128]{2,1,0:T(4,128)S(1)} %collective-permute-done.8.refs_3_, ...), custom_call_target="tpu_custom_call" | custom-call | tf_op jit(solution)/shard_map/assemble/pallas_call | solution.py:595
  (5 shorter events, 0.0 us)
Async XLA Ops:
  0.6 9.1 %collective-permute-start.3 = (f32[8,8,16]{2,1,0:T(8,128)}, f32[8,8,16]{2,1,0:T(8,128)S(1)}, u32[]{:S(2)}, u32[]{:S(2)}) collective-permute-start(f32[8,8,16]{2,1,0:T(8,128)} %bitcast.8), channel_id=1, source_target_pairs={{0,4},{4,8},{8,12},{12,16},{16,20},{20,24},{24,28},{28,0},{1,5},{5... | collective-permute-start | bytes 12296 | tf_op jit(solution)/shard_map/ppermute | solution.py:499
  4.4 6.0 %collective-permute-start = (f32[2,8,16]{2,1,0:T(8,128)S(1)}, f32[2,8,16]{2,1,0:T(8,128)S(1)}, u32[]{:S(2)}, u32[]{:S(2)}) collective-permute-start(f32[2,8,16]{2,1,0:T(8,128)S(1)} %slice.24), channel_id=1, source_target_pairs={{0,28},{4,0},{8,4},{12,8},{16,12},{20,16},{24,20},{28,24},{1,29},{... | collective-permute-start | bytes 3080 | tf_op jit(solution)/shard_map/ppermute | solution.py:499
  7.5 1.2 %copy-start = (bf16[1,1,2,1728,128]{4,3,2,1,0:T(8,128)(2,1)S(1)}, bf16[1,1,2,1728,128]{4,3,2,1,0:T(8,128)(2,1)}, u32[]{:S(2)}) copy-start(bf16[1,1,2,1728,128]{4,3,2,1,0:T(8,128)(2,1)} %param.3) | copy-start | bytes 2654212
  9.8 2.5 %collective-permute-start.5 = (f32[10,2,16]{2,1,0:T(2,128)S(1)}, f32[10,2,16]{2,1,0:T(2,128)S(1)}, u32[]{:S(2)}, u32[]{:S(2)}) collective-permute-start(f32[10,2,16]{2,1,0:T(2,128)S(1)} %get-tuple-element.48), channel_id=1, source_target_pairs={{0,3},{1,0},{2,1},{3,2},{4,7},{5,4},{6,5},{7,6},{8,11},{9,8},{10,9... | collective-permute-start | bytes 3848 | tf_op jit(solution)/shard_map/ppermute | solution.py:499
  10.5 3.1 %collective-permute-start.4 = (f32[10,2,16]{2,1,0:T(2,128)S(1)}, f32[10,2,16]{2,1,0:T(2,128)S(1)}, u32[]{:S(2)}, u32[]{:S(2)}) collective-permute-start(f32[10,2,16]{2,1,0:T(2,128)S(1)} %get-tuple-element.49), channel_id=1, source_target_pairs={{0,1},{1,2},{2,3},{3,0},{4,5},{5,6},{6,7},{7,4},{8,9},{9,10},{10,1... | collective-permute-start | bytes 3848 | tf_op jit(solution)/shard_map/ppermute | solution.py:499
  10.5 6.1 %collective-permute-start.2 = (f32[2,2,16]{2,1,0:T(2,128)S(1)}, f32[2,2,16]{2,1,0:T(2,128)S(1)}, u32[]{:S(2)}, u32[]{:S(2)}) collective-permute-start(f32[2,2,16]{2,1,0:T(2,128)S(1)} %get-tuple-element.50), channel_id=1, source_target_pairs={{0,3},{1,0},{2,1},{3,2},{4,7},{5,4},{6,5},{7,6},{8,11},{9,8},{10,9... | collective-permute-start | bytes 776 | tf_op jit(solution)/shard_map/ppermute | solution.py:499
  12.2 4.4 %collective-permute-start.1 = (f32[2,2,16]{2,1,0:T(2,128)S(1)}, f32[2,2,16]{2,1,0:T(2,128)S(1)}, u32[]{:S(2)}, u32[]{:S(2)}) collective-permute-start(f32[2,2,16]{2,1,0:T(2,128)S(1)} %get-tuple-element.51), channel_id=1, source_target_pairs={{0,1},{1,2},{2,3},{3,0},{4,5},{5,6},{6,7},{7,4},{8,9},{9,10},{10,1... | collective-permute-start | bytes 776 | tf_op jit(solution)/shard_map/ppermute | solution.py:499
  21.5 6.4 %collective-permute-start.9 = (f32[2,128,128]{2,1,0:T(8,128)S(1)}, f32[2,128,128]{2,1,0:T(8,128)S(1)}, u32[]{:S(2)}, u32[]{:S(2)}) collective-permute-start(f32[2,128,128]{2,1,0:T(8,128)S(1)} %get-tuple-element.40), channel_id=1, source_target_pairs={{0,28},{4,0},{8,4},{12,8},{16,12},{20,16},{24,20},{28,24},{1,29},{... | collective-permute-start | bytes 393224 | tf_op jit(solution)/shard_map/ppermute | solution.py:499
  23.3 4.6 %collective-permute-start.10 = (f32[2,128,128]{2,1,0:T(8,128)S(1)}, f32[2,128,128]{2,1,0:T(8,128)S(1)}, u32[]{:S(2)}, u32[]{:S(2)}) collective-permute-start(f32[2,128,128]{2,1,0:T(8,128)S(1)} %get-tuple-element.41), channel_id=1, source_target_pairs={{0,3},{1,0},{2,1},{3,2},{4,7},{5,4},{6,5},{7,6},{8,11},{9,8},{10,9... | collective-permute-start | bytes 393224 | tf_op jit(solution)/shard_map/ppermute | solution.py:499
  24.9 4.1 %collective-permute-start.6 = (f32[32,4,128]{2,1,0:T(4,128)S(1)}, f32[32,4,128]{2,1,0:T(4,128)S(1)}, u32[]{:S(2)}, u32[]{:S(2)}) collective-permute-start(f32[32,4,128]{2,1,0:T(4,128)S(1)} %get-tuple-element.36), channel_id=1, source_target_pairs={{0,1},{1,2},{2,3},{3,0},{4,5},{5,6},{6,7},{7,4},{8,9},{9,10},{10,1... | collective-permute-start | bytes 196616 | tf_op jit(solution)/shard_map/ppermute | solution.py:499
  25.3 5.0 %collective-permute-start.7 = (f32[32,4,128]{2,1,0:T(4,128)S(1)}, f32[32,4,128]{2,1,0:T(4,128)S(1)}, u32[]{:S(2)}, u32[]{:S(2)}) collective-permute-start(f32[32,4,128]{2,1,0:T(4,128)S(1)} %get-tuple-element.37), channel_id=1, source_target_pairs={{0,2},{1,3},{2,0},{3,1},{4,6},{5,7},{6,4},{7,5},{8,10},{9,11},{10,... | collective-permute-start | bytes 196616 | tf_op jit(solution)/shard_map/ppermute | solution.py:499
  26.5 3.8 %collective-permute-start.8 = (f32[32,4,128]{2,1,0:T(4,128)S(1)}, f32[32,4,128]{2,1,0:T(4,128)S(1)}, u32[]{:S(2)}, u32[]{:S(2)}) collective-permute-start(f32[32,4,128]{2,1,0:T(4,128)S(1)} %get-tuple-element.38), channel_id=1, source_target_pairs={{0,3},{1,0},{2,1},{3,2},{4,7},{5,4},{6,5},{7,6},{8,11},{9,8},{10,9... | collective-permute-start | bytes 196616 | tf_op jit(solution)/shard_map/ppermute | solution.py:499
  28.3 3.8 %collective-permute-start.11 = (f32[32,4,128]{2,1,0:T(4,128)S(1)}, f32[32,4,128]{2,1,0:T(4,128)S(1)}, u32[]{:S(2)}, u32[]{:S(2)}) collective-permute-start(f32[32,4,128]{2,1,0:T(4,128)S(1)} %get-tuple-element.43), channel_id=1, source_target_pairs={{0,1},{1,2},{2,3},{3,0},{4,5},{5,6},{6,7},{7,4},{8,9},{9,10},{10,1... | collective-permute-start | bytes 196616 | tf_op jit(solution)/shard_map/ppermute | solution.py:499
  28.4 5.0 %collective-permute-start.12 = (f32[32,4,128]{2,1,0:T(4,128)S(1)}, f32[32,4,128]{2,1,0:T(4,128)S(1)}, u32[]{:S(2)}, u32[]{:S(2)}) collective-permute-start(f32[32,4,128]{2,1,0:T(4,128)S(1)} %get-tuple-element.44), channel_id=1, source_target_pairs={{0,2},{1,3},{2,0},{3,1},{4,6},{5,7},{6,4},{7,5},{8,10},{9,11},{10,... | collective-permute-start | bytes 196616 | tf_op jit(solution)/shard_map/ppermute | solution.py:499
  28.9 4.4 %collective-permute-start.13 = (f32[32,4,128]{2,1,0:T(4,128)S(1)}, f32[32,4,128]{2,1,0:T(4,128)S(1)}, u32[]{:S(2)}, u32[]{:S(2)}) collective-permute-start(f32[32,4,128]{2,1,0:T(4,128)S(1)} %get-tuple-element.45), channel_id=1, source_target_pairs={{0,3},{1,0},{2,1},{3,2},{4,7},{5,4},{6,5},{7,6},{8,11},{9,8},{10,9... | collective-permute-start | bytes 196616 | tf_op jit(solution)/shard_map/ppermute | solution.py:499

commit v4 on v3

--- a/solution.py
+++ b/solution.py
@@ -17,6 +17,7 @@
 bf16 = jnp.bfloat16
 
 LEAD = 8
+AHEAD = 1
 COL = 16
 BLOCK = 16
 
@@ -262,7 +263,7 @@
             slab_step(x, source, scaled_ref, target, target, pair, margin)
             return carry
 
-        lax.fori_loop(*ranges(index), next_step, 0)
+        lax.fori_loop(*ranges(index), next_step, 0, unroll=2)
         fields = fields[::-1]
     return fields[0]
 
@@ -378,10 +379,10 @@
     field,
     scaled_ref,
     plus_ref,
+    near_ref,
     *rest,
 ):
-    out_refs = rest[:count]
-    inner_ref, applied_ref, near_ref = rest[count:]
+    *out_refs, inner_ref, applied_ref = rest
     elements, columns = inverse_ref.shape[0], inverse_ref.shape[-1]
     y_points = scaled_ref.shape[1]
 
@@ -455,39 +456,63 @@
         near_ref[0, e] = product(half, held[e], True)
         following = weights(split(minus[(e + 1) % elements]), False)
         near_ref[1, e] = product(plus[e], following, False)
-    send_rows(count, near_ref, out_refs)
-
-
-def send_rows(count, blocks_ref, out_refs):
-    kinds, elements, size = blocks_ref.shape[:3]
+    send_rows(count, [near_ref], out_refs, parted(count)[1])
+
+
+def partner(index, step, count):
+    return index ^ step if count & (count - 1) == 0 else (index + step) % count
+
+
+def send_rows(count, sources, out_refs, steps):
+    elements, size = sources[0].shape[1:3]
     rows = size // count
     me = lax.axis_index("ez")
-    for step in range(count):
-        at = pl.ds(pl.multiple_of(lax.rem(me + step, count) * rows, rows), rows)
-        for kind in range(kinds):
-            for e in range(elements):
-                out_refs[step][:, elements * kind + e, :] = blocks_ref[kind, e, at, :]
-
-
-def far_kernel(count, plus_ref, next_x_ref, next_z_ref, *rest):
+    for out_ref, step in zip(out_refs, steps):
+        owner = me ^ step if count & (count - 1) == 0 else lax.rem(me + step, count)
+        at = pl.ds(pl.multiple_of(owner * rows, rows), rows)
+        slot = 0
+        for blocks_ref in sources:
+            for kind in range(blocks_ref.shape[0]):
+                for e in range(elements):
+                    out_ref[:, slot, :] = blocks_ref[kind, e, at, :]
+                    slot += 1
+
+
+def far_kernel(count, plus_ref, next_x_ref, next_z_ref, near_ref, *rest):
     out_refs, far_ref = rest[:-1], rest[-1]
     for e in range(plus_ref.shape[0]):
         for d, ref in ((0, next_x_ref), (1, next_z_ref)):
             far_ref[d, e] = product(plus_ref[e, d], weights(split(ref[e]), False), False)
-    send_rows(count, far_ref, out_refs)
+    whole, ahead = parted(count)
+    send_rows(count, [near_ref, far_ref], out_refs[: len(whole)], whole)
+    send_rows(count, [far_ref], out_refs[len(whole) :], ahead)
+
+
+def parted(count):
+    return [step for step in range(count) if step < AHEAD], [
+        step for step in range(count) if step >= AHEAD
+    ]
 
 
 def assemble_kernel(count, *refs):
-    near_refs, far_refs = refs[:count], refs[count : 2 * count]
-    diagonal_ref, coupling_ref = refs[2 * count :]
+    whole, ahead = parted(count)
+    whole_refs, refs = refs[: len(whole)], refs[len(whole) :]
+    near_refs, refs = refs[: len(ahead)], refs[len(ahead) :]
+    far_refs, (diagonal_ref, coupling_ref) = refs[: len(ahead)], refs[len(ahead) :]
     elements = diagonal_ref.shape[2]
     me = lax.axis_index("ez")
-    for step in range(count):
-        z = lax.rem(me + (count - step), count)
-        diagonal_ref[:, z] = near_refs[step][:, :elements]
-        coupling_ref[:, z, 1] = near_refs[step][:, elements:]
-        coupling_ref[:, z, 0] = far_refs[step][:, :elements]
-        coupling_ref[:, z, 2] = far_refs[step][:, elements:]
+
+    def place(step, near_ref, far_ref, far_at):
+        z = me ^ step if count & (count - 1) == 0 else lax.rem(me + (count - step), count)
+        diagonal_ref[:, z] = near_ref[:, :elements]
+        coupling_ref[:, z, 1] = near_ref[:, elements : 2 * elements]
+        coupling_ref[:, z, 0] = far_ref[:, far_at : far_at + elements]
+        coupling_ref[:, z, 2] = far_ref[:, far_at + elements : far_at + 2 * elements]
+
+    for step, ref in zip(whole, whole_refs):
+        place(step, ref, ref, 2 * elements)
+    for step, near_ref, far_ref in zip(ahead, near_refs, far_refs):
+        place(step, near_ref, far_ref, 0)
 
 
 def vmem(count):
@@ -497,6 +522,13 @@
 def shift(block, axis, distance):
     count = lax.axis_size(axis)
     return lax.ppermute(block, axis, [(i, (i + distance) % count) for i in range(count)])
+
+
+def exchange(block, step):
+    count = lax.axis_size("ez")
+    if step == 0:
+        return block
+    return lax.ppermute(block, "ez", [(i, partner(i, step, count)) for i in range(count)])
 
 
 def local(potential, basis_start):
@@ -563,33 +595,35 @@
 
     next_x = shift(minus_x, "ex", -1)
     next_z = shift(minus_z, "ez", -1)
+    whole, ahead = parted(count)
     block = shape((columns // count, 2 * elements, columns), f32)
-    plus, *near = pl.pallas_call(
+    double = shape((columns // count, 4 * elements, columns), f32)
+    squares = shape((2, elements, columns, columns), f32)
+    plus, own_near, *near = pl.pallas_call(
         functools.partial(near_kernel, count, margin),
-        out_shape=[shape((elements, 2, columns, 2 * G * G), f32)] + [block] * count,
+        out_shape=[shape((elements, 2, columns, 2 * G * G), f32), squares] + [block] * len(ahead),
         in_specs=vmem(3),
-        out_specs=vmem(1 + count),
+        out_specs=vmem(2 + len(ahead)),
         scratch_shapes=[
             pltpu.VMEM((elements, G**3, 2 * columns), bf16),
             pltpu.VMEM((elements, G**3, 2 * columns), bf16),
-            pltpu.VMEM((2, elements, columns, columns), f32),
         ],
         compiler_params=pltpu.CompilerParams(vmem_limit_bytes=24 * 2**20),
         cost_estimate=pl.CostEstimate(flops=10**8, bytes_accessed=10**7, transcendentals=0),
         name="near",
     )(inverse, filtered, whole_scaled)
-    near = list(near[:1]) + [shift(near[step], "ez", step) for step in range(1, count)]
+    near = [exchange(value, step) for value, step in zip(near, ahead)]
 
     far = pl.pallas_call(
         functools.partial(far_kernel, count),
-        out_shape=[block] * count,
-        in_specs=vmem(3),
+        out_shape=[double] * len(whole) + [block] * len(ahead),
+        in_specs=vmem(4),
         out_specs=vmem(count),
-        scratch_shapes=[pltpu.VMEM((2, elements, columns, columns), f32)],
+        scratch_shapes=[pltpu.VMEM(squares.shape, f32)],
         compiler_params=pltpu.CompilerParams(vmem_limit_bytes=16 * 2**20),
         name="far",
-    )(plus, next_x, next_z)
-    far = list(far[:1]) + [shift(far[step], "ez", step) for step in range(1, count)]
+    )(plus, next_x, next_z, own_near)
+    far = [exchange(value, step) for value, step in zip(far, whole + ahead)]
 
     rows = columns // count
     diagonal, coupled = pl.pallas_call(
@@ -598,11 +632,11 @@
             shape((rows, count, elements, columns), f32),
             shape((rows, count, 3, elements, columns), f32),
         ],
-        in_specs=vmem(2 * count),
+        in_specs=vmem(len(whole) + 2 * len(ahead)),
         out_specs=vmem(2),
         compiler_params=pltpu.CompilerParams(vmem_limit_bytes=16 * 2**20),
         name="assemble",
-    )(*near, *far)
+    )(*far[: len(whole)], *near, *far[len(whole) :])
     return (diagonal[None], coupled.transpose(0, 1, 3, 2, 4)[None])
 
 

time: 34.7 us -> 34.4 us (level)
  waiting for transfers between devices: 4.4 us -> 5.21 us
  starting transfers between devices: 15.5 us -> 14.8 us
    ppermute x14 -> x8, starting transfers between devices: 15.5 us -> 10.4 us  [shift(): lax.ppermute(block, axis, [(i, (i + distance) % count) for i in range(cou...]
    ppermute x0 -> x6, starting transfers between devices: none -> 4.35 us  [exchange(): lax.ppermute(block, 'ez', [(i, partner(i, step, count)) for i in range(co...]
    ppermute x0 -> x6, waiting for transfers between devices: none -> 3.85 us  [exchange(): lax.ppermute(block, 'ez', [(i, partner(i, step, count)) for i in range(co...]
    ppermute x14 -> x8, waiting for transfers between devices: 4.4 us -> 1.36 us  [shift(): lax.ppermute(block, axis, [(i, (i + distance) % count) for i in range(cou...]
  transfers between devices with their start and end apart: 14 -> 14, of which waited for: 3 -> 4; matrix products, arithmetic and copies ran while one was open for 2% -> 2% of each run, Pallas kernels for 17% -> 17%
where the time goes in v4:
time: 34.4 us; the launch traced here: 34.2 us
  starting transfers between devices  14.8 us (43%)
  Pallas kernels  11.5 us (33%)
  waiting for transfers between devices  5.21 us (15%)
  local copies, waits for them, and re-layouts  1.18 us (3%)
  other arithmetic  0.81 us (2%)
  between operations  0.73 us (2%)
    ppermute x8, starting transfers between devices, shift(): lax.ppermute(block, axis, [(i, (i + distance) % count) for i in range(cou...  10.4 us
    pallas_call x1, Pallas kernels, local(): pl.pallas_call(functools.partial(basis_kernel, margin), out_shape=[face,...  4.85 us
    ppermute x6, starting transfers between devices, exchange(): lax.ppermute(block, 'ez', [(i, partner(i, step, count)) for i in range(co...  4.35 us
    ppermute x6, waiting for transfers between devices, exchange(): lax.ppermute(block, 'ez', [(i, partner(i, step, count)) for i in range(co...  3.85 us
    pallas_call x1, Pallas kernels, local(): pl.pallas_call(functools.partial(middle_kernel, margin), out_shape=[field...  2.83 us
    pallas_call x1, Pallas kernels, local(): pl.pallas_call(functools.partial(near_kernel, count, margin), out_shape=[...  1.43 us
    ppermute x8, waiting for transfers between devices, shift(): lax.ppermute(block, axis, [(i, (i + distance) % count) for i in range(cou...  1.36 us
    unnamed x2, local copies, waits for them, and re-layouts  1.17 us
  transfers between devices with their start and end apart: 14, of which 4 were waited for; matrix products, arithmetic and copies ran while one was open for 2% of the time, Pallas kernels for 17%

profile of v4, /device:TPU:0, one launch (start us, length us, event | category | flops | bytes accessed | tf_op | source)
XLA Modules:
  0.0 34.2 jit_solution(11548993621039661107)
XLA Ops:
  0.6 3.0 %collective-permute-start.3 = (f32[8,8,16]{2,1,0:T(8,128)}, f32[8,8,16]{2,1,0:T(8,128)S(1)}, u32[]{:S(2)}, u32[]{:S(2)}) collective-permute-start(f32[8,8,16]{2,1,0:T(8,128)} %bitcast.8), channel_id=1, source_target_pairs={{0,4},{4,8},{8,12},{12,16},{16,20},{20,24},{24,28},{28,0},{1,5},{5... | collective-permute-start | bytes 12296 | tf_op jit(solution)/shard_map/ppermute | solution.py:524
  3.6 0.8 %add_multiply_fusion = f32[8,8,16]{2,1,0:T(8,128)S(1)} fusion(f32[8,16,8]{1,2,0:T(8,128)} %param.2), kind=kLoop, calls=%fused_computation.1 | loop fusion | flops 2048 | bytes 8192 | tf_op jit(solution)/shard_map/mul | solution.py:542
  4.4 3.0 %collective-permute-start = (f32[2,8,16]{2,1,0:T(8,128)S(1)}, f32[2,8,16]{2,1,0:T(8,128)S(1)}, u32[]{:S(2)}, u32[]{:S(2)}) collective-permute-start(f32[2,8,16]{2,1,0:T(8,128)S(1)} %slice.24), channel_id=1, source_target_pairs={{0,28},{4,0},{8,4},{12,8},{16,12},{20,16},{24,20},{28,24},{1,29},{... | collective-permute-start | bytes 3080 | tf_op jit(solution)/shard_map/ppermute | solution.py:524
  7.5 0.0 copy-start
  7.5 1.2 %copy-done = bf16[1,1,2,1728,128]{4,3,2,1,0:T(8,128)(2,1)S(1)} copy-done((bf16[1,1,2,1728,128]{4,3,2,1,0:T(8,128)(2,1)S(1)}, bf16[1,1,2,1728,128]{4,3,2,1,0:T(8,128)(2,1)}, u32[]{:S(2)}) %copy-start) | copy-done | bytes 884760
  8.7 1.0 %first.1 = (f32[2,14,208,128]{3,2,1,0:T(8,128)S(1)}, f32[2,14,208,128]{3,2,1,0:T(8,128)S(1)}) custom-call(bf16[2,1728,128]{2,1,0:T(8,128)(2,1)S(1)} %bitcast.7), custom_call_target="tpu_custom_call" | custom-call | flops 100000 | bytes 10000 | tf_op jit(solution)/shard_map/first/pallas_call | solution.py:549
  9.7 0.0 collective-permute-done.3
  9.8 0.7 %collective-permute-start.5 = (f32[10,2,16]{2,1,0:T(2,128)S(1)}, f32[10,2,16]{2,1,0:T(2,128)S(1)}, u32[]{:S(2)}, u32[]{:S(2)}) collective-permute-start(f32[10,2,16]{2,1,0:T(2,128)S(1)} %get-tuple-element.48), channel_id=1, source_target_pairs={{0,3},{1,0},{2,1},{3,2},{4,7},{5,4},{6,5},{7,6},{8,11},{9,8},{10,9... | collective-permute-start | bytes 3848 | tf_op jit(solution)/shard_map/ppermute | solution.py:524
  10.5 0.0 collective-permute-start.4
  10.5 0.0 collective-permute-done.x_after_ref
  10.5 1.7 %collective-permute-start.2 = (f32[2,2,16]{2,1,0:T(2,128)S(1)}, f32[2,2,16]{2,1,0:T(2,128)S(1)}, u32[]{:S(2)}, u32[]{:S(2)}) collective-permute-start(f32[2,2,16]{2,1,0:T(2,128)S(1)} %get-tuple-element.50), channel_id=1, source_target_pairs={{0,3},{1,0},{2,1},{3,2},{4,7},{5,4},{6,5},{7,6},{8,11},{9,8},{10,9... | collective-permute-start | bytes 776 | tf_op jit(solution)/shard_map/ppermute | solution.py:524
  12.2 0.0 collective-permute-start.1
  12.2 0.0 collective-permute-done.5.z_after_ref
  12.2 1.3 %collective-permute-done.4.z_before_ref = f32[10,2,16]{2,1,0:T(2,128)S(1)} collective-permute-done((f32[10,2,16]{2,1,0:T(2,128)S(1)}, f32[10,2,16]{2,1,0:T(2,128)S(1)}, u32[]{:S(2)}, u32[]{:S(2)}) %collective-permute-start.4) | collective-permute-done | bytes 1312 | tf_op jit(solution)/shard_map/ppermute | solution.py:524
  13.6 2.8 %middle.1 = (f32[2,14,208,128]{3,2,1,0:T(8,128)S(1)}, f32[2,14,208,128]{3,2,1,0:T(8,128)S(1)}, f32[12,16,16,128]{3,2,1,0:T(8,128)S(1)}, bf16[2,2304,256]{2,1,0:T(8,128)(2,1)S(1)}, f32[2,128,256]{2,1,0:T(8,128)S(1)}) custom-call(f32[10,8,16]{2,1,0:T(8,128)S(1)} %pad_maximum_fusion.low_ref, ...), custom_call_target="tpu_custom_call", output_to_operand_aliasing={{0}: (3, {}), {1}: (4, {})} | custom-call | flops 100000000 | bytes 10000000 | tf_op jit(solution)/shard_map/middle/pallas_call | solution.py:567
  16.4 0.0 collective-permute-done.2.z_after_ref
  16.4 0.0 collective-permute-done.1.z_before_ref
  16.4 4.9 %basis.1 = (f32[2,128,128]{2,1,0:T(8,128)S(1)}, f32[2,128,128]{2,1,0:T(8,128)S(1)}, f32[2,128,128]{2,1,0:T(8,128)S(1)}, f32[2,14,208,128]{3,2,1,0:T(8,128)S(1)},...) custom-call(f32[2,8,16]{2,1,0:T(8,128)S(1)} %collective-permute-done, ...), custom_call_target="tpu_custom_call", output_to_operand_aliasing={{3}: (3, {}), {4}: (4, {}), {5}: (5, {}), {6}: (6, {})} | custom-call | tf_op jit(solution)/shard_map/basis/pallas_call | solution.py:581
  21.3 1.8 %collective-permute-start.6 = (f32[2,128,128]{2,1,0:T(8,128)S(1)}, f32[2,128,128]{2,1,0:T(8,128)S(1)}, u32[]{:S(2)}, u32[]{:S(2)}) collective-permute-start(f32[2,128,128]{2,1,0:T(8,128)S(1)} %get-tuple-element.36), channel_id=1, source_target_pairs={{0,28},{4,0},{8,4},{12,8},{16,12},{20,16},{24,20},{28,24},{1,29},{... | collective-permute-start | bytes 393224 | tf_op jit(solution)/shard_map/ppermute | solution.py:524
  23.1 0.1 collective-permute-start.7
  23.2 1.4 %near.1 = (f32[2,2,128,128]{3,2,1,0:T(8,128)S(1)}, f32[2,2,128,128]{3,2,1,0:T(8,128)S(1)}, f32[32,4,128]{2,1,0:T(4,128)S(1)}, f32[32,4,128]{2,1,0:T(4,128)S(1)}, f32[32,4,128]{2,1,0:T(4,128)S(1)}) custom-call(f32[2,128,128]{2,1,0:T(8,128)S(1)} %get-tuple-element.32.inverse_ref, f32[2,14,208,128]{3,2,1,0:T(8,128)S(1)} %get-tuple-element.33.field, ...), custom_call_target="tpu_custom_call" | custom-call | flops 100000000 | bytes 10000000 | tf_op jit(solution)/shard_map/near/pallas_call | solution.py:602
  24.6 0.4 %collective-permute-start.8 = (f32[32,4,128]{2,1,0:T(4,128)S(1)}, f32[32,4,128]{2,1,0:T(4,128)S(1)}, u32[]{:S(2)}, u32[]{:S(2)}) collective-permute-start(f32[32,4,128]{2,1,0:T(4,128)S(1)} %get-tuple-element.40), channel_id=1, source_target_pairs={{0,1},{1,0},{2,3},{3,2},{4,5},{5,4},{6,7},{7,6},{8,9},{9,8},{10,11... | collective-permute-start | bytes 196616 | tf_op jit(solution)/shard_map/ppermute | solution.py:531
  25.1 1.2 %collective-permute-start.9 = (f32[32,4,128]{2,1,0:T(4,128)S(1)}, f32[32,4,128]{2,1,0:T(4,128)S(1)}, u32[]{:S(2)}, u32[]{:S(2)}) collective-permute-start(f32[32,4,128]{2,1,0:T(4,128)S(1)} %get-tuple-element.41), channel_id=1, source_target_pairs={{0,2},{1,3},{2,0},{3,1},{4,6},{5,7},{6,4},{7,5},{8,10},{9,11},{10,... | collective-permute-start | bytes 196616 | tf_op jit(solution)/shard_map/ppermute | solution.py:531
  26.3 0.2 collective-permute-start.10
  26.6 0.0 collective-permute-done.6.next_x_ref
  26.6 0.0 collective-permute-done.7.next_z_ref
  26.6 0.4 %far.1 = (f32[32,8,128]{2,1,0:T(8,128)S(1)}, f32[32,4,128]{2,1,0:T(4,128)S(1)}, f32[32,4,128]{2,1,0:T(4,128)S(1)}, f32[32,4,128]{2,1,0:T(4,128)S(1)}) custom-call(f32[2,2,128,128]{3,2,1,0:T(8,128)S(1)} %get-tuple-element.35.plus_ref, f32[2,128,128]{2,1,0:T(8,128)S(1)} %collective-permute-done.6.next_x_ref, ...), custom_call_target="tpu_custom_call" | custom-call | tf_op jit(solution)/shard_map/far/pallas_call | solution.py:617
  27.0 1.0 %collective-permute-start.11 = (f32[32,4,128]{2,1,0:T(4,128)S(1)}, f32[32,4,128]{2,1,0:T(4,128)S(1)}, u32[]{:S(2)}, u32[]{:S(2)}) collective-permute-start(f32[32,4,128]{2,1,0:T(4,128)S(1)} %get-tuple-element.43), channel_id=1, source_target_pairs={{0,1},{1,0},{2,3},{3,2},{4,5},{5,4},{6,7},{7,6},{8,9},{9,8},{10,11... | collective-permute-start | bytes 196616 | tf_op jit(solution)/shard_map/ppermute | solution.py:531
  28.0 1.0 %collective-permute-start.12 = (f32[32,4,128]{2,1,0:T(4,128)S(1)}, f32[32,4,128]{2,1,0:T(4,128)S(1)}, u32[]{:S(2)}, u32[]{:S(2)}) collective-permute-start(f32[32,4,128]{2,1,0:T(4,128)S(1)} %get-tuple-element.44), channel_id=1, source_target_pairs={{0,2},{1,3},{2,0},{3,1},{4,6},{5,7},{6,4},{7,5},{8,10},{9,11},{10,... | collective-permute-start | bytes 196616 | tf_op jit(solution)/shard_map/ppermute | solution.py:531
  28.9 0.0 collective-permute-done.8.refs_1_
  28.9 0.5 %collective-permute-start.13 = (f32[32,4,128]{2,1,0:T(4,128)S(1)}, f32[32,4,128]{2,1,0:T(4,128)S(1)}, u32[]{:S(2)}, u32[]{:S(2)}) collective-permute-start(f32[32,4,128]{2,1,0:T(4,128)S(1)} %get-tuple-element.45), channel_id=1, source_target_pairs={{0,3},{1,2},{2,1},{3,0},{4,7},{5,6},{6,5},{7,4},{8,11},{9,10},{10,... | collective-permute-start | bytes 196616 | tf_op jit(solution)/shard_map/ppermute | solution.py:531
  29.4 0.0 collective-permute-done.9.refs_2_
  29.4 1.0 %collective-permute-done.10.refs_3_ = f32[32,4,128]{2,1,0:T(4,128)S(1)} collective-permute-done((f32[32,4,128]{2,1,0:T(4,128)S(1)}, f32[32,4,128]{2,1,0:T(4,128)S(1)}, u32[]{:S(2)}, u32[]{:S(2)}) %collective-permute-start.10) | collective-permute-done | bytes 65568 | tf_op jit(solution)/shard_map/ppermute | solution.py:531
  30.4 0.0 collective-permute-done.11.refs_4_
  30.4 2.2 %collective-permute-done.12.refs_5_ = f32[32,4,128]{2,1,0:T(4,128)S(1)} collective-permute-done((f32[32,4,128]{2,1,0:T(4,128)S(1)}, f32[32,4,128]{2,1,0:T(4,128)S(1)}, u32[]{:S(2)}, u32[]{:S(2)}) %collective-permute-start.12) | collective-permute-done | bytes 65568 | tf_op jit(solution)/shard_map/ppermute | solution.py:531
  32.6 0.6 %collective-permute-done.13.refs_6_ = f32[32,4,128]{2,1,0:T(4,128)S(1)} collective-permute-done((f32[32,4,128]{2,1,0:T(4,128)S(1)}, f32[32,4,128]{2,1,0:T(4,128)S(1)}, u32[]{:S(2)}, u32[]{:S(2)}) %collective-permute-start.13) | collective-permute-done | bytes 65568 | tf_op jit(solution)/shard_map/ppermute | solution.py:531
  33.2 1.0 %assemble.1 = (f32[32,4,2,128]{3,2,1,0:T(2,128)}, f32[32,4,3,2,128]{4,3,2,1,0:T(2,128)}) custom-call(f32[32,8,128]{2,1,0:T(8,128)S(1)} %get-tuple-element.39.refs_0_, f32[32,4,128]{2,1,0:T(4,128)S(1)} %collective-permute-done.8.refs_1_, f32[32,4,128]{2,1,0:T(4,128)S(1)} %collective-permute-done.9.refs_2_, f32[32,4,128]{2,1,0:T(4,128)S(1)} %collective-permute-done.10.refs_3_, ...), custom_call_target="tpu_custom_call" | custom-call | tf_op jit(solution)/shard_map/assemble/pallas_call | solution.py:629
  (5 shorter events, 0.0 us)
Async XLA Ops:
  0.6 9.1 %collective-permute-start.3 = (f32[8,8,16]{2,1,0:T(8,128)}, f32[8,8,16]{2,1,0:T(8,128)S(1)}, u32[]{:S(2)}, u32[]{:S(2)}) collective-permute-start(f32[8,8,16]{2,1,0:T(8,128)} %bitcast.8), channel_id=1, source_target_pairs={{0,4},{4,8},{8,12},{12,16},{16,20},{20,24},{24,28},{28,0},{1,5},{5... | collective-permute-start | bytes 12296 | tf_op jit(solution)/shard_map/ppermute | solution.py:524
  4.4 6.0 %collective-permute-start = (f32[2,8,16]{2,1,0:T(8,128)S(1)}, f32[2,8,16]{2,1,0:T(8,128)S(1)}, u32[]{:S(2)}, u32[]{:S(2)}) collective-permute-start(f32[2,8,16]{2,1,0:T(8,128)S(1)} %slice.24), channel_id=1, source_target_pairs={{0,28},{4,0},{8,4},{12,8},{16,12},{20,16},{24,20},{28,24},{1,29},{... | collective-permute-start | bytes 3080 | tf_op jit(solution)/shard_map/ppermute | solution.py:524
  7.5 1.2 %copy-start = (bf16[1,1,2,1728,128]{4,3,2,1,0:T(8,128)(2,1)S(1)}, bf16[1,1,2,1728,128]{4,3,2,1,0:T(8,128)(2,1)}, u32[]{:S(2)}) copy-start(bf16[1,1,2,1728,128]{4,3,2,1,0:T(8,128)(2,1)} %param.3) | copy-start | bytes 2654212
  9.8 2.5 %collective-permute-start.5 = (f32[10,2,16]{2,1,0:T(2,128)S(1)}, f32[10,2,16]{2,1,0:T(2,128)S(1)}, u32[]{:S(2)}, u32[]{:S(2)}) collective-permute-start(f32[10,2,16]{2,1,0:T(2,128)S(1)} %get-tuple-element.48), channel_id=1, source_target_pairs={{0,3},{1,0},{2,1},{3,2},{4,7},{5,4},{6,5},{7,6},{8,11},{9,8},{10,9... | collective-permute-start | bytes 3848 | tf_op jit(solution)/shard_map/ppermute | solution.py:524
  10.5 3.1 %collective-permute-start.4 = (f32[10,2,16]{2,1,0:T(2,128)S(1)}, f32[10,2,16]{2,1,0:T(2,128)S(1)}, u32[]{:S(2)}, u32[]{:S(2)}) collective-permute-start(f32[10,2,16]{2,1,0:T(2,128)S(1)} %get-tuple-element.49), channel_id=1, source_target_pairs={{0,1},{1,2},{2,3},{3,0},{4,5},{5,6},{6,7},{7,4},{8,9},{9,10},{10,1... | collective-permute-start | bytes 3848 | tf_op jit(solution)/shard_map/ppermute | solution.py:524
  10.5 5.9 %collective-permute-start.2 = (f32[2,2,16]{2,1,0:T(2,128)S(1)}, f32[2,2,16]{2,1,0:T(2,128)S(1)}, u32[]{:S(2)}, u32[]{:S(2)}) collective-permute-start(f32[2,2,16]{2,1,0:T(2,128)S(1)} %get-tuple-element.50), channel_id=1, source_target_pairs={{0,3},{1,0},{2,1},{3,2},{4,7},{5,4},{6,5},{7,6},{8,11},{9,8},{10,9... | collective-permute-start | bytes 776 | tf_op jit(solution)/shard_map/ppermute | solution.py:524
  12.2 4.2 %collective-permute-start.1 = (f32[2,2,16]{2,1,0:T(2,128)S(1)}, f32[2,2,16]{2,1,0:T(2,128)S(1)}, u32[]{:S(2)}, u32[]{:S(2)}) collective-permute-start(f32[2,2,16]{2,1,0:T(2,128)S(1)} %get-tuple-element.51), channel_id=1, source_target_pairs={{0,1},{1,2},{2,3},{3,0},{4,5},{5,6},{6,7},{7,4},{8,9},{9,10},{10,1... | collective-permute-start | bytes 776 | tf_op jit(solution)/shard_map/ppermute | solution.py:524
  21.3 5.3 %collective-permute-start.6 = (f32[2,128,128]{2,1,0:T(8,128)S(1)}, f32[2,128,128]{2,1,0:T(8,128)S(1)}, u32[]{:S(2)}, u32[]{:S(2)}) collective-permute-start(f32[2,128,128]{2,1,0:T(8,128)S(1)} %get-tuple-element.36), channel_id=1, source_target_pairs={{0,28},{4,0},{8,4},{12,8},{16,12},{20,16},{24,20},{28,24},{1,29},{... | collective-permute-start | bytes 393224 | tf_op jit(solution)/shard_map/ppermute | solution.py:524
  23.1 3.5 %collective-permute-start.7 = (f32[2,128,128]{2,1,0:T(8,128)S(1)}, f32[2,128,128]{2,1,0:T(8,128)S(1)}, u32[]{:S(2)}, u32[]{:S(2)}) collective-permute-start(f32[2,128,128]{2,1,0:T(8,128)S(1)} %get-tuple-element.37), channel_id=1, source_target_pairs={{0,3},{1,0},{2,1},{3,2},{4,7},{5,4},{6,5},{7,6},{8,11},{9,8},{10,9... | collective-permute-start | bytes 393224 | tf_op jit(solution)/shard_map/ppermute | solution.py:524
  24.6 4.3 %collective-permute-start.8 = (f32[32,4,128]{2,1,0:T(4,128)S(1)}, f32[32,4,128]{2,1,0:T(4,128)S(1)}, u32[]{:S(2)}, u32[]{:S(2)}) collective-permute-start(f32[32,4,128]{2,1,0:T(4,128)S(1)} %get-tuple-element.40), channel_id=1, source_target_pairs={{0,1},{1,0},{2,3},{3,2},{4,5},{5,4},{6,7},{7,6},{8,9},{9,8},{10,11... | collective-permute-start | bytes 196616 | tf_op jit(solution)/shard_map/ppermute | solution.py:531
  25.1 4.3 %collective-permute-start.9 = (f32[32,4,128]{2,1,0:T(4,128)S(1)}, f32[32,4,128]{2,1,0:T(4,128)S(1)}, u32[]{:S(2)}, u32[]{:S(2)}) collective-permute-start(f32[32,4,128]{2,1,0:T(4,128)S(1)} %get-tuple-element.41), channel_id=1, source_target_pairs={{0,2},{1,3},{2,0},{3,1},{4,6},{5,7},{6,4},{7,5},{8,10},{9,11},{10,... | collective-permute-start | bytes 196616 | tf_op jit(solution)/shard_map/ppermute | solution.py:531
  26.3 4.1 %collective-permute-start.10 = (f32[32,4,128]{2,1,0:T(4,128)S(1)}, f32[32,4,128]{2,1,0:T(4,128)S(1)}, u32[]{:S(2)}, u32[]{:S(2)}) collective-permute-start(f32[32,4,128]{2,1,0:T(4,128)S(1)} %get-tuple-element.42), channel_id=1, source_target_pairs={{0,3},{1,2},{2,1},{3,0},{4,7},{5,6},{6,5},{7,4},{8,11},{9,10},{10,... | collective-permute-start | bytes 196616 | tf_op jit(solution)/shard_map/ppermute | solution.py:531
  27.0 3.5 %collective-permute-start.11 = (f32[32,4,128]{2,1,0:T(4,128)S(1)}, f32[32,4,128]{2,1,0:T(4,128)S(1)}, u32[]{:S(2)}, u32[]{:S(2)}) collective-permute-start(f32[32,4,128]{2,1,0:T(4,128)S(1)} %get-tuple-element.43), channel_id=1, source_target_pairs={{0,1},{1,0},{2,3},{3,2},{4,5},{5,4},{6,7},{7,6},{8,9},{9,8},{10,11... | collective-permute-start | bytes 196616 | tf_op jit(solution)/shard_map/ppermute | solution.py:531
  28.0 4.6 %collective-permute-start.12 = (f32[32,4,128]{2,1,0:T(4,128)S(1)}, f32[32,4,128]{2,1,0:T(4,128)S(1)}, u32[]{:S(2)}, u32[]{:S(2)}) collective-permute-start(f32[32,4,128]{2,1,0:T(4,128)S(1)} %get-tuple-element.44), channel_id=1, source_target_pairs={{0,2},{1,3},{2,0},{3,1},{4,6},{5,7},{6,4},{7,5},{8,10},{9,11},{10,... | collective-permute-start | bytes 196616 | tf_op jit(solution)/shard_map/ppermute | solution.py:531
  28.9 4.3 %collective-permute-start.13 = (f32[32,4,128]{2,1,0:T(4,128)S(1)}, f32[32,4,128]{2,1,0:T(4,128)S(1)}, u32[]{:S(2)}, u32[]{:S(2)}) collective-permute-start(f32[32,4,128]{2,1,0:T(4,128)S(1)} %get-tuple-element.45), channel_id=1, source_target_pairs={{0,3},{1,2},{2,1},{3,0},{4,7},{5,6},{6,5},{7,4},{8,11},{9,10},{10,... | collective-permute-start | bytes 196616 | tf_op jit(solution)/shard_map/ppermute | solution.py:531

commit v5 on v4

--- a/solution.py
+++ b/solution.py
@@ -55,12 +55,6 @@
     return jnp.broadcast_to(value[:, k : k + 1], (value.shape[0], lanes))
 
 
-def triple(value):
-    high, rest = split(value)
-    low = (value - high.astype(f32) - rest.astype(f32)).astype(bf16)
-    return high, rest, low
-
-
 def pack(values):
     first, second = values
     half = first.shape[1] // 2
@@ -77,6 +71,44 @@
     return terms[0]
 
 
+def triple(value):
+    high = value.astype(bf16).astype(f32)
+    middle = (value - high).astype(bf16).astype(f32)
+    return high, middle, value - high - middle
+
+
+def far_rows(value, solved, at):
+    size = value.shape[1]
+    half = size // 2
+    lane = lax.broadcasted_iota(jnp.int32, value.shape, 1) % half
+    parts = triple(jnp.where((lane >= at) & (lane < at + BLOCK), value, 0.0))
+    left = lax.broadcasted_iota(jnp.int32, (BLOCK, size), 1) < half
+    taken = [[], []]
+    for part in solved:
+        pieces = triple(part)
+        taken[0].append([jnp.where(left, piece, 0.0).astype(bf16) for piece in pieces])
+        taken[1].append([jnp.where(left, 0.0, piece).astype(bf16) for piece in pieces])
+    nothing = jnp.zeros((BLOCK, size * len(solved)), bf16)
+    spots = half // BLOCK
+    pairs = ((0, 0), (0, 1), (1, 0), (0, 2), (2, 0), (1, 1))
+    operands, tiles = [], []
+    for first in range(0, len(pairs), spots):
+        operand, group = None, [nothing] * (2 * spots)
+        for i, (mine, theirs) in enumerate(pairs[first : first + spots]):
+            moved = pltpu.roll(parts[mine], i * BLOCK, 1) if i else parts[mine]
+            operand = moved if operand is None else operand + moved
+            for side in range(2):
+                spot = (side * spots + at // BLOCK + i) % (2 * spots)
+                group[spot] = jnp.concatenate([t[theirs] for t in taken[side]], axis=1)
+        operands.append(operand.astype(bf16))
+        tiles += group
+    return jnp.dot(
+        jnp.concatenate(operands, axis=1),
+        jnp.concatenate(tiles, axis=0),
+        preferred_element_type=f32,
+    )
+
+
 def inverse_factors(matrix_ref, inverse_ref):
     size = matrix_ref.shape[1]
     half = size // 2
@@ -87,64 +119,55 @@
     def columns_of(value, at):
         return jnp.take_along_axis(value, other + at, axis=1)
 
-    for top in (0, half):
-        parts = (0, 1, 2) if top == 0 else (1, 2, 3)
-        pivot_part = 0 if top == 0 else 1
-        kept = []
-        for start in range(top, top + half, BLOCK):
-            rows = slice(start, start + BLOCK)
-            panel = [matrix_ref[part, rows, :] for part in parts]
-            at = start - top
-            columns = [columns_of(panel[0], at + j) for j in range(BLOCK)]
-            pivot_rows = list(panel)
-            pivot = bcast_row(columns[0], 0)
-            pivots = pivot
-            for k in range(BLOCK):
-                reciprocal = 1.0 / pivot
-                if k > 0:
-                    pivots = jnp.where(row >= k, pivot, pivots)
-                    pivot_rows = [
-                        jnp.where(row >= k, new, old) for new, old in zip(panel, pivot_rows)
-                    ]
-                if k + 1 < BLOCK:
-                    beside = bcast_row(columns[k + 1], k)
-                    pivot = bcast_row(columns[k + 1], k + 1) - (beside * beside) * reciprocal
-                factor = jnp.where(row == k, 0.0, columns[k]) * reciprocal
-                for j in range(k + 1, BLOCK):
-                    columns[j] = columns[j] - factor * bcast_row(columns[j], k)
-                panel = [value - factor * bcast_row(value, k) for value in panel]
-            reciprocals = 1.0 / pivots
-            solved = [value * reciprocals for value in panel]
-            scale = lax.rsqrt(pivots)
-            kept.append([value * scale for value in pivot_rows])
-            inverse_ref[0, rows, :] = kept[-1][parts.index(2)]
-            if 3 in parts:
-                inverse_ref[1, rows, :] = kept[-1][parts.index(3)]
+    parts = (0, 1, 2)
+    panel = [matrix_ref[part, :BLOCK, :] for part in parts]
+    columns = [columns_of(panel[0], j) for j in range(BLOCK)]
+    for start in range(0, size, BLOCK):
+        rows = slice(start, start + BLOCK)
+        at = start % half
+        pivot_rows = list(panel)
+        pivot = bcast_row(columns[0], 0)
+        for k in range(BLOCK):
+            reciprocal = 1.0 / pivot
+            if k == 0:
+                pivots, reciprocals = pivot, reciprocal
             else:
-                inverse_ref[1, rows, :] = jnp.zeros((BLOCK, size), f32)
-            for below in range(start + BLOCK, top + half, BLOCK):
-                rows = slice(below, below + BLOCK)
-                values = [matrix_ref[part, rows, :] for part in parts]
-                factors = [columns_of(values[0], at + k) for k in range(BLOCK)]
-                for part, value, taken in zip(parts, values, solved):
-                    terms = [factors[k] * bcast_row(taken, k) for k in range(BLOCK)]
-                    matrix_ref[part, rows, :] = value - tree_sum(terms)
-        if top == 0:
-            right = [jnp.concatenate([k[i] for k in kept], axis=0) for i in (1, 2)]
-            left = triple(right[0])
-            both = [jnp.concatenate(p, axis=1) for p in zip(left, triple(right[1]))]
-            order = ((0, 0), (0, 1), (1, 0), (0, 2), (2, 0), (1, 1))
-            taken = lax.dot_general(
-                jnp.concatenate([left[i] for i, _ in order], axis=0),
-                jnp.concatenate([both[j] for _, j in order], axis=0),
-                (((0,), (0,)), ((), ())),
-                preferred_element_type=f32,
-            )
-            is_left = lax.broadcasted_iota(jnp.int32, (half, size), 1) < half
-            for i, part in enumerate((1, 2)):
-                at = slice(size * i, size * (i + 1))
-                mine = jnp.where(is_left, taken[:half, at], taken[half:, at])
-                matrix_ref[part, half:, :] = matrix_ref[part, half:, :] - mine
+                later = row >= k
+                pivots = jnp.where(later, pivot, pivots)
+                reciprocals = jnp.where(later, reciprocal, reciprocals)
+                pivot_rows = [jnp.where(later, new, old) for new, old in zip(panel, pivot_rows)]
+            if k + 1 < BLOCK:
+                beside = bcast_row(columns[k + 1], k)
+                pivot = bcast_row(columns[k + 1], k + 1) - (beside * beside) * reciprocal
+            factor = jnp.where(row == k, 0.0, columns[k]) * reciprocal
+            for j in range(k + 1, BLOCK):
+                columns[j] = columns[j] - factor * bcast_row(columns[j], k)
+            panel = [value - factor * bcast_row(value, k) for value in panel]
+        solved = [value * reciprocals for value in panel]
+        scale = lax.rsqrt(pivots)
+        kept = [value * scale for value in pivot_rows]
+        inverse_ref[0, rows, :] = kept[parts.index(2)]
+        inverse_ref[1, rows, :] = kept[parts.index(3)] if 3 in parts else jnp.zeros_like(scale)
+        below = start + BLOCK
+        if below == size:
+            break
+        values = [matrix_ref[part, below : below + BLOCK, :] for part in parts]
+        factors = [columns_of(values[0], at + k) for k in range(BLOCK)]
+        panel = []
+        for value, taken in zip(values, solved):
+            terms = [factors[k] * bcast_row(taken, k) for k in range(BLOCK)]
+            panel.append(value - tree_sum(terms))
+        if below == half:
+            panel = panel[1:] + [matrix_ref[3, below : below + BLOCK, :]]
+        columns = [columns_of(panel[0], below % half + j) for j in range(BLOCK)]
+        rest = slice(below + BLOCK, size)
+        if below + BLOCK < size:
+            taken = far_rows(matrix_ref[parts[0], rest, :], solved, at)
+            for i, part in enumerate(parts):
+                mine = taken[:, i * size : (i + 1) * size]
+                matrix_ref[part, rest, :] = matrix_ref[part, rest, :] - mine
+        if below == half:
+            parts = (1, 2, 3)
 
 
 def zero_ends(ref, elements, side):
@@ -367,9 +390,12 @@
 
     for e in range(elements):
         held = weights(split(inverse_ref[e]), True)
-        for d, ref in ((0, minus_x_ref), (2, minus_z_ref)):
-            rows = layer(field, margin, e, d, 0) + layer(field, margin, e, d, 1)
-            ref[e] = product(jnp.concatenate(rows, 0), held, True)
+        rows = []
+        for d in (0, 2):
+            rows += layer(field, margin, e, d, 0) + layer(field, margin, e, d, 1)
+        faces = product(jnp.concatenate(rows, 0), held, True)
+        minus_x_ref[e] = faces[: 2 * G * G]
+        minus_z_ref[e] = faces[2 * G * G :]
 
 
 def near_kernel(

time: 34.4 us -> 33.7 us (0.980)
  Pallas kernels: 11.5 us -> 10.7 us
    pallas_call x1, Pallas kernels: 4.85 us -> 4.07 us  [local(): pl.pallas_call(functools.partial(basis_kernel, margin), out_shape=[face,...]
where the time goes in v5:
time: 33.7 us; the launch traced here: 33.4 us
  starting transfers between devices  14.8 us (44%)
  Pallas kernels  10.7 us (32%)
  waiting for transfers between devices  5.21 us (15%)
  local copies, waits for them, and re-layouts  1.18 us (4%)
  other arithmetic  0.81 us (2%)
  between operations  0.73 us (2%)
    ppermute x8, starting transfers between devices, shift(): lax.ppermute(block, axis, [(i, (i + distance) % count) for i in range(cou...  10.4 us
    ppermute x6, starting transfers between devices, exchange(): lax.ppermute(block, 'ez', [(i, partner(i, step, count)) for i in range(co...  4.35 us
    pallas_call x1, Pallas kernels, local(): pl.pallas_call(functools.partial(basis_kernel, margin), out_shape=[face,...  4.07 us
    ppermute x6, waiting for transfers between devices, exchange(): lax.ppermute(block, 'ez', [(i, partner(i, step, count)) for i in range(co...  3.85 us
    pallas_call x1, Pallas kernels, local(): pl.pallas_call(functools.partial(middle_kernel, margin), out_shape=[field...  2.83 us
    pallas_call x1, Pallas kernels, local(): pl.pallas_call(functools.partial(near_kernel, count, margin), out_shape=[...  1.43 us
    ppermute x8, waiting for transfers between devices, shift(): lax.ppermute(block, axis, [(i, (i + distance) % count) for i in range(cou...  1.36 us
    unnamed x2, local copies, waits for them, and re-layouts  1.17 us
  transfers between devices with their start and end apart: 14, of which 4 were waited for; matrix products, arithmetic and copies ran while one was open for 2% of the time, Pallas kernels for 17%

profile of v5, /device:TPU:0, one launch (start us, length us, event | category | flops | bytes accessed | tf_op | source)
XLA Modules:
  0.0 33.4 jit_solution(3336983331473400471)
XLA Ops:
  0.6 3.0 %collective-permute-start.3 = (f32[8,8,16]{2,1,0:T(8,128)}, f32[8,8,16]{2,1,0:T(8,128)S(1)}, u32[]{:S(2)}, u32[]{:S(2)}) collective-permute-start(f32[8,8,16]{2,1,0:T(8,128)} %bitcast.8), channel_id=1, source_target_pairs={{0,4},{4,8},{8,12},{12,16},{16,20},{20,24},{24,28},{28,0},{1,5},{5... | collective-permute-start | bytes 12296 | tf_op jit(solution)/shard_map/ppermute | solution.py:550
  3.6 0.8 %add_multiply_fusion = f32[8,8,16]{2,1,0:T(8,128)S(1)} fusion(f32[8,16,8]{1,2,0:T(8,128)} %param.2), kind=kLoop, calls=%fused_computation.1 | loop fusion | flops 2048 | bytes 8192 | tf_op jit(solution)/shard_map/mul | solution.py:568
  4.4 3.0 %collective-permute-start = (f32[2,8,16]{2,1,0:T(8,128)S(1)}, f32[2,8,16]{2,1,0:T(8,128)S(1)}, u32[]{:S(2)}, u32[]{:S(2)}) collective-permute-start(f32[2,8,16]{2,1,0:T(8,128)S(1)} %slice.24), channel_id=1, source_target_pairs={{0,28},{4,0},{8,4},{12,8},{16,12},{20,16},{24,20},{28,24},{1,29},{... | collective-permute-start | bytes 3080 | tf_op jit(solution)/shard_map/ppermute | solution.py:550
  7.5 0.0 copy-start
  7.5 1.2 %copy-done = bf16[1,1,2,1728,128]{4,3,2,1,0:T(8,128)(2,1)S(1)} copy-done((bf16[1,1,2,1728,128]{4,3,2,1,0:T(8,128)(2,1)S(1)}, bf16[1,1,2,1728,128]{4,3,2,1,0:T(8,128)(2,1)}, u32[]{:S(2)}) %copy-start) | copy-done | bytes 884760
  8.7 1.0 %first.1 = (f32[2,14,208,128]{3,2,1,0:T(8,128)S(1)}, f32[2,14,208,128]{3,2,1,0:T(8,128)S(1)}) custom-call(bf16[2,1728,128]{2,1,0:T(8,128)(2,1)S(1)} %bitcast.7), custom_call_target="tpu_custom_call" | custom-call | flops 100000 | bytes 10000 | tf_op jit(solution)/shard_map/first/pallas_call | solution.py:575
  9.7 0.0 collective-permute-done.3
  9.8 0.7 %collective-permute-start.5 = (f32[10,2,16]{2,1,0:T(2,128)S(1)}, f32[10,2,16]{2,1,0:T(2,128)S(1)}, u32[]{:S(2)}, u32[]{:S(2)}) collective-permute-start(f32[10,2,16]{2,1,0:T(2,128)S(1)} %get-tuple-element.48), channel_id=1, source_target_pairs={{0,3},{1,0},{2,1},{3,2},{4,7},{5,4},{6,5},{7,6},{8,11},{9,8},{10,9... | collective-permute-start | bytes 3848 | tf_op jit(solution)/shard_map/ppermute | solution.py:550
  10.5 0.0 collective-permute-start.4
  10.5 0.0 collective-permute-done.x_after_ref
  10.5 1.7 %collective-permute-start.2 = (f32[2,2,16]{2,1,0:T(2,128)S(1)}, f32[2,2,16]{2,1,0:T(2,128)S(1)}, u32[]{:S(2)}, u32[]{:S(2)}) collective-permute-start(f32[2,2,16]{2,1,0:T(2,128)S(1)} %get-tuple-element.50), channel_id=1, source_target_pairs={{0,3},{1,0},{2,1},{3,2},{4,7},{5,4},{6,5},{7,6},{8,11},{9,8},{10,9... | collective-permute-start | bytes 776 | tf_op jit(solution)/shard_map/ppermute | solution.py:550
  12.2 0.0 collective-permute-start.1
  12.2 0.0 collective-permute-done.5.z_after_ref
  12.2 1.3 %collective-permute-done.4.z_before_ref = f32[10,2,16]{2,1,0:T(2,128)S(1)} collective-permute-done((f32[10,2,16]{2,1,0:T(2,128)S(1)}, f32[10,2,16]{2,1,0:T(2,128)S(1)}, u32[]{:S(2)}, u32[]{:S(2)}) %collective-permute-start.4) | collective-permute-done | bytes 1312 | tf_op jit(solution)/shard_map/ppermute | solution.py:550
  13.6 2.8 %middle.1 = (f32[2,14,208,128]{3,2,1,0:T(8,128)S(1)}, f32[2,14,208,128]{3,2,1,0:T(8,128)S(1)}, f32[12,16,16,128]{3,2,1,0:T(8,128)S(1)}, bf16[2,2304,256]{2,1,0:T(8,128)(2,1)S(1)}, f32[2,128,256]{2,1,0:T(8,128)S(1)}) custom-call(f32[10,8,16]{2,1,0:T(8,128)S(1)} %pad_maximum_fusion.low_ref, ...), custom_call_target="tpu_custom_call", output_to_operand_aliasing={{0}: (3, {}), {1}: (4, {})} | custom-call | flops 100000000 | bytes 10000000 | tf_op jit(solution)/shard_map/middle/pallas_call | solution.py:593
  16.4 0.0 collective-permute-done.2.z_after_ref
  16.4 0.0 collective-permute-done.1.z_before_ref
  16.4 4.1 %basis.1 = (f32[2,128,128]{2,1,0:T(8,128)S(1)}, f32[2,128,128]{2,1,0:T(8,128)S(1)}, f32[2,128,128]{2,1,0:T(8,128)S(1)}, f32[2,14,208,128]{3,2,1,0:T(8,128)S(1)},...) custom-call(f32[2,8,16]{2,1,0:T(8,128)S(1)} %collective-permute-done, ...), custom_call_target="tpu_custom_call", output_to_operand_aliasing={{3}: (3, {}), {4}: (4, {}), {5}: (5, {}), {6}: (6, {})} | custom-call | tf_op jit(solution)/shard_map/basis/pallas_call | solution.py:607
  20.5 1.8 %collective-permute-start.6 = (f32[2,128,128]{2,1,0:T(8,128)S(1)}, f32[2,128,128]{2,1,0:T(8,128)S(1)}, u32[]{:S(2)}, u32[]{:S(2)}) collective-permute-start(f32[2,128,128]{2,1,0:T(8,128)S(1)} %get-tuple-element.36), channel_id=1, source_target_pairs={{0,28},{4,0},{8,4},{12,8},{16,12},{20,16},{24,20},{28,24},{1,29},{... | collective-permute-start | bytes 393224 | tf_op jit(solution)/shard_map/ppermute | solution.py:550
  22.3 0.1 collective-permute-start.7
  22.4 1.4 %near.1 = (f32[2,2,128,128]{3,2,1,0:T(8,128)S(1)}, f32[2,2,128,128]{3,2,1,0:T(8,128)S(1)}, f32[32,4,128]{2,1,0:T(4,128)S(1)}, f32[32,4,128]{2,1,0:T(4,128)S(1)}, f32[32,4,128]{2,1,0:T(4,128)S(1)}) custom-call(f32[2,128,128]{2,1,0:T(8,128)S(1)} %get-tuple-element.32.inverse_ref, f32[2,14,208,128]{3,2,1,0:T(8,128)S(1)} %get-tuple-element.33.field, ...), custom_call_target="tpu_custom_call" | custom-call | flops 100000000 | bytes 10000000 | tf_op jit(solution)/shard_map/near/pallas_call | solution.py:628
  23.9 0.4 %collective-permute-start.8 = (f32[32,4,128]{2,1,0:T(4,128)S(1)}, f32[32,4,128]{2,1,0:T(4,128)S(1)}, u32[]{:S(2)}, u32[]{:S(2)}) collective-permute-start(f32[32,4,128]{2,1,0:T(4,128)S(1)} %get-tuple-element.40), channel_id=1, source_target_pairs={{0,1},{1,0},{2,3},{3,2},{4,5},{5,4},{6,7},{7,6},{8,9},{9,8},{10,11... | collective-permute-start | bytes 196616 | tf_op jit(solution)/shard_map/ppermute | solution.py:557
  24.3 1.3 %collective-permute-start.9 = (f32[32,4,128]{2,1,0:T(4,128)S(1)}, f32[32,4,128]{2,1,0:T(4,128)S(1)}, u32[]{:S(2)}, u32[]{:S(2)}) collective-permute-start(f32[32,4,128]{2,1,0:T(4,128)S(1)} %get-tuple-element.41), channel_id=1, source_target_pairs={{0,2},{1,3},{2,0},{3,1},{4,6},{5,7},{6,4},{7,5},{8,10},{9,11},{10,... | collective-permute-start | bytes 196616 | tf_op jit(solution)/shard_map/ppermute | solution.py:557
  25.5 0.2 collective-permute-start.10
  25.8 0.0 collective-permute-done.6.next_x_ref
  25.8 0.0 collective-permute-done.7.next_z_ref
  25.8 0.4 %far.1 = (f32[32,8,128]{2,1,0:T(8,128)S(1)}, f32[32,4,128]{2,1,0:T(4,128)S(1)}, f32[32,4,128]{2,1,0:T(4,128)S(1)}, f32[32,4,128]{2,1,0:T(4,128)S(1)}) custom-call(f32[2,2,128,128]{3,2,1,0:T(8,128)S(1)} %get-tuple-element.35.plus_ref, f32[2,128,128]{2,1,0:T(8,128)S(1)} %collective-permute-done.6.next_x_ref, ...), custom_call_target="tpu_custom_call" | custom-call | tf_op jit(solution)/shard_map/far/pallas_call | solution.py:643
  26.2 1.0 %collective-permute-start.11 = (f32[32,4,128]{2,1,0:T(4,128)S(1)}, f32[32,4,128]{2,1,0:T(4,128)S(1)}, u32[]{:S(2)}, u32[]{:S(2)}) collective-permute-start(f32[32,4,128]{2,1,0:T(4,128)S(1)} %get-tuple-element.43), channel_id=1, source_target_pairs={{0,1},{1,0},{2,3},{3,2},{4,5},{5,4},{6,7},{7,6},{8,9},{9,8},{10,11... | collective-permute-start | bytes 196616 | tf_op jit(solution)/shard_map/ppermute | solution.py:557
  27.2 1.0 %collective-permute-start.12 = (f32[32,4,128]{2,1,0:T(4,128)S(1)}, f32[32,4,128]{2,1,0:T(4,128)S(1)}, u32[]{:S(2)}, u32[]{:S(2)}) collective-permute-start(f32[32,4,128]{2,1,0:T(4,128)S(1)} %get-tuple-element.44), channel_id=1, source_target_pairs={{0,2},{1,3},{2,0},{3,1},{4,6},{5,7},{6,4},{7,5},{8,10},{9,11},{10,... | collective-permute-start | bytes 196616 | tf_op jit(solution)/shard_map/ppermute | solution.py:557
  28.1 0.0 collective-permute-done.8.refs_1_
  28.1 0.5 %collective-permute-start.13 = (f32[32,4,128]{2,1,0:T(4,128)S(1)}, f32[32,4,128]{2,1,0:T(4,128)S(1)}, u32[]{:S(2)}, u32[]{:S(2)}) collective-permute-start(f32[32,4,128]{2,1,0:T(4,128)S(1)} %get-tuple-element.45), channel_id=1, source_target_pairs={{0,3},{1,2},{2,1},{3,0},{4,7},{5,6},{6,5},{7,4},{8,11},{9,10},{10,... | collective-permute-start | bytes 196616 | tf_op jit(solution)/shard_map/ppermute | solution.py:557
  28.6 0.0 collective-permute-done.9.refs_2_
  28.6 1.0 %collective-permute-done.10.refs_3_ = f32[32,4,128]{2,1,0:T(4,128)S(1)} collective-permute-done((f32[32,4,128]{2,1,0:T(4,128)S(1)}, f32[32,4,128]{2,1,0:T(4,128)S(1)}, u32[]{:S(2)}, u32[]{:S(2)}) %collective-permute-start.10) | collective-permute-done | bytes 65568 | tf_op jit(solution)/shard_map/ppermute | solution.py:557
  29.6 0.0 collective-permute-done.11.refs_4_
  29.6 2.2 %collective-permute-done.12.refs_5_ = f32[32,4,128]{2,1,0:T(4,128)S(1)} collective-permute-done((f32[32,4,128]{2,1,0:T(4,128)S(1)}, f32[32,4,128]{2,1,0:T(4,128)S(1)}, u32[]{:S(2)}, u32[]{:S(2)}) %collective-permute-start.12) | collective-permute-done | bytes 65568 | tf_op jit(solution)/shard_map/ppermute | solution.py:557
  31.8 0.6 %collective-permute-done.13.refs_6_ = f32[32,4,128]{2,1,0:T(4,128)S(1)} collective-permute-done((f32[32,4,128]{2,1,0:T(4,128)S(1)}, f32[32,4,128]{2,1,0:T(4,128)S(1)}, u32[]{:S(2)}, u32[]{:S(2)}) %collective-permute-start.13) | collective-permute-done | bytes 65568 | tf_op jit(solution)/shard_map/ppermute | solution.py:557
  32.5 1.0 %assemble.1 = (f32[32,4,2,128]{3,2,1,0:T(2,128)}, f32[32,4,3,2,128]{4,3,2,1,0:T(2,128)}) custom-call(f32[32,8,128]{2,1,0:T(8,128)S(1)} %get-tuple-element.39.refs_0_, f32[32,4,128]{2,1,0:T(4,128)S(1)} %collective-permute-done.8.refs_1_, f32[32,4,128]{2,1,0:T(4,128)S(1)} %collective-permute-done.9.refs_2_, f32[32,4,128]{2,1,0:T(4,128)S(1)} %collective-permute-done.10.refs_3_, ...), custom_call_target="tpu_custom_call" | custom-call | tf_op jit(solution)/shard_map/assemble/pallas_call | solution.py:655
  (5 shorter events, 0.0 us)
Async XLA Ops:
  0.6 9.1 %collective-permute-start.3 = (f32[8,8,16]{2,1,0:T(8,128)}, f32[8,8,16]{2,1,0:T(8,128)S(1)}, u32[]{:S(2)}, u32[]{:S(2)}) collective-permute-start(f32[8,8,16]{2,1,0:T(8,128)} %bitcast.8), channel_id=1, source_target_pairs={{0,4},{4,8},{8,12},{12,16},{16,20},{20,24},{24,28},{28,0},{1,5},{5... | collective-permute-start | bytes 12296 | tf_op jit(solution)/shard_map/ppermute | solution.py:550
  4.4 6.0 %collective-permute-start = (f32[2,8,16]{2,1,0:T(8,128)S(1)}, f32[2,8,16]{2,1,0:T(8,128)S(1)}, u32[]{:S(2)}, u32[]{:S(2)}) collective-permute-start(f32[2,8,16]{2,1,0:T(8,128)S(1)} %slice.24), channel_id=1, source_target_pairs={{0,28},{4,0},{8,4},{12,8},{16,12},{20,16},{24,20},{28,24},{1,29},{... | collective-permute-start | bytes 3080 | tf_op jit(solution)/shard_map/ppermute | solution.py:550
  7.5 1.2 %copy-start = (bf16[1,1,2,1728,128]{4,3,2,1,0:T(8,128)(2,1)S(1)}, bf16[1,1,2,1728,128]{4,3,2,1,0:T(8,128)(2,1)}, u32[]{:S(2)}) copy-start(bf16[1,1,2,1728,128]{4,3,2,1,0:T(8,128)(2,1)} %param.3) | copy-start | bytes 2654212
  9.8 2.5 %collective-permute-start.5 = (f32[10,2,16]{2,1,0:T(2,128)S(1)}, f32[10,2,16]{2,1,0:T(2,128)S(1)}, u32[]{:S(2)}, u32[]{:S(2)}) collective-permute-start(f32[10,2,16]{2,1,0:T(2,128)S(1)} %get-tuple-element.48), channel_id=1, source_target_pairs={{0,3},{1,0},{2,1},{3,2},{4,7},{5,4},{6,5},{7,6},{8,11},{9,8},{10,9... | collective-permute-start | bytes 3848 | tf_op jit(solution)/shard_map/ppermute | solution.py:550
  10.5 3.1 %collective-permute-start.4 = (f32[10,2,16]{2,1,0:T(2,128)S(1)}, f32[10,2,16]{2,1,0:T(2,128)S(1)}, u32[]{:S(2)}, u32[]{:S(2)}) collective-permute-start(f32[10,2,16]{2,1,0:T(2,128)S(1)} %get-tuple-element.49), channel_id=1, source_target_pairs={{0,1},{1,2},{2,3},{3,0},{4,5},{5,6},{6,7},{7,4},{8,9},{9,10},{10,1... | collective-permute-start | bytes 3848 | tf_op jit(solution)/shard_map/ppermute | solution.py:550
  10.5 5.9 %collective-permute-start.2 = (f32[2,2,16]{2,1,0:T(2,128)S(1)}, f32[2,2,16]{2,1,0:T(2,128)S(1)}, u32[]{:S(2)}, u32[]{:S(2)}) collective-permute-start(f32[2,2,16]{2,1,0:T(2,128)S(1)} %get-tuple-element.50), channel_id=1, source_target_pairs={{0,3},{1,0},{2,1},{3,2},{4,7},{5,4},{6,5},{7,6},{8,11},{9,8},{10,9... | collective-permute-start | bytes 776 | tf_op jit(solution)/shard_map/ppermute | solution.py:550
  12.2 4.2 %collective-permute-start.1 = (f32[2,2,16]{2,1,0:T(2,128)S(1)}, f32[2,2,16]{2,1,0:T(2,128)S(1)}, u32[]{:S(2)}, u32[]{:S(2)}) collective-permute-start(f32[2,2,16]{2,1,0:T(2,128)S(1)} %get-tuple-element.51), channel_id=1, source_target_pairs={{0,1},{1,2},{2,3},{3,0},{4,5},{5,6},{6,7},{7,4},{8,9},{9,10},{10,1... | collective-permute-start | bytes 776 | tf_op jit(solution)/shard_map/ppermute | solution.py:550
  20.5 5.3 %collective-permute-start.6 = (f32[2,128,128]{2,1,0:T(8,128)S(1)}, f32[2,128,128]{2,1,0:T(8,128)S(1)}, u32[]{:S(2)}, u32[]{:S(2)}) collective-permute-start(f32[2,128,128]{2,1,0:T(8,128)S(1)} %get-tuple-element.36), channel_id=1, source_target_pairs={{0,28},{4,0},{8,4},{12,8},{16,12},{20,16},{24,20},{28,24},{1,29},{... | collective-permute-start | bytes 393224 | tf_op jit(solution)/shard_map/ppermute | solution.py:550
  22.3 3.5 %collective-permute-start.7 = (f32[2,128,128]{2,1,0:T(8,128)S(1)}, f32[2,128,128]{2,1,0:T(8,128)S(1)}, u32[]{:S(2)}, u32[]{:S(2)}) collective-permute-start(f32[2,128,128]{2,1,0:T(8,128)S(1)} %get-tuple-element.37), channel_id=1, source_target_pairs={{0,3},{1,0},{2,1},{3,2},{4,7},{5,4},{6,5},{7,6},{8,11},{9,8},{10,9... | collective-permute-start | bytes 393224 | tf_op jit(solution)/shard_map/ppermute | solution.py:550
  23.9 4.3 %collective-permute-start.8 = (f32[32,4,128]{2,1,0:T(4,128)S(1)}, f32[32,4,128]{2,1,0:T(4,128)S(1)}, u32[]{:S(2)}, u32[]{:S(2)}) collective-permute-start(f32[32,4,128]{2,1,0:T(4,128)S(1)} %get-tuple-element.40), channel_id=1, source_target_pairs={{0,1},{1,0},{2,3},{3,2},{4,5},{5,4},{6,7},{7,6},{8,9},{9,8},{10,11... | collective-permute-start | bytes 196616 | tf_op jit(solution)/shard_map/ppermute | solution.py:557
  24.3 4.3 %collective-permute-start.9 = (f32[32,4,128]{2,1,0:T(4,128)S(1)}, f32[32,4,128]{2,1,0:T(4,128)S(1)}, u32[]{:S(2)}, u32[]{:S(2)}) collective-permute-start(f32[32,4,128]{2,1,0:T(4,128)S(1)} %get-tuple-element.41), channel_id=1, source_target_pairs={{0,2},{1,3},{2,0},{3,1},{4,6},{5,7},{6,4},{7,5},{8,10},{9,11},{10,... | collective-permute-start | bytes 196616 | tf_op jit(solution)/shard_map/ppermute | solution.py:557
  25.5 4.1 %collective-permute-start.10 = (f32[32,4,128]{2,1,0:T(4,128)S(1)}, f32[32,4,128]{2,1,0:T(4,128)S(1)}, u32[]{:S(2)}, u32[]{:S(2)}) collective-permute-start(f32[32,4,128]{2,1,0:T(4,128)S(1)} %get-tuple-element.42), channel_id=1, source_target_pairs={{0,3},{1,2},{2,1},{3,0},{4,7},{5,6},{6,5},{7,4},{8,11},{9,10},{10,... | collective-permute-start | bytes 196616 | tf_op jit(solution)/shard_map/ppermute | solution.py:557
  26.2 3.5 %collective-permute-start.11 = (f32[32,4,128]{2,1,0:T(4,128)S(1)}, f32[32,4,128]{2,1,0:T(4,128)S(1)}, u32[]{:S(2)}, u32[]{:S(2)}) collective-permute-start(f32[32,4,128]{2,1,0:T(4,128)S(1)} %get-tuple-element.43), channel_id=1, source_target_pairs={{0,1},{1,0},{2,3},{3,2},{4,5},{5,4},{6,7},{7,6},{8,9},{9,8},{10,11... | collective-permute-start | bytes 196616 | tf_op jit(solution)/shard_map/ppermute | solution.py:557
  27.2 4.6 %collective-permute-start.12 = (f32[32,4,128]{2,1,0:T(4,128)S(1)}, f32[32,4,128]{2,1,0:T(4,128)S(1)}, u32[]{:S(2)}, u32[]{:S(2)}) collective-permute-start(f32[32,4,128]{2,1,0:T(4,128)S(1)} %get-tuple-element.44), channel_id=1, source_target_pairs={{0,2},{1,3},{2,0},{3,1},{4,6},{5,7},{6,4},{7,5},{8,10},{9,11},{10,... | collective-permute-start | bytes 196616 | tf_op jit(solution)/shard_map/ppermute | solution.py:557
  28.1 4.3 %collective-permute-start.13 = (f32[32,4,128]{2,1,0:T(4,128)S(1)}, f32[32,4,128]{2,1,0:T(4,128)S(1)}, u32[]{:S(2)}, u32[]{:S(2)}) collective-permute-start(f32[32,4,128]{2,1,0:T(4,128)S(1)} %get-tuple-element.45), channel_id=1, source_target_pairs={{0,3},{1,2},{2,1},{3,0},{4,7},{5,6},{6,5},{7,4},{8,11},{9,10},{10,... | collective-permute-start | bytes 196616 | tf_op jit(solution)/shard_map/ppermute | solution.py:557

commit v6 on v5

--- a/solution.py
+++ b/solution.py
@@ -125,6 +125,9 @@
     for start in range(0, size, BLOCK):
         rows = slice(start, start + BLOCK)
         at = start % half
+        below = start + BLOCK
+        if below < size:
+            values = [matrix_ref[part, below : below + BLOCK, :] for part in parts]
         pivot_rows = list(panel)
         pivot = bcast_row(columns[0], 0)
         for k in range(BLOCK):
@@ -143,16 +146,15 @@
             for j in range(k + 1, BLOCK):
                 columns[j] = columns[j] - factor * bcast_row(columns[j], k)
             panel = [value - factor * bcast_row(value, k) for value in panel]
+            if k == 3 and below < size:
+                factors = [columns_of(values[0], at + j) for j in range(BLOCK)]
         solved = [value * reciprocals for value in panel]
         scale = lax.rsqrt(pivots)
         kept = [value * scale for value in pivot_rows]
         inverse_ref[0, rows, :] = kept[parts.index(2)]
         inverse_ref[1, rows, :] = kept[parts.index(3)] if 3 in parts else jnp.zeros_like(scale)
-        below = start + BLOCK
         if below == size:
             break
-        values = [matrix_ref[part, below : below + BLOCK, :] for part in parts]
-        factors = [columns_of(values[0], at + k) for k in range(BLOCK)]
         panel = []
         for value, taken in zip(values, solved):
             terms = [factors[k] * bcast_row(taken, k) for k in range(BLOCK)]
@@ -188,8 +190,6 @@
     elements, side = source.shape[0], source.shape[1] - 2
     columns = source.shape[-1]
     weight = beside_weight(side, columns)
-    if previous is None:
-        weight = 0.5 * weight
     for e in range(elements):
 
         def column(y):
@@ -208,11 +208,12 @@
                 beside = beside + before
             if after is not None:
                 beside = beside + after
+            scaled = scaled_ref[x, (e * G - margin + y) % scaled_ref.shape[1]]
+            value = scaled * here - weight * beside
             if previous is None:
-                value = -weight * beside
+                value = 0.5 * value
             else:
-                scaled = scaled_ref[x, (e * G - margin + y) % scaled_ref.shape[1]]
-                value = scaled * here - weight * beside - previous[e, x + 1, low : low + COL]
+                value = value - previous[e, x + 1, low : low + COL]
             target[e, x + 1, low : low + COL] = value
             if pair_ref is not None:
                 high, rest = split(value)
@@ -222,12 +223,12 @@
             before, here = here, after
 
 
-def first_kernel(start_ref, field_ref, first_ref, flat_ref):
+def first_kernel(start_ref, field_ref, next_ref, flat_ref):
     elements, columns = start_ref.shape[0], start_ref.shape[-1]
     side = field_ref.shape[1] - 2
     slab = side * side
     zero_ends(field_ref, elements, side)
-    zero_ends(first_ref, elements, side)
+    zero_ends(next_ref, elements, side)
     inside = lax.broadcasted_iota(jnp.int32, (COL, columns), 0) < side
 
     def prepare(x, carry):
@@ -238,13 +239,7 @@
                 field_ref[e, x + 1, LEAD + COL * y : LEAD + COL * (y + 1)] = value
         return carry
 
-    lax.fori_loop(0, side, prepare, 0)
-
-    def step(x, carry):
-        slab_step(x, field_ref, None, None, first_ref, None, 0)
-        return carry
-
-    lax.fori_loop(0, side, step, 0)
+    lax.fori_loop(0, side, prepare, 0, unroll=2)
 
 
 def point_rows(field, margin, e, x, y):
@@ -261,19 +256,10 @@
     return [field[e, margin + x + 1, pl.ds(low, G, stride=COL)] for x in range(G)]
 
 
-def potential_part(x, box_ref, margin, scaled_ref, first_in, start_in, first_ref):
-    elements, columns = start_in.shape[0], start_in.shape[-1]
-    side, y_points = scaled_ref.shape[:2]
+def spread_potential(x, box_ref, scaled_ref):
     rows = box_ref[x]
-    for y in range(y_points):
-        scaled = bcast_lane(rows, y, columns)
-        scaled_ref[x, y] = scaled
-        scaled = 0.5 * scaled
-        for e in range(elements):
-            box_y = (y - e * G + margin) % y_points
-            if box_y < side:
-                at = slice(LEAD + COL * box_y, LEAD + COL * (box_y + 1))
-                first_ref[e, x + 1, at] = first_in[e, x + 1, at] + scaled * start_in[e, x + 1, at]
+    for y in range(scaled_ref.shape[1]):
+        scaled_ref[x, y] = bcast_lane(rows, y, scaled_ref.shape[-1])
 
 
 def steps(ranges, first_ref, start_ref, scaled_ref, pair_ref, margin):
@@ -286,7 +272,7 @@
             slab_step(x, source, scaled_ref, target, target, pair, margin)
             return carry
 
-        lax.fori_loop(*ranges(index), next_step, 0, unroll=2)
+        lax.fori_loop(*ranges(index), next_step, 0, unroll=4)
         fields = fields[::-1]
     return fields[0]
 
@@ -304,112 +290,8 @@
     ]
 
 
-def middle_kernel(
-    margin,
-    low_ref,
-    z_before_ref,
-    z_after_ref,
-    start_in,
-    first_in,
-    start_ref,
-    first_ref,
-    scaled_ref,
-    pair_ref,
-    overlap_ref,
-    box_ref,
-):
-    side, y_points = scaled_ref.shape[:2]
-    end = side - margin
-    box_ref[...] = jnp.zeros_like(box_ref)
-    box_ref[:end, margin : margin + G, :y_points] = low_ref[...]
-    box_ref[:end, :margin, :y_points] = z_before_ref[...]
-    box_ref[:end, margin + G : side, :y_points] = z_after_ref[...]
-
-    def complete(x, carry):
-        potential_part(x, box_ref, margin, scaled_ref, first_in, start_in, first_ref)
-        return carry
-
-    lax.fori_loop(0, end, complete, 0, unroll=2)
-    steps(lambda i: (0, end - i), first_ref, start_ref, scaled_ref, pair_ref, margin)
-    for e, value in enumerate(overlaps(pair_ref, 0, (end - FILTER + 1) * side * COL)):
-        overlap_ref[e] = value
-
-
-def basis_kernel(
-    margin,
-    x_after_ref,
-    z_before_ref,
-    z_after_ref,
-    start_in,
-    first_in,
-    scaled_in,
-    pair_in,
-    overlap_ref,
-    minus_x_ref,
-    minus_z_ref,
-    inverse_ref,
-    start_ref,
-    first_ref,
-    scaled_ref,
-    pair_ref,
-    box_ref,
-    matrix_ref,
-    packed_ref,
-):
-    elements, columns = start_ref.shape[0], start_ref.shape[-1]
-    side, y_points = scaled_ref.shape[:2]
-    end = side - margin
-    box_ref[...] = jnp.zeros_like(box_ref)
-    box_ref[end:, margin : margin + G, :y_points] = x_after_ref[...]
-    box_ref[end:, :margin, :y_points] = z_before_ref[...]
-    box_ref[end:, margin + G : side, :y_points] = z_after_ref[...]
-    for x in range(end, side):
-        potential_part(x, box_ref, margin, scaled_ref, first_in, start_in, first_ref)
-    field = steps(
-        lambda i: (end - i, side), first_ref, start_ref, scaled_ref, pair_ref, margin
-    )
-    rest = overlaps(pair_ref, (end - FILTER + 1) * side * COL, side * side * COL)
-
-    identity = (
-        lax.broadcasted_iota(jnp.int32, (columns, columns), 0)
-        == lax.broadcasted_iota(jnp.int32, (columns, columns), 1)
-    ).astype(f32)
-    grams = []
-    for e in range(elements):
-        products = overlap_ref[e] + rest[e]
-        cross = products[:, columns:]
-        grams.append(products[:, :columns] + (cross + cross.T))
-    for e in range(0, elements, 2):
-        pairs = [grams[e], grams[min(e + 1, elements - 1)]]
-        for i, value in enumerate(pack(pairs) + pack([identity, identity])):
-            matrix_ref[i] = value
-        inverse_factors(matrix_ref, packed_ref)
-        solved = pack([packed_ref[0], packed_ref[1]])
-        for i in range(min(2, elements - e)):
-            inverse_ref[e + i] = solved[i]
-
-    for e in range(elements):
-        held = weights(split(inverse_ref[e]), True)
-        rows = []
-        for d in (0, 2):
-            rows += layer(field, margin, e, d, 0) + layer(field, margin, e, d, 1)
-        faces = product(jnp.concatenate(rows, 0), held, True)
-        minus_x_ref[e] = faces[: 2 * G * G]
-        minus_z_ref[e] = faces[2 * G * G :]
-
-
-def near_kernel(
-    count,
-    margin,
-    inverse_ref,
-    field,
-    scaled_ref,
-    plus_ref,
-    near_ref,
-    *rest,
-):
-    *out_refs, inner_ref, applied_ref = rest
-    elements, columns = inverse_ref.shape[0], inverse_ref.shape[-1]
+def own_operator(field, scaled_ref, inner_ref, applied_ref, raw_ref, margin):
+    elements, columns = field.shape[0], field.shape[-1]
     y_points = scaled_ref.shape[1]
 
     z = lax.broadcasted_iota(jnp.int32, (G, columns), 0)
@@ -447,6 +329,138 @@
                     ref[e, at, :columns] = high
                     ref[e, at, columns:] = low
 
+    for e in range(elements):
+        both = lax.dot_general(
+            inner_ref[e, :, :columns],
+            applied_ref[e],
+            (((0,), (0,)), ((), ())),
+            preferred_element_type=f32,
+        )
+        raw = both[:, :columns] + both[:, columns:]
+        raw = raw + lax.dot_general(
+            inner_ref[e, :, columns:],
+            applied_ref[e, :, :columns],
+            (((0,), (0,)), ((), ())),
+            preferred_element_type=f32,
+        )
+        raw_ref[e] = raw
+
+
+def middle_kernel(
+    margin,
+    low_ref,
+    z_before_ref,
+    z_after_ref,
+    start_in,
+    first_in,
+    start_ref,
+    first_ref,
+    scaled_ref,
+    pair_ref,
+    overlap_ref,
+    box_ref,
+):
+    side, y_points = scaled_ref.shape[:2]
+    end = side - margin
+    box_ref[...] = jnp.zeros_like(box_ref)
+    box_ref[:end, margin : margin + G, :y_points] = low_ref[...]
+    box_ref[:end, :margin, :y_points] = z_before_ref[...]
+    box_ref[:end, margin + G : side, :y_points] = z_after_ref[...]
+
+    spread_potential(0, box_ref, scaled_ref)
+
+    def first_step(x, carry):
+        spread_potential(x + 1, box_ref, scaled_ref)
+        slab_step(x, start_ref, scaled_ref, None, first_ref, None, margin)
+        return carry
+
+    lax.fori_loop(0, end, first_step, 0, unroll=5)
+    steps(lambda i: (0, end - i), first_ref, start_ref, scaled_ref, pair_ref, margin)
+    for e, value in enumerate(overlaps(pair_ref, 0, (end - FILTER + 1) * side * COL)):
+        overlap_ref[e] = value
+
+
+def basis_kernel(
+    margin,
+    x_after_ref,
+    z_before_ref,
+    z_after_ref,
+    start_in,
+    first_in,
+    scaled_in,
+    pair_in,
+    overlap_ref,
+    minus_x_ref,
+    minus_z_ref,
+    inverse_ref,
+    raw_ref,
+    start_ref,
+    first_ref,
+    scaled_ref,
+    pair_ref,
+    box_ref,
+    matrix_ref,
+    packed_ref,
+    inner_ref,
+    applied_ref,
+):
+    elements, columns = start_ref.shape[0], start_ref.shape[-1]
+    side, y_points = scaled_ref.shape[:2]
+    end = side - margin
+    box_ref[...] = jnp.zeros_like(box_ref)
+    box_ref[end:, margin : margin + G, :y_points] = x_after_ref[...]
+    box_ref[end:, :margin, :y_points] = z_before_ref[...]
+    box_ref[end:, margin + G : side, :y_points] = z_after_ref[...]
+    for x in range(end, side):
+        spread_potential(x, box_ref, scaled_ref)
+    for x in range(end, side):
+        slab_step(x, start_ref, scaled_ref, None, first_ref, None, margin)
+    field = steps(
+        lambda i: (end - i, side), first_ref, start_ref, scaled_ref, pair_ref, margin
+    )
+    rest = overlaps(pair_ref, (end - FILTER + 1) * side * COL, side * side * COL)
+
+    own_operator(field, scaled_ref, inner_ref, applied_ref, raw_ref, margin)
+
+    identity = (
+        lax.broadcasted_iota(jnp.int32, (columns, columns), 0)
+        == lax.broadcasted_iota(jnp.int32, (columns, columns), 1)
+    ).astype(f32)
+    grams = []
+    for e in range(elements):
+        products = overlap_ref[e] + rest[e]
+        cross = products[:, columns:]
+        grams.append(products[:, :columns] + (cross + cross.T))
+    for e in range(0, elements, 2):
+        pairs = [grams[e], grams[min(e + 1, elements - 1)]]
+        for i, value in enumerate(pack(pairs) + pack([identity, identity])):
+            matrix_ref[i] = value
+        inverse_factors(matrix_ref, packed_ref)
+        solved = pack([packed_ref[0], packed_ref[1]])
+        for i in range(min(2, elements - e)):
+            inverse_ref[e + i] = solved[i]
+
+    for e in range(elements):
+        held = weights(split(inverse_ref[e]), True)
+        rows = []
+        for d in (0, 2):
+            rows += layer(field, margin, e, d, 0) + layer(field, margin, e, d, 1)
+        faces = product(jnp.concatenate(rows, 0), held, True)
+        minus_x_ref[e] = faces[: 2 * G * G]
+        minus_z_ref[e] = faces[2 * G * G :]
+
+
+def near_kernel(
+    count,
+    margin,
+    inverse_ref,
+    raw_ref,
+    field,
+    plus_ref,
+    near_ref,
+    *out_refs,
+):
+    elements, columns = inverse_ref.shape[0], inverse_ref.shape[-1]
     face = 2 * G * G
     minus, plus, held = [], [], []
     for e in range(elements):
@@ -465,20 +479,7 @@
         plus_ref[e, 1] = faces[3 * face :].T
 
     for e in range(elements):
-        both = lax.dot_general(
-            inner_ref[e, :, :columns],
-            applied_ref[e],
-            (((0,), (0,)), ((), ())),
-            preferred_element_type=f32,
-        )
-        raw = both[:, :columns] + both[:, columns:]
-        raw = raw + lax.dot_general(
-            inner_ref[e, :, columns:],
-            applied_ref[e, :, :columns],
-            (((0,), (0,)), ((), ())),
-            preferred_element_type=f32,
-        )
-        half = product(inverse_ref[e], weights(split(raw), False), False)
+        half = product(inverse_ref[e], weights(split(raw_ref[e]), False), False)
         near_ref[0, e] = product(half, held[e], True)
         following = weights(split(minus[(e + 1) % elements]), False)
         near_ref[1, e] = product(plus[e], following, False)
@@ -604,16 +605,18 @@
 
     face = shape((elements, 2 * G * G, columns), f32)
     square = shape((elements, columns, columns), f32)
-    minus_x, minus_z, inverse, _, filtered, whole_scaled, _ = pl.pallas_call(
+    minus_x, minus_z, inverse, raw, _, filtered, _, _ = pl.pallas_call(
         functools.partial(basis_kernel, margin),
-        out_shape=[face, face, square, field, field, scaled, pair],
+        out_shape=[face, face, square, square, field, field, scaled, pair],
         in_specs=vmem(8),
-        out_specs=vmem(7),
-        input_output_aliases={3: 3, 4: 4, 5: 5, 6: 6},
+        out_specs=vmem(8),
+        input_output_aliases={3: 4, 4: 5, 5: 6, 6: 7},
         scratch_shapes=[
             box,
             pltpu.VMEM((4, columns, columns), f32),
             pltpu.VMEM((2, columns, columns), f32),
+            pltpu.VMEM((elements, G**3, 2 * columns), bf16),
+            pltpu.VMEM((elements, G**3, 2 * columns), bf16),
         ],
         compiler_params=pltpu.CompilerParams(vmem_limit_bytes=32 * 2**20),
         name="basis",
@@ -630,14 +633,10 @@
         out_shape=[shape((elements, 2, columns, 2 * G * G), f32), squares] + [block] * len(ahead),
         in_specs=vmem(3),
         out_specs=vmem(2 + len(ahead)),
-        scratch_shapes=[
-            pltpu.VMEM((elements, G**3, 2 * columns), bf16),
-            pltpu.VMEM((elements, G**3, 2 * columns), bf16),
-        ],
         compiler_params=pltpu.CompilerParams(vmem_limit_bytes=24 * 2**20),
         cost_estimate=pl.CostEstimate(flops=10**8, bytes_accessed=10**7, transcendentals=0),
         name="near",
-    )(inverse, filtered, whole_scaled)
+    )(inverse, raw, filtered)
     near = [exchange(value, step) for value, step in zip(near, ahead)]
 
     far = pl.pallas_call(

time: 33.7 us -> 33.7 us (level)
  starting transfers between devices: 14.8 us -> 16.2 us
  Pallas kernels: 10.7 us -> 9.31 us
    ppermute x6, starting transfers between devices: 4.35 us -> 5.24 us  [exchange(): lax.ppermute(block, 'ez', [(i, partner(i, step, count)) for i in range(co...]
    pallas_call x1, Pallas kernels: 1.43 us -> 0.77 us  [local(): pl.pallas_call(functools.partial(near_kernel, count, margin), out_shape=[...]
    pallas_call x1, Pallas kernels: 1.04 us -> 0.46 us  [local(): pl.pallas_call(first_kernel, out_shape=[field, field], in_specs=vmem(1),...]
    ppermute x6, waiting for transfers between devices: 3.85 us -> 3.35 us  [exchange(): lax.ppermute(block, 'ez', [(i, partner(i, step, count)) for i in range(co...]
    ppermute x8, starting transfers between devices: 10.4 us -> 10.9 us  [shift(): lax.ppermute(block, axis, [(i, (i + distance) % count) for i in range(cou...]
    ppermute x8, waiting for transfers between devices: 1.36 us -> 1.84 us  [shift(): lax.ppermute(block, axis, [(i, (i + distance) % count) for i in range(cou...]
  transfers between devices with their start and end apart: 14 -> 14, of which waited for: 4 -> 4; matrix products, arithmetic and copies ran while one was open for 2% -> 2% of each run, Pallas kernels for 17% -> 13%
where the time goes in v6:
time: 33.7 us; the launch traced here: 33.4 us
  starting transfers between devices  16.2 us (48%)
  Pallas kernels  9.31 us (28%)
  waiting for transfers between devices  5.19 us (15%)
  local copies, waits for them, and re-layouts  1.18 us (4%)
  other arithmetic  0.81 us (2%)
  between operations  0.73 us (2%)
    ppermute x8, starting transfers between devices, shift(): lax.ppermute(block, axis, [(i, (i + distance) % count) for i in range(cou...  10.9 us
    ppermute x6, starting transfers between devices, exchange(): lax.ppermute(block, 'ez', [(i, partner(i, step, count)) for i in range(co...  5.24 us
    pallas_call x1, Pallas kernels, local(): pl.pallas_call(functools.partial(basis_kernel, margin), out_shape=[face,...  4.16 us
    ppermute x6, waiting for transfers between devices, exchange(): lax.ppermute(block, 'ez', [(i, partner(i, step, count)) for i in range(co...  3.35 us
    pallas_call x1, Pallas kernels, local(): pl.pallas_call(functools.partial(middle_kernel, margin), out_shape=[field...  2.57 us
    ppermute x8, waiting for transfers between devices, shift(): lax.ppermute(block, axis, [(i, (i + distance) % count) for i in range(cou...  1.84 us
    unnamed x2, local copies, waits for them, and re-layouts  1.17 us
    pallas_call x1, Pallas kernels, local(): pl.pallas_call(functools.partial(assemble_kernel, count), out_shape=[shap...  0.97 us
  transfers between devices with their start and end apart: 14, of which 4 were waited for; matrix products, arithmetic and copies ran while one was open for 2% of the time, Pallas kernels for 13%

profile of v6, /device:TPU:0, one launch (start us, length us, event | category | flops | bytes accessed | tf_op | source)
XLA Modules:
  0.0 33.4 jit_solution(4777304814783888021)
XLA Ops:
  0.6 3.0 %collective-permute-start.3 = (f32[8,8,16]{2,1,0:T(8,128)}, f32[8,8,16]{2,1,0:T(8,128)S(1)}, u32[]{:S(2)}, u32[]{:S(2)}) collective-permute-start(f32[8,8,16]{2,1,0:T(8,128)} %bitcast.8), channel_id=1, source_target_pairs={{0,4},{4,8},{8,12},{12,16},{16,20},{20,24},{24,28},{28,0},{1,5},{5... | collective-permute-start | bytes 12296 | tf_op jit(solution)/shard_map/ppermute | solution.py:551
  3.6 0.8 %add_multiply_fusion = f32[8,8,16]{2,1,0:T(8,128)S(1)} fusion(f32[8,16,8]{1,2,0:T(8,128)} %param.2), kind=kLoop, calls=%fused_computation.1 | loop fusion | flops 2048 | bytes 8192 | tf_op jit(solution)/shard_map/mul | solution.py:569
  4.4 3.0 %collective-permute-start = (f32[2,8,16]{2,1,0:T(8,128)S(1)}, f32[2,8,16]{2,1,0:T(8,128)S(1)}, u32[]{:S(2)}, u32[]{:S(2)}) collective-permute-start(f32[2,8,16]{2,1,0:T(8,128)S(1)} %slice.24), channel_id=1, source_target_pairs={{0,28},{4,0},{8,4},{12,8},{16,12},{20,16},{24,20},{28,24},{1,29},{... | collective-permute-start | bytes 3080 | tf_op jit(solution)/shard_map/ppermute | solution.py:551
  7.5 0.0 copy-start
  7.5 1.2 %copy-done = bf16[1,1,2,1728,128]{4,3,2,1,0:T(8,128)(2,1)S(1)} copy-done((bf16[1,1,2,1728,128]{4,3,2,1,0:T(8,128)(2,1)S(1)}, bf16[1,1,2,1728,128]{4,3,2,1,0:T(8,128)(2,1)}, u32[]{:S(2)}) %copy-start) | copy-done | bytes 884760
  8.7 0.5 %first.1 = (f32[2,14,208,128]{3,2,1,0:T(8,128)S(1)}, f32[2,14,208,128]{3,2,1,0:T(8,128)S(1)}) custom-call(bf16[2,1728,128]{2,1,0:T(8,128)(2,1)S(1)} %bitcast.7), custom_call_target="tpu_custom_call" | custom-call | flops 100000 | bytes 10000 | tf_op jit(solution)/shard_map/first/pallas_call | solution.py:576
  9.1 0.0 collective-permute-done.3
  9.2 0.7 %collective-permute-start.5 = (f32[10,2,16]{2,1,0:T(2,128)S(1)}, f32[10,2,16]{2,1,0:T(2,128)S(1)}, u32[]{:S(2)}, u32[]{:S(2)}) collective-permute-start(f32[10,2,16]{2,1,0:T(2,128)S(1)} %get-tuple-element.48), channel_id=1, source_target_pairs={{0,3},{1,0},{2,1},{3,2},{4,7},{5,4},{6,5},{7,6},{8,11},{9,8},{10,9... | collective-permute-start | bytes 3848 | tf_op jit(solution)/shard_map/ppermute | solution.py:551
  9.9 0.0 collective-permute-start.4
  9.9 0.0 collective-permute-done.x_after_ref
  9.9 1.7 %collective-permute-start.2 = (f32[2,2,16]{2,1,0:T(2,128)S(1)}, f32[2,2,16]{2,1,0:T(2,128)S(1)}, u32[]{:S(2)}, u32[]{:S(2)}) collective-permute-start(f32[2,2,16]{2,1,0:T(2,128)S(1)} %get-tuple-element.50), channel_id=1, source_target_pairs={{0,3},{1,0},{2,1},{3,2},{4,7},{5,4},{6,5},{7,6},{8,11},{9,8},{10,9... | collective-permute-start | bytes 776 | tf_op jit(solution)/shard_map/ppermute | solution.py:551
  11.6 0.0 collective-permute-start.1
  11.6 0.0 collective-permute-done.5.z_after_ref
  11.6 1.3 %collective-permute-done.4.z_before_ref = f32[10,2,16]{2,1,0:T(2,128)S(1)} collective-permute-done((f32[10,2,16]{2,1,0:T(2,128)S(1)}, f32[10,2,16]{2,1,0:T(2,128)S(1)}, u32[]{:S(2)}, u32[]{:S(2)}) %collective-permute-start.4) | collective-permute-done | bytes 1312 | tf_op jit(solution)/shard_map/ppermute | solution.py:551
  13.0 2.6 %middle.1 = (f32[2,14,208,128]{3,2,1,0:T(8,128)S(1)}, f32[2,14,208,128]{3,2,1,0:T(8,128)S(1)}, f32[12,16,16,128]{3,2,1,0:T(8,128)S(1)}, bf16[2,2304,256]{2,1,0:T(8,128)(2,1)S(1)}, f32[2,128,256]{2,1,0:T(8,128)S(1)}) custom-call(f32[10,8,16]{2,1,0:T(8,128)S(1)} %pad_maximum_fusion.low_ref, ...), custom_call_target="tpu_custom_call", output_to_operand_aliasing={{0}: (3, {}), {1}: (4, {})} | custom-call | flops 100000000 | bytes 10000000 | tf_op jit(solution)/shard_map/middle/pallas_call | solution.py:594
  15.6 0.0 collective-permute-done.2.z_after_ref
  15.6 0.0 collective-permute-done.1.z_before_ref
  15.6 4.2 %basis.1 = (f32[2,128,128]{2,1,0:T(8,128)S(1)}, f32[2,128,128]{2,1,0:T(8,128)S(1)}, f32[2,128,128]{2,1,0:T(8,128)S(1)}, f32[2,128,128]{2,1,0:T(8,128)S(1)}, f32[...) custom-call(f32[2,8,16]{2,1,0:T(8,128)S(1)} %collective-permute-done, ...), custom_call_target="tpu_custom_call", output_to_operand_aliasing={{4}: (3, {}), {5}: (4, {}), {6}: (5, {}), {7}: (6, {})} | custom-call | tf_op jit(solution)/shard_map/basis/pallas_call | solution.py:608
  19.7 1.8 %collective-permute-start.6 = (f32[2,128,128]{2,1,0:T(8,128)S(1)}, f32[2,128,128]{2,1,0:T(8,128)S(1)}, u32[]{:S(2)}, u32[]{:S(2)}) collective-permute-start(f32[2,128,128]{2,1,0:T(8,128)S(1)} %get-tuple-element.36), channel_id=1, source_target_pairs={{0,28},{4,0},{8,4},{12,8},{16,12},{20,16},{24,20},{28,24},{1,29},{... | collective-permute-start | bytes 393224 | tf_op jit(solution)/shard_map/ppermute | solution.py:551
  21.5 0.6 %collective-permute-start.7 = (f32[2,128,128]{2,1,0:T(8,128)S(1)}, f32[2,128,128]{2,1,0:T(8,128)S(1)}, u32[]{:S(2)}, u32[]{:S(2)}) collective-permute-start(f32[2,128,128]{2,1,0:T(8,128)S(1)} %get-tuple-element.37), channel_id=1, source_target_pairs={{0,3},{1,0},{2,1},{3,2},{4,7},{5,4},{6,5},{7,6},{8,11},{9,8},{10,9... | collective-permute-start | bytes 393224 | tf_op jit(solution)/shard_map/ppermute | solution.py:551
  22.2 0.8 %near.1 = (f32[2,2,128,128]{3,2,1,0:T(8,128)S(1)}, f32[2,2,128,128]{3,2,1,0:T(8,128)S(1)}, f32[32,4,128]{2,1,0:T(4,128)S(1)}, f32[32,4,128]{2,1,0:T(4,128)S(1)}, f32[32,4,128]{2,1,0:T(4,128)S(1)}) custom-call(f32[2,128,128]{2,1,0:T(8,128)S(1)} %get-tuple-element.32.inverse_ref, f32[2,128,128]{2,1,0:T(8,128)S(1)} %get-tuple-element.33.raw_ref, ...), custom_call_target="tpu_custom_call" | custom-call | flops 100000000 | bytes 10000000 | tf_op jit(solution)/shard_map/near/pallas_call | solution.py:631
  22.9 0.1 collective-permute-start.8
  23.0 1.7 %collective-permute-start.9 = (f32[32,4,128]{2,1,0:T(4,128)S(1)}, f32[32,4,128]{2,1,0:T(4,128)S(1)}, u32[]{:S(2)}, u32[]{:S(2)}) collective-permute-start(f32[32,4,128]{2,1,0:T(4,128)S(1)} %get-tuple-element.41), channel_id=1, source_target_pairs={{0,2},{1,3},{2,0},{3,1},{4,6},{5,7},{6,4},{7,5},{8,10},{9,11},{10,... | collective-permute-start | bytes 196616 | tf_op jit(solution)/shard_map/ppermute | solution.py:558
  24.7 0.2 collective-permute-start.10
  24.9 0.5 %collective-permute-done.6.next_x_ref = f32[2,128,128]{2,1,0:T(8,128)S(1)} collective-permute-done((f32[2,128,128]{2,1,0:T(8,128)S(1)}, f32[2,128,128]{2,1,0:T(8,128)S(1)}, u32[]{:S(2)}, u32[]{:S(2)}) %collective-permute-start.6) | collective-permute-done | bytes 131104 | tf_op jit(solution)/shard_map/ppermute | solution.py:551
  25.4 0.0 collective-permute-done.7.next_z_ref
  25.4 0.4 %far.1 = (f32[32,8,128]{2,1,0:T(8,128)S(1)}, f32[32,4,128]{2,1,0:T(4,128)S(1)}, f32[32,4,128]{2,1,0:T(4,128)S(1)}, f32[32,4,128]{2,1,0:T(4,128)S(1)}) custom-call(f32[2,2,128,128]{3,2,1,0:T(8,128)S(1)} %get-tuple-element.35.plus_ref, f32[2,128,128]{2,1,0:T(8,128)S(1)} %collective-permute-done.6.next_x_ref, ...), custom_call_target="tpu_custom_call" | custom-call | tf_op jit(solution)/shard_map/far/pallas_call | solution.py:642
  25.8 1.9 %collective-permute-start.11 = (f32[32,4,128]{2,1,0:T(4,128)S(1)}, f32[32,4,128]{2,1,0:T(4,128)S(1)}, u32[]{:S(2)}, u32[]{:S(2)}) collective-permute-start(f32[32,4,128]{2,1,0:T(4,128)S(1)} %get-tuple-element.43), channel_id=1, source_target_pairs={{0,1},{1,0},{2,3},{3,2},{4,5},{5,4},{6,7},{7,6},{8,9},{9,8},{10,11... | collective-permute-start | bytes 196616 | tf_op jit(solution)/shard_map/ppermute | solution.py:558
  27.6 0.0 collective-permute-start.12
  27.6 0.0 collective-permute-done.8.refs_1_
  27.6 1.4 %collective-permute-start.13 = (f32[32,4,128]{2,1,0:T(4,128)S(1)}, f32[32,4,128]{2,1,0:T(4,128)S(1)}, u32[]{:S(2)}, u32[]{:S(2)}) collective-permute-start(f32[32,4,128]{2,1,0:T(4,128)S(1)} %get-tuple-element.45), channel_id=1, source_target_pairs={{0,3},{1,2},{2,1},{3,0},{4,7},{5,6},{6,5},{7,4},{8,11},{9,10},{10,... | collective-permute-start | bytes 196616 | tf_op jit(solution)/shard_map/ppermute | solution.py:558
  29.1 0.0 collective-permute-done.9.refs_2_
  29.1 0.1 collective-permute-done.10.refs_3_
  29.2 0.0 collective-permute-done.11.refs_4_
  29.2 3.2 %collective-permute-done.12.refs_5_ = f32[32,4,128]{2,1,0:T(4,128)S(1)} collective-permute-done((f32[32,4,128]{2,1,0:T(4,128)S(1)}, f32[32,4,128]{2,1,0:T(4,128)S(1)}, u32[]{:S(2)}, u32[]{:S(2)}) %collective-permute-start.12) | collective-permute-done | bytes 65568 | tf_op jit(solution)/shard_map/ppermute | solution.py:558
  32.4 0.0 collective-permute-done.13.refs_6_
  32.4 1.0 %assemble.1 = (f32[32,4,2,128]{3,2,1,0:T(2,128)}, f32[32,4,3,2,128]{4,3,2,1,0:T(2,128)}) custom-call(f32[32,8,128]{2,1,0:T(8,128)S(1)} %get-tuple-element.39.refs_0_, f32[32,4,128]{2,1,0:T(4,128)S(1)} %collective-permute-done.8.refs_1_, f32[32,4,128]{2,1,0:T(4,128)S(1)} %collective-permute-done.9.refs_2_, f32[32,4,128]{2,1,0:T(4,128)S(1)} %collective-permute-done.10.refs_3_, ...), custom_call_target="tpu_custom_call" | custom-call | tf_op jit(solution)/shard_map/assemble/pallas_call | solution.py:654
  (5 shorter events, 0.0 us)
Async XLA Ops:
  0.6 8.5 %collective-permute-start.3 = (f32[8,8,16]{2,1,0:T(8,128)}, f32[8,8,16]{2,1,0:T(8,128)S(1)}, u32[]{:S(2)}, u32[]{:S(2)}) collective-permute-start(f32[8,8,16]{2,1,0:T(8,128)} %bitcast.8), channel_id=1, source_target_pairs={{0,4},{4,8},{8,12},{12,16},{16,20},{20,24},{24,28},{28,0},{1,5},{5... | collective-permute-start | bytes 12296 | tf_op jit(solution)/shard_map/ppermute | solution.py:551
  4.4 5.4 %collective-permute-start = (f32[2,8,16]{2,1,0:T(8,128)S(1)}, f32[2,8,16]{2,1,0:T(8,128)S(1)}, u32[]{:S(2)}, u32[]{:S(2)}) collective-permute-start(f32[2,8,16]{2,1,0:T(8,128)S(1)} %slice.24), channel_id=1, source_target_pairs={{0,28},{4,0},{8,4},{12,8},{16,12},{20,16},{24,20},{28,24},{1,29},{... | collective-permute-start | bytes 3080 | tf_op jit(solution)/shard_map/ppermute | solution.py:551
  7.5 1.2 %copy-start = (bf16[1,1,2,1728,128]{4,3,2,1,0:T(8,128)(2,1)S(1)}, bf16[1,1,2,1728,128]{4,3,2,1,0:T(8,128)(2,1)}, u32[]{:S(2)}) copy-start(bf16[1,1,2,1728,128]{4,3,2,1,0:T(8,128)(2,1)} %param.3) | copy-start | bytes 2654212
  9.2 2.5 %collective-permute-start.5 = (f32[10,2,16]{2,1,0:T(2,128)S(1)}, f32[10,2,16]{2,1,0:T(2,128)S(1)}, u32[]{:S(2)}, u32[]{:S(2)}) collective-permute-start(f32[10,2,16]{2,1,0:T(2,128)S(1)} %get-tuple-element.48), channel_id=1, source_target_pairs={{0,3},{1,0},{2,1},{3,2},{4,7},{5,4},{6,5},{7,6},{8,11},{9,8},{10,9... | collective-permute-start | bytes 3848 | tf_op jit(solution)/shard_map/ppermute | solution.py:551
  9.9 3.1 %collective-permute-start.4 = (f32[10,2,16]{2,1,0:T(2,128)S(1)}, f32[10,2,16]{2,1,0:T(2,128)S(1)}, u32[]{:S(2)}, u32[]{:S(2)}) collective-permute-start(f32[10,2,16]{2,1,0:T(2,128)S(1)} %get-tuple-element.49), channel_id=1, source_target_pairs={{0,1},{1,2},{2,3},{3,0},{4,5},{5,6},{6,7},{7,4},{8,9},{9,10},{10,1... | collective-permute-start | bytes 3848 | tf_op jit(solution)/shard_map/ppermute | solution.py:551
  9.9 5.7 %collective-permute-start.2 = (f32[2,2,16]{2,1,0:T(2,128)S(1)}, f32[2,2,16]{2,1,0:T(2,128)S(1)}, u32[]{:S(2)}, u32[]{:S(2)}) collective-permute-start(f32[2,2,16]{2,1,0:T(2,128)S(1)} %get-tuple-element.50), channel_id=1, source_target_pairs={{0,3},{1,0},{2,1},{3,2},{4,7},{5,4},{6,5},{7,6},{8,11},{9,8},{10,9... | collective-permute-start | bytes 776 | tf_op jit(solution)/shard_map/ppermute | solution.py:551
  11.6 3.9 %collective-permute-start.1 = (f32[2,2,16]{2,1,0:T(2,128)S(1)}, f32[2,2,16]{2,1,0:T(2,128)S(1)}, u32[]{:S(2)}, u32[]{:S(2)}) collective-permute-start(f32[2,2,16]{2,1,0:T(2,128)S(1)} %get-tuple-element.51), channel_id=1, source_target_pairs={{0,1},{1,2},{2,3},{3,0},{4,5},{5,6},{6,7},{7,4},{8,9},{9,10},{10,1... | collective-permute-start | bytes 776 | tf_op jit(solution)/shard_map/ppermute | solution.py:551
  19.7 5.6 %collective-permute-start.6 = (f32[2,128,128]{2,1,0:T(8,128)S(1)}, f32[2,128,128]{2,1,0:T(8,128)S(1)}, u32[]{:S(2)}, u32[]{:S(2)}) collective-permute-start(f32[2,128,128]{2,1,0:T(8,128)S(1)} %get-tuple-element.36), channel_id=1, source_target_pairs={{0,28},{4,0},{8,4},{12,8},{16,12},{20,16},{24,20},{28,24},{1,29},{... | collective-permute-start | bytes 393224 | tf_op jit(solution)/shard_map/ppermute | solution.py:551
  21.5 3.8 %collective-permute-start.7 = (f32[2,128,128]{2,1,0:T(8,128)S(1)}, f32[2,128,128]{2,1,0:T(8,128)S(1)}, u32[]{:S(2)}, u32[]{:S(2)}) collective-permute-start(f32[2,128,128]{2,1,0:T(8,128)S(1)} %get-tuple-element.37), channel_id=1, source_target_pairs={{0,3},{1,0},{2,1},{3,2},{4,7},{5,4},{6,5},{7,6},{8,11},{9,8},{10,9... | collective-permute-start | bytes 393224 | tf_op jit(solution)/shard_map/ppermute | solution.py:551
  22.9 4.7 %collective-permute-start.8 = (f32[32,4,128]{2,1,0:T(4,128)S(1)}, f32[32,4,128]{2,1,0:T(4,128)S(1)}, u32[]{:S(2)}, u32[]{:S(2)}) collective-permute-start(f32[32,4,128]{2,1,0:T(4,128)S(1)} %get-tuple-element.40), channel_id=1, source_target_pairs={{0,1},{1,0},{2,3},{3,2},{4,5},{5,4},{6,7},{7,6},{8,9},{9,8},{10,11... | collective-permute-start | bytes 196616 | tf_op jit(solution)/shard_map/ppermute | solution.py:558
  23.0 6.1 %collective-permute-start.9 = (f32[32,4,128]{2,1,0:T(4,128)S(1)}, f32[32,4,128]{2,1,0:T(4,128)S(1)}, u32[]{:S(2)}, u32[]{:S(2)}) collective-permute-start(f32[32,4,128]{2,1,0:T(4,128)S(1)} %get-tuple-element.41), channel_id=1, source_target_pairs={{0,2},{1,3},{2,0},{3,1},{4,6},{5,7},{6,4},{7,5},{8,10},{9,11},{10,... | collective-permute-start | bytes 196616 | tf_op jit(solution)/shard_map/ppermute | solution.py:558
  24.7 4.5 %collective-permute-start.10 = (f32[32,4,128]{2,1,0:T(4,128)S(1)}, f32[32,4,128]{2,1,0:T(4,128)S(1)}, u32[]{:S(2)}, u32[]{:S(2)}) collective-permute-start(f32[32,4,128]{2,1,0:T(4,128)S(1)} %get-tuple-element.42), channel_id=1, source_target_pairs={{0,3},{1,2},{2,1},{3,0},{4,7},{5,6},{6,5},{7,4},{8,11},{9,10},{10,... | collective-permute-start | bytes 196616 | tf_op jit(solution)/shard_map/ppermute | solution.py:558
  25.8 3.4 %collective-permute-start.11 = (f32[32,4,128]{2,1,0:T(4,128)S(1)}, f32[32,4,128]{2,1,0:T(4,128)S(1)}, u32[]{:S(2)}, u32[]{:S(2)}) collective-permute-start(f32[32,4,128]{2,1,0:T(4,128)S(1)} %get-tuple-element.43), channel_id=1, source_target_pairs={{0,1},{1,0},{2,3},{3,2},{4,5},{5,4},{6,7},{7,6},{8,9},{9,8},{10,11... | collective-permute-start | bytes 196616 | tf_op jit(solution)/shard_map/ppermute | solution.py:558
  27.6 4.8 %collective-permute-start.12 = (f32[32,4,128]{2,1,0:T(4,128)S(1)}, f32[32,4,128]{2,1,0:T(4,128)S(1)}, u32[]{:S(2)}, u32[]{:S(2)}) collective-permute-start(f32[32,4,128]{2,1,0:T(4,128)S(1)} %get-tuple-element.44), channel_id=1, source_target_pairs={{0,2},{1,3},{2,0},{3,1},{4,6},{5,7},{6,4},{7,5},{8,10},{9,11},{10,... | collective-permute-start | bytes 196616 | tf_op jit(solution)/shard_map/ppermute | solution.py:558
  27.6 4.8 %collective-permute-start.13 = (f32[32,4,128]{2,1,0:T(4,128)S(1)}, f32[32,4,128]{2,1,0:T(4,128)S(1)}, u32[]{:S(2)}, u32[]{:S(2)}) collective-permute-start(f32[32,4,128]{2,1,0:T(4,128)S(1)} %get-tuple-element.45), channel_id=1, source_target_pairs={{0,3},{1,2},{2,1},{3,0},{4,7},{5,6},{6,5},{7,4},{8,11},{9,10},{10,... | collective-permute-start | bytes 196616 | tf_op jit(solution)/shard_map/ppermute | solution.py:558

commit v7 on v6

--- a/solution.py
+++ b/solution.py
@@ -17,7 +17,6 @@
 bf16 = jnp.bfloat16
 
 LEAD = 8
-AHEAD = 1
 COL = 16
 BLOCK = 16
 
@@ -457,9 +456,9 @@
     raw_ref,
     field,
     plus_ref,
-    near_ref,
-    *out_refs,
+    *rest,
 ):
+    out_refs, near_ref = rest[:-1], rest[-1]
     elements, columns = inverse_ref.shape[0], inverse_ref.shape[-1]
     face = 2 * G * G
     minus, plus, held = [], [], []
@@ -483,63 +482,68 @@
         near_ref[0, e] = product(half, held[e], True)
         following = weights(split(minus[(e + 1) % elements]), False)
         near_ref[1, e] = product(plus[e], following, False)
-    send_rows(count, [near_ref], out_refs, parted(count)[1])
+    send_rows(count, near_ref, out_refs)
 
 
 def partner(index, step, count):
     return index ^ step if count & (count - 1) == 0 else (index + step) % count
 
 
-def send_rows(count, sources, out_refs, steps):
-    elements, size = sources[0].shape[1:3]
+def partner(index, step, count):
+    return index ^ step if count & (count - 1) == 0 else (index + step) % count
+
+
+def send_rows(count, blocks_ref, out_refs):
+    kinds, elements, size = blocks_ref.shape[:3]
     rows = size // count
     me = lax.axis_index("ez")
-    for out_ref, step in zip(out_refs, steps):
+    for step, out_ref in enumerate(out_refs):
         owner = me ^ step if count & (count - 1) == 0 else lax.rem(me + step, count)
         at = pl.ds(pl.multiple_of(owner * rows, rows), rows)
-        slot = 0
-        for blocks_ref in sources:
-            for kind in range(blocks_ref.shape[0]):
-                for e in range(elements):
-                    out_ref[:, slot, :] = blocks_ref[kind, e, at, :]
-                    slot += 1
-
-
-def far_kernel(count, plus_ref, next_x_ref, next_z_ref, near_ref, *rest):
+        for kind in range(kinds):
+            for e in range(elements):
+                out_ref[:, kind, e, :] = blocks_ref[kind, e, at, :]
+
+
+def far_kernel(count, plus_ref, next_x_ref, next_z_ref, *rest):
     out_refs, far_ref = rest[:-1], rest[-1]
     for e in range(plus_ref.shape[0]):
         for d, ref in ((0, next_x_ref), (1, next_z_ref)):
             far_ref[d, e] = product(plus_ref[e, d], weights(split(ref[e]), False), False)
-    whole, ahead = parted(count)
-    send_rows(count, [near_ref, far_ref], out_refs[: len(whole)], whole)
-    send_rows(count, [far_ref], out_refs[len(whole) :], ahead)
-
-
-def parted(count):
-    return [step for step in range(count) if step < AHEAD], [
-        step for step in range(count) if step >= AHEAD
-    ]
-
-
-def assemble_kernel(count, *refs):
-    whole, ahead = parted(count)
-    whole_refs, refs = refs[: len(whole)], refs[len(whole) :]
-    near_refs, refs = refs[: len(ahead)], refs[len(ahead) :]
-    far_refs, (diagonal_ref, coupling_ref) = refs[: len(ahead)], refs[len(ahead) :]
-    elements = diagonal_ref.shape[2]
+    send_rows(count, far_ref, out_refs)
+
+
+def place(refs, targets, semaphores):
+    count = len(refs)
     me = lax.axis_index("ez")
-
-    def place(step, near_ref, far_ref, far_at):
+    copies = []
+    for step, ref in enumerate(refs):
         z = me ^ step if count & (count - 1) == 0 else lax.rem(me + (count - step), count)
-        diagonal_ref[:, z] = near_ref[:, :elements]
-        coupling_ref[:, z, 1] = near_ref[:, elements : 2 * elements]
-        coupling_ref[:, z, 0] = far_ref[:, far_at : far_at + elements]
-        coupling_ref[:, z, 2] = far_ref[:, far_at + elements : far_at + 2 * elements]
-
-    for step, ref in zip(whole, whole_refs):
-        place(step, ref, ref, 2 * elements)
-    for step, near_ref, far_ref in zip(ahead, near_refs, far_refs):
-        place(step, near_ref, far_ref, 0)
+        for kind, target in enumerate(targets(z)):
+            copies.append(
+                pltpu.make_async_copy(ref.at[:, kind], target, semaphores.at[step, kind])
+            )
+            copies[-1].start()
+    for copy in copies:
+        copy.wait()
+
+
+def place_near_kernel(count, *refs):
+    diagonal_ref, coupling_ref, semaphores = refs[count:]
+    place(
+        refs[:count],
+        lambda z: (diagonal_ref.at[:, z], coupling_ref.at[:, z, 1]),
+        semaphores,
+    )
+
+
+def place_far_kernel(count, *refs):
+    coupling_ref, semaphores = refs[count + 1 :]
+    place(
+        refs[:count],
+        lambda z: (coupling_ref.at[:, z, 0], coupling_ref.at[:, z, 2]),
+        semaphores,
+    )
 
 
 def vmem(count):
@@ -624,44 +628,54 @@
 
     next_x = shift(minus_x, "ex", -1)
     next_z = shift(minus_z, "ez", -1)
-    whole, ahead = parted(count)
-    block = shape((columns // count, 2 * elements, columns), f32)
-    double = shape((columns // count, 4 * elements, columns), f32)
-    squares = shape((2, elements, columns, columns), f32)
-    plus, own_near, *near = pl.pallas_call(
+    rows = columns // count
+    block = shape((rows, 2, elements, columns), f32)
+    squares = pltpu.VMEM((2, elements, columns, columns), f32)
+    plus, *near = pl.pallas_call(
         functools.partial(near_kernel, count, margin),
-        out_shape=[shape((elements, 2, columns, 2 * G * G), f32), squares] + [block] * len(ahead),
+        out_shape=[shape((elements, 2, columns, 2 * G * G), f32)] + [block] * count,
         in_specs=vmem(3),
-        out_specs=vmem(2 + len(ahead)),
+        out_specs=vmem(1 + count),
+        scratch_shapes=[squares],
         compiler_params=pltpu.CompilerParams(vmem_limit_bytes=24 * 2**20),
         cost_estimate=pl.CostEstimate(flops=10**8, bytes_accessed=10**7, transcendentals=0),
         name="near",
     )(inverse, raw, filtered)
-    near = [exchange(value, step) for value, step in zip(near, ahead)]
+    near = [exchange(value, step) for step, value in enumerate(near)]
 
     far = pl.pallas_call(
         functools.partial(far_kernel, count),
-        out_shape=[double] * len(whole) + [block] * len(ahead),
-        in_specs=vmem(4),
+        out_shape=[block] * count,
+        in_specs=vmem(3),
         out_specs=vmem(count),
-        scratch_shapes=[pltpu.VMEM(squares.shape, f32)],
+        scratch_shapes=[squares],
         compiler_params=pltpu.CompilerParams(vmem_limit_bytes=16 * 2**20),
         name="far",
-    )(plus, next_x, next_z, own_near)
-    far = [exchange(value, step) for value, step in zip(far, whole + ahead)]
-
-    rows = columns // count
+    )(plus, next_x, next_z)
+    far = [exchange(far[step], step) for step in reversed(range(count))][::-1]
+
+    anywhere = pl.BlockSpec(memory_space=pltpu.HBM)
+    semaphores = pltpu.SemaphoreType.DMA((count, 2))
+    half = shape((rows, count, 3, elements, columns), f32)
     diagonal, coupled = pl.pallas_call(
-        functools.partial(assemble_kernel, count),
-        out_shape=[
-            shape((rows, count, elements, columns), f32),
-            shape((rows, count, 3, elements, columns), f32),
-        ],
-        in_specs=vmem(len(whole) + 2 * len(ahead)),
-        out_specs=vmem(2),
+        functools.partial(place_near_kernel, count),
+        out_shape=[shape((rows, count, elements, columns), f32), half],
+        in_specs=vmem(count),
+        out_specs=[anywhere] * 2,
+        scratch_shapes=[semaphores],
         compiler_params=pltpu.CompilerParams(vmem_limit_bytes=16 * 2**20),
-        name="assemble",
-    )(*far[: len(whole)], *near, *far[len(whole) :])
+        name="place_near",
+    )(*near)
+    coupled = pl.pallas_call(
+        functools.partial(place_far_kernel, count),
+        out_shape=half,
+        in_specs=vmem(count) + [anywhere],
+        out_specs=anywhere,
+        input_output_aliases={count: 0},
+        scratch_shapes=[semaphores],
+        compiler_params=pltpu.CompilerParams(vmem_limit_bytes=16 * 2**20),
+        name="place_far",
+    )(*far, coupled)
     return (diagonal[None], coupled.transpose(0, 1, 3, 2, 4)[None])
 
 

time: 33.7 us -> 33.4 us (level)
  waiting for transfers between devices: 5.19 us -> 4.39 us
  Pallas kernels: 9.31 us -> 9.88 us
    ppermute x6, waiting for transfers between devices: 3.35 us -> 2.57 us  [exchange(): lax.ppermute(block, 'ez', [(i, partner(i, step, count)) for i in range(co...]
    pallas_call x2 -> x3, Pallas kernels: 1.35 us -> 1.89 us  [the longest x1 0.76 us: local(): pl.pallas_call(functools.partial(place_far_kernel, count), out_shape=half...]
  transfers between devices with their start and end apart: 14 -> 14, of which waited for: 4 -> 4; matrix products, arithmetic and copies ran while one was open for 2% -> 2% of each run, Pallas kernels for 13% -> 15%
where the time goes in v7:
time: 33.4 us; the launch traced here: 33.1 us
  starting transfers between devices  16.1 us (48%)
  Pallas kernels  9.88 us (30%)
  waiting for transfers between devices  4.39 us (13%)
  local copies, waits for them, and re-layouts  1.18 us (4%)
  other arithmetic  0.81 us (2%)
  between operations  0.75 us (2%)
    ppermute x8, starting transfers between devices, shift(): lax.ppermute(block, axis, [(i, (i + distance) % count) for i in range(cou...  10.9 us
    ppermute x6, starting transfers between devices, exchange(): lax.ppermute(block, 'ez', [(i, partner(i, step, count)) for i in range(co...  5.21 us
    pallas_call x1, Pallas kernels, local(): pl.pallas_call(functools.partial(basis_kernel, margin), out_shape=[face,...  4.16 us
    ppermute x6, waiting for transfers between devices, exchange(): lax.ppermute(block, 'ez', [(i, partner(i, step, count)) for i in range(co...  2.57 us
    pallas_call x1, Pallas kernels, local(): pl.pallas_call(functools.partial(middle_kernel, margin), out_shape=[field...  2.57 us
    ppermute x8, waiting for transfers between devices, shift(): lax.ppermute(block, axis, [(i, (i + distance) % count) for i in range(cou...  1.81 us
    unnamed x2, local copies, waits for them, and re-layouts  1.17 us
    pallas_call x1, Pallas kernels, local(): pl.pallas_call(functools.partial(near_kernel, count, margin), out_shape=[...  0.8 us
  transfers between devices with their start and end apart: 14, of which 4 were waited for; matrix products, arithmetic and copies ran while one was open for 2% of the time, Pallas kernels for 15%

profile of v7, /device:TPU:0, one launch (start us, length us, event | category | flops | bytes accessed | tf_op | source)
XLA Modules:
  0.0 33.1 jit_solution(16389256258743440299)
XLA Ops:
  0.6 3.0 %collective-permute-start.3 = (f32[8,8,16]{2,1,0:T(8,128)}, f32[8,8,16]{2,1,0:T(8,128)S(1)}, u32[]{:S(2)}, u32[]{:S(2)}) collective-permute-start(f32[8,8,16]{2,1,0:T(8,128)} %bitcast.9), channel_id=1, source_target_pairs={{0,4},{4,8},{8,12},{12,16},{16,20},{20,24},{24,28},{28,0},{1,5},{5... | collective-permute-start | bytes 12296 | tf_op jit(solution)/shard_map/ppermute | solution.py:555
  3.6 0.8 %add_multiply_fusion = f32[8,8,16]{2,1,0:T(8,128)S(1)} fusion(f32[8,16,8]{1,2,0:T(8,128)} %param.2), kind=kLoop, calls=%fused_computation.1 | loop fusion | flops 2048 | bytes 8192 | tf_op jit(solution)/shard_map/mul | solution.py:573
  4.4 3.0 %collective-permute-start = (f32[2,8,16]{2,1,0:T(8,128)S(1)}, f32[2,8,16]{2,1,0:T(8,128)S(1)}, u32[]{:S(2)}, u32[]{:S(2)}) collective-permute-start(f32[2,8,16]{2,1,0:T(8,128)S(1)} %slice.24), channel_id=1, source_target_pairs={{0,28},{4,0},{8,4},{12,8},{16,12},{20,16},{24,20},{28,24},{1,29},{... | collective-permute-start | bytes 3080 | tf_op jit(solution)/shard_map/ppermute | solution.py:555
  7.5 0.0 copy-start
  7.5 1.2 %copy-done = bf16[1,1,2,1728,128]{4,3,2,1,0:T(8,128)(2,1)S(1)} copy-done((bf16[1,1,2,1728,128]{4,3,2,1,0:T(8,128)(2,1)S(1)}, bf16[1,1,2,1728,128]{4,3,2,1,0:T(8,128)(2,1)}, u32[]{:S(2)}) %copy-start) | copy-done | bytes 884760
  8.7 0.5 %first.1 = (f32[2,14,208,128]{3,2,1,0:T(8,128)S(1)}, f32[2,14,208,128]{3,2,1,0:T(8,128)S(1)}) custom-call(bf16[2,1728,128]{2,1,0:T(8,128)(2,1)S(1)} %bitcast.7), custom_call_target="tpu_custom_call" | custom-call | flops 100000 | bytes 10000 | tf_op jit(solution)/shard_map/first/pallas_call | solution.py:580
  9.1 0.0 collective-permute-done.3
  9.2 0.7 %collective-permute-start.5 = (f32[10,2,16]{2,1,0:T(2,128)S(1)}, f32[10,2,16]{2,1,0:T(2,128)S(1)}, u32[]{:S(2)}, u32[]{:S(2)}) collective-permute-start(f32[10,2,16]{2,1,0:T(2,128)S(1)} %get-tuple-element.48), channel_id=1, source_target_pairs={{0,3},{1,0},{2,1},{3,2},{4,7},{5,4},{6,5},{7,6},{8,11},{9,8},{10,9... | collective-permute-start | bytes 3848 | tf_op jit(solution)/shard_map/ppermute | solution.py:555
  9.9 0.0 collective-permute-start.4
  9.9 0.0 collective-permute-done.x_after_ref
  9.9 1.7 %collective-permute-start.2 = (f32[2,2,16]{2,1,0:T(2,128)S(1)}, f32[2,2,16]{2,1,0:T(2,128)S(1)}, u32[]{:S(2)}, u32[]{:S(2)}) collective-permute-start(f32[2,2,16]{2,1,0:T(2,128)S(1)} %get-tuple-element.50), channel_id=1, source_target_pairs={{0,3},{1,0},{2,1},{3,2},{4,7},{5,4},{6,5},{7,6},{8,11},{9,8},{10,9... | collective-permute-start | bytes 776 | tf_op jit(solution)/shard_map/ppermute | solution.py:555
  11.6 0.0 collective-permute-start.1
  11.6 0.0 collective-permute-done.5.z_after_ref
  11.6 1.3 %collective-permute-done.4.z_before_ref = f32[10,2,16]{2,1,0:T(2,128)S(1)} collective-permute-done((f32[10,2,16]{2,1,0:T(2,128)S(1)}, f32[10,2,16]{2,1,0:T(2,128)S(1)}, u32[]{:S(2)}, u32[]{:S(2)}) %collective-permute-start.4) | collective-permute-done | bytes 1312 | tf_op jit(solution)/shard_map/ppermute | solution.py:555
  13.0 2.6 %middle.1 = (f32[2,14,208,128]{3,2,1,0:T(8,128)S(1)}, f32[2,14,208,128]{3,2,1,0:T(8,128)S(1)}, f32[12,16,16,128]{3,2,1,0:T(8,128)S(1)}, bf16[2,2304,256]{2,1,0:T(8,128)(2,1)S(1)}, f32[2,128,256]{2,1,0:T(8,128)S(1)}) custom-call(f32[10,8,16]{2,1,0:T(8,128)S(1)} %pad_maximum_fusion.low_ref, ...), custom_call_target="tpu_custom_call", output_to_operand_aliasing={{0}: (3, {}), {1}: (4, {})} | custom-call | flops 100000000 | bytes 10000000 | tf_op jit(solution)/shard_map/middle/pallas_call | solution.py:598
  15.6 0.0 collective-permute-done.2.z_after_ref
  15.6 0.0 collective-permute-done.1.z_before_ref
  15.6 4.2 %basis.1 = (f32[2,128,128]{2,1,0:T(8,128)S(1)}, f32[2,128,128]{2,1,0:T(8,128)S(1)}, f32[2,128,128]{2,1,0:T(8,128)S(1)}, f32[2,128,128]{2,1,0:T(8,128)S(1)}, f32[...) custom-call(f32[2,8,16]{2,1,0:T(8,128)S(1)} %collective-permute-done, ...), custom_call_target="tpu_custom_call", output_to_operand_aliasing={{4}: (3, {}), {5}: (4, {}), {6}: (5, {}), {7}: (6, {})} | custom-call | tf_op jit(solution)/shard_map/basis/pallas_call | solution.py:612
  19.7 1.8 %collective-permute-start.9 = (f32[2,128,128]{2,1,0:T(8,128)S(1)}, f32[2,128,128]{2,1,0:T(8,128)S(1)}, u32[]{:S(2)}, u32[]{:S(2)}) collective-permute-start(f32[2,128,128]{2,1,0:T(8,128)S(1)} %get-tuple-element.41), channel_id=1, source_target_pairs={{0,28},{4,0},{8,4},{12,8},{16,12},{20,16},{24,20},{28,24},{1,29},{... | collective-permute-start | bytes 393224 | tf_op jit(solution)/shard_map/ppermute | solution.py:555
  21.5 0.6 %collective-permute-start.10 = (f32[2,128,128]{2,1,0:T(8,128)S(1)}, f32[2,128,128]{2,1,0:T(8,128)S(1)}, u32[]{:S(2)}, u32[]{:S(2)}) collective-permute-start(f32[2,128,128]{2,1,0:T(8,128)S(1)} %get-tuple-element.42), channel_id=1, source_target_pairs={{0,3},{1,0},{2,1},{3,2},{4,7},{5,4},{6,5},{7,6},{8,11},{9,8},{10,9... | collective-permute-start | bytes 393224 | tf_op jit(solution)/shard_map/ppermute | solution.py:555
  22.2 0.8 %near.1 = (f32[2,2,128,128]{3,2,1,0:T(8,128)S(1)}, f32[32,2,2,128]{3,2,1,0:T(2,128)S(1)}, f32[32,2,2,128]{3,2,1,0:T(2,128)S(1)}, f32[32,2,2,128]{3,2,1,0:T(2,128)S(1)}, f32[32,2,2,128]{3,2,1,0:T(2,128)S(1)}) custom-call(f32[2,128,128]{2,1,0:T(8,128)S(1)} %get-tuple-element.32.inverse_ref, f32[2,128,128]{2,1,0:T(8,128)S(1)} %get-tuple-element.33.raw_ref, ...), custom_call_target="tpu_custom_call" | custom-call | flops 100000000 | bytes 10000000 | tf_op jit(solution)/shard_map/near/pallas_call | solution.py:634
  23.0 0.1 collective-permute-start.6
  23.0 1.7 %collective-permute-start.7 = (f32[32,2,2,128]{3,2,1,0:T(2,128)S(1)}, f32[32,2,2,128]{3,2,1,0:T(2,128)S(1)}, u32[]{:S(2)}, u32[]{:S(2)}) collective-permute-start(f32[32,2,2,128]{3,2,1,0:T(2,128)S(1)} %get-tuple-element.37), channel_id=1, source_target_pairs={{0,2},{1,3},{2,0},{3,1},{4,6},{5,7},{6,4},{7,5},{8,10},{9,11},{10,... | collective-permute-start | bytes 196616 | tf_op jit(solution)/shard_map/ppermute | solution.py:562
  24.7 0.2 collective-permute-start.8
  24.9 0.5 %collective-permute-done.9.next_x_ref = f32[2,128,128]{2,1,0:T(8,128)S(1)} collective-permute-done((f32[2,128,128]{2,1,0:T(8,128)S(1)}, f32[2,128,128]{2,1,0:T(8,128)S(1)}, u32[]{:S(2)}, u32[]{:S(2)}) %collective-permute-start.9) | collective-permute-done | bytes 131104 | tf_op jit(solution)/shard_map/ppermute | solution.py:555
  25.4 0.0 collective-permute-done.10.next_z_ref
  25.4 0.4 %far.1 = (f32[32,2,2,128]{3,2,1,0:T(2,128)S(1)}, f32[32,2,2,128]{3,2,1,0:T(2,128)S(1)}, f32[32,2,2,128]{3,2,1,0:T(2,128)S(1)}, f32[32,2,2,128]{3,2,1,0:T(2,128)S(1)}) custom-call(f32[2,2,128,128]{3,2,1,0:T(8,128)S(1)} %get-tuple-element.40.plus_ref, f32[2,128,128]{2,1,0:T(8,128)S(1)} %collective-permute-done.9.next_x_ref, ...), custom_call_target="tpu_custom_call" | custom-call | tf_op jit(solution)/shard_map/far/pallas_call | solution.py:646
  25.8 1.8 %collective-permute-start.11 = (f32[32,2,2,128]{3,2,1,0:T(2,128)S(1)}, f32[32,2,2,128]{3,2,1,0:T(2,128)S(1)}, u32[]{:S(2)}, u32[]{:S(2)}) collective-permute-start(f32[32,2,2,128]{3,2,1,0:T(2,128)S(1)} %get-tuple-element.44), channel_id=1, source_target_pairs={{0,1},{1,0},{2,3},{3,2},{4,5},{5,4},{6,7},{7,6},{8,9},{9,8},{10,11... | collective-permute-start | bytes 196616 | tf_op jit(solution)/shard_map/ppermute | solution.py:562
  27.6 0.0 collective-permute-start.12
  27.6 0.0 collective-permute-done.6.refs_1_
  27.6 1.4 %collective-permute-start.13 = (f32[32,2,2,128]{3,2,1,0:T(2,128)S(1)}, f32[32,2,2,128]{3,2,1,0:T(2,128)S(1)}, u32[]{:S(2)}, u32[]{:S(2)}) collective-permute-start(f32[32,2,2,128]{3,2,1,0:T(2,128)S(1)} %get-tuple-element.46), channel_id=1, source_target_pairs={{0,3},{1,2},{2,1},{3,0},{4,7},{5,6},{6,5},{7,4},{8,11},{9,10},{10,... | collective-permute-start | bytes 196616 | tf_op jit(solution)/shard_map/ppermute | solution.py:562
  29.0 0.0 collective-permute-done.7.refs_2_
  29.0 0.2 collective-permute-done.8.refs_3_
  29.2 0.8 %place_near.1 = (f32[32,4,2,128]{3,2,1,0:T(2,128)}, f32[32,4,3,2,128]{4,3,2,1,0:T(2,128)}) custom-call(f32[32,2,2,128]{3,2,1,0:T(2,128)S(1)} %get-tuple-element.35.refs_0_, f32[32,2,2,128]{3,2,1,0:T(2,128)S(1)} %collective-permute-done.6.refs_1_, f32[32,2,2,128]{3,2,1,0:T(2,128)S(1)} %collective-permute-done.7.refs_2_, ...), custom_call_target="tpu_custom_call" | custom-call | tf_op jit(solution)/shard_map/place_near/pallas_call | solution.py:660
  30.0 0.0 collective-permute-done.11.refs_1_
  30.0 2.4 %collective-permute-done.12.refs_2_ = f32[32,2,2,128]{3,2,1,0:T(2,128)S(1)} collective-permute-done((f32[32,2,2,128]{3,2,1,0:T(2,128)S(1)}, f32[32,2,2,128]{3,2,1,0:T(2,128)S(1)}, u32[]{:S(2)}, u32[]{:S(2)}) %collective-permute-start.12) | collective-permute-done | bytes 65568 | tf_op jit(solution)/shard_map/ppermute | solution.py:562
  32.4 0.0 collective-permute-done.13.refs_3_
  32.4 0.8 %place_far.1 = f32[32,4,3,2,128]{4,3,2,1,0:T(2,128)} custom-call(f32[32,2,2,128]{3,2,1,0:T(2,128)S(1)} %get-tuple-element.43.refs_0_, f32[32,2,2,128]{3,2,1,0:T(2,128)S(1)} %collective-permute-done.11.refs_1_, f32[32,2,2,128]{3,2,1,0:T(2,128)S(1)} %collective-permute-done.12.refs_2_, ...), custom_call_target="tpu_custom_call", output_to_operand_aliasing={{}: (4, {})} | custom-call | tf_op jit(solution)/shard_map/place_far/pallas_call | solution.py:669
  (5 shorter events, 0.0 us)
Async XLA Ops:
  0.6 8.5 %collective-permute-start.3 = (f32[8,8,16]{2,1,0:T(8,128)}, f32[8,8,16]{2,1,0:T(8,128)S(1)}, u32[]{:S(2)}, u32[]{:S(2)}) collective-permute-start(f32[8,8,16]{2,1,0:T(8,128)} %bitcast.9), channel_id=1, source_target_pairs={{0,4},{4,8},{8,12},{12,16},{16,20},{20,24},{24,28},{28,0},{1,5},{5... | collective-permute-start | bytes 12296 | tf_op jit(solution)/shard_map/ppermute | solution.py:555
  4.4 5.4 %collective-permute-start = (f32[2,8,16]{2,1,0:T(8,128)S(1)}, f32[2,8,16]{2,1,0:T(8,128)S(1)}, u32[]{:S(2)}, u32[]{:S(2)}) collective-permute-start(f32[2,8,16]{2,1,0:T(8,128)S(1)} %slice.24), channel_id=1, source_target_pairs={{0,28},{4,0},{8,4},{12,8},{16,12},{20,16},{24,20},{28,24},{1,29},{... | collective-permute-start | bytes 3080 | tf_op jit(solution)/shard_map/ppermute | solution.py:555
  7.5 1.2 %copy-start = (bf16[1,1,2,1728,128]{4,3,2,1,0:T(8,128)(2,1)S(1)}, bf16[1,1,2,1728,128]{4,3,2,1,0:T(8,128)(2,1)}, u32[]{:S(2)}) copy-start(bf16[1,1,2,1728,128]{4,3,2,1,0:T(8,128)(2,1)} %param.3) | copy-start | bytes 2654212
  9.2 2.5 %collective-permute-start.5 = (f32[10,2,16]{2,1,0:T(2,128)S(1)}, f32[10,2,16]{2,1,0:T(2,128)S(1)}, u32[]{:S(2)}, u32[]{:S(2)}) collective-permute-start(f32[10,2,16]{2,1,0:T(2,128)S(1)} %get-tuple-element.48), channel_id=1, source_target_pairs={{0,3},{1,0},{2,1},{3,2},{4,7},{5,4},{6,5},{7,6},{8,11},{9,8},{10,9... | collective-permute-start | bytes 3848 | tf_op jit(solution)/shard_map/ppermute | solution.py:555
  9.9 3.1 %collective-permute-start.4 = (f32[10,2,16]{2,1,0:T(2,128)S(1)}, f32[10,2,16]{2,1,0:T(2,128)S(1)}, u32[]{:S(2)}, u32[]{:S(2)}) collective-permute-start(f32[10,2,16]{2,1,0:T(2,128)S(1)} %get-tuple-element.49), channel_id=1, source_target_pairs={{0,1},{1,2},{2,3},{3,0},{4,5},{5,6},{6,7},{7,4},{8,9},{9,10},{10,1... | collective-permute-start | bytes 3848 | tf_op jit(solution)/shard_map/ppermute | solution.py:555
  9.9 5.7 %collective-permute-start.2 = (f32[2,2,16]{2,1,0:T(2,128)S(1)}, f32[2,2,16]{2,1,0:T(2,128)S(1)}, u32[]{:S(2)}, u32[]{:S(2)}) collective-permute-start(f32[2,2,16]{2,1,0:T(2,128)S(1)} %get-tuple-element.50), channel_id=1, source_target_pairs={{0,3},{1,0},{2,1},{3,2},{4,7},{5,4},{6,5},{7,6},{8,11},{9,8},{10,9... | collective-permute-start | bytes 776 | tf_op jit(solution)/shard_map/ppermute | solution.py:555
  11.6 3.9 %collective-permute-start.1 = (f32[2,2,16]{2,1,0:T(2,128)S(1)}, f32[2,2,16]{2,1,0:T(2,128)S(1)}, u32[]{:S(2)}, u32[]{:S(2)}) collective-permute-start(f32[2,2,16]{2,1,0:T(2,128)S(1)} %get-tuple-element.51), channel_id=1, source_target_pairs={{0,1},{1,2},{2,3},{3,0},{4,5},{5,6},{6,7},{7,4},{8,9},{9,10},{10,1... | collective-permute-start | bytes 776 | tf_op jit(solution)/shard_map/ppermute | solution.py:555
  19.7 5.6 %collective-permute-start.9 = (f32[2,128,128]{2,1,0:T(8,128)S(1)}, f32[2,128,128]{2,1,0:T(8,128)S(1)}, u32[]{:S(2)}, u32[]{:S(2)}) collective-permute-start(f32[2,128,128]{2,1,0:T(8,128)S(1)} %get-tuple-element.41), channel_id=1, source_target_pairs={{0,28},{4,0},{8,4},{12,8},{16,12},{20,16},{24,20},{28,24},{1,29},{... | collective-permute-start | bytes 393224 | tf_op jit(solution)/shard_map/ppermute | solution.py:555
  21.5 3.8 %collective-permute-start.10 = (f32[2,128,128]{2,1,0:T(8,128)S(1)}, f32[2,128,128]{2,1,0:T(8,128)S(1)}, u32[]{:S(2)}, u32[]{:S(2)}) collective-permute-start(f32[2,128,128]{2,1,0:T(8,128)S(1)} %get-tuple-element.42), channel_id=1, source_target_pairs={{0,3},{1,0},{2,1},{3,2},{4,7},{5,4},{6,5},{7,6},{8,11},{9,8},{10,9... | collective-permute-start | bytes 393224 | tf_op jit(solution)/shard_map/ppermute | solution.py:555
  23.0 4.6 %collective-permute-start.6 = (f32[32,2,2,128]{3,2,1,0:T(2,128)S(1)}, f32[32,2,2,128]{3,2,1,0:T(2,128)S(1)}, u32[]{:S(2)}, u32[]{:S(2)}) collective-permute-start(f32[32,2,2,128]{3,2,1,0:T(2,128)S(1)} %get-tuple-element.36), channel_id=1, source_target_pairs={{0,1},{1,0},{2,3},{3,2},{4,5},{5,4},{6,7},{7,6},{8,9},{9,8},{10,11... | collective-permute-start | bytes 196616 | tf_op jit(solution)/shard_map/ppermute | solution.py:562
  23.0 6.0 %collective-permute-start.7 = (f32[32,2,2,128]{3,2,1,0:T(2,128)S(1)}, f32[32,2,2,128]{3,2,1,0:T(2,128)S(1)}, u32[]{:S(2)}, u32[]{:S(2)}) collective-permute-start(f32[32,2,2,128]{3,2,1,0:T(2,128)S(1)} %get-tuple-element.37), channel_id=1, source_target_pairs={{0,2},{1,3},{2,0},{3,1},{4,6},{5,7},{6,4},{7,5},{8,10},{9,11},{10,... | collective-permute-start | bytes 196616 | tf_op jit(solution)/shard_map/ppermute | solution.py:562
  24.7 4.5 %collective-permute-start.8 = (f32[32,2,2,128]{3,2,1,0:T(2,128)S(1)}, f32[32,2,2,128]{3,2,1,0:T(2,128)S(1)}, u32[]{:S(2)}, u32[]{:S(2)}) collective-permute-start(f32[32,2,2,128]{3,2,1,0:T(2,128)S(1)} %get-tuple-element.38), channel_id=1, source_target_pairs={{0,3},{1,2},{2,1},{3,0},{4,7},{5,6},{6,5},{7,4},{8,11},{9,10},{10,... | collective-permute-start | bytes 196616 | tf_op jit(solution)/shard_map/ppermute | solution.py:562
  25.8 4.2 %collective-permute-start.11 = (f32[32,2,2,128]{3,2,1,0:T(2,128)S(1)}, f32[32,2,2,128]{3,2,1,0:T(2,128)S(1)}, u32[]{:S(2)}, u32[]{:S(2)}) collective-permute-start(f32[32,2,2,128]{3,2,1,0:T(2,128)S(1)} %get-tuple-element.44), channel_id=1, source_target_pairs={{0,1},{1,0},{2,3},{3,2},{4,5},{5,4},{6,7},{7,6},{8,9},{9,8},{10,11... | collective-permute-start | bytes 196616 | tf_op jit(solution)/shard_map/ppermute | solution.py:562
  27.6 4.8 %collective-permute-start.12 = (f32[32,2,2,128]{3,2,1,0:T(2,128)S(1)}, f32[32,2,2,128]{3,2,1,0:T(2,128)S(1)}, u32[]{:S(2)}, u32[]{:S(2)}) collective-permute-start(f32[32,2,2,128]{3,2,1,0:T(2,128)S(1)} %get-tuple-element.45), channel_id=1, source_target_pairs={{0,2},{1,3},{2,0},{3,1},{4,6},{5,7},{6,4},{7,5},{8,10},{9,11},{10,... | collective-permute-start | bytes 196616 | tf_op jit(solution)/shard_map/ppermute | solution.py:562
  27.6 4.8 %collective-permute-start.13 = (f32[32,2,2,128]{3,2,1,0:T(2,128)S(1)}, f32[32,2,2,128]{3,2,1,0:T(2,128)S(1)}, u32[]{:S(2)}, u32[]{:S(2)}) collective-permute-start(f32[32,2,2,128]{3,2,1,0:T(2,128)S(1)} %get-tuple-element.46), channel_id=1, source_target_pairs={{0,3},{1,2},{2,1},{3,0},{4,7},{5,6},{6,5},{7,4},{8,11},{9,10},{10,... | collective-permute-start | bytes 196616 | tf_op jit(solution)/shard_map/ppermute | solution.py:562

commit v8 on v7

--- a/solution.py
+++ b/solution.py
@@ -145,7 +145,7 @@
             for j in range(k + 1, BLOCK):
                 columns[j] = columns[j] - factor * bcast_row(columns[j], k)
             panel = [value - factor * bcast_row(value, k) for value in panel]
-            if k == 3 and below < size:
+            if k == 8 and below < size:
                 factors = [columns_of(values[0], at + j) for j in range(BLOCK)]
         solved = [value * reciprocals for value in panel]
         scale = lax.rsqrt(pivots)
@@ -271,7 +271,8 @@
             slab_step(x, source, scaled_ref, target, target, pair, margin)
             return carry
 
-        lax.fori_loop(*ranges(index), next_step, 0, unroll=4)
+        low, high = ranges(index)
+        lax.fori_loop(low, high, next_step, 0, unroll=min(4, high - low))
         fields = fields[::-1]
     return fields[0]
 
@@ -540,7 +541,7 @@
 def place_far_kernel(count, *refs):
     coupling_ref, semaphores = refs[count + 1 :]
     place(
-        refs[:count],
+        refs[:count][::-1],
         lambda z: (coupling_ref.at[:, z, 0], coupling_ref.at[:, z, 2]),
         semaphores,
     )
@@ -675,7 +676,7 @@
         scratch_shapes=[semaphores],
         compiler_params=pltpu.CompilerParams(vmem_limit_bytes=16 * 2**20),
         name="place_far",
-    )(*far, coupled)
+    )(*far[::-1], coupled)
     return (diagonal[None], coupled.transpose(0, 1, 3, 2, 4)[None])
 
 

time: 33.4 us -> 33.4 us (level)
  no operation moved by 1% of the time
where the time goes in v8:
time: 33.4 us; the launch traced here: 33.2 us
  starting transfers between devices  16.3 us (49%)
  Pallas kernels  9.9 us (30%)
  waiting for transfers between devices  4.17 us (12%)
  local copies, waits for them, and re-layouts  1.18 us (4%)
  other arithmetic  0.81 us (2%)
  between operations  0.75 us (2%)
    ppermute x8, starting transfers between devices, shift(): lax.ppermute(block, axis, [(i, (i + distance) % count) for i in range(cou...  10.9 us
    ppermute x6, starting transfers between devices, exchange(): lax.ppermute(block, 'ez', [(i, partner(i, step, count)) for i in range(co...  5.41 us
    pallas_call x1, Pallas kernels, local(): pl.pallas_call(functools.partial(basis_kernel, margin), out_shape=[face,...  4.17 us
    pallas_call x1, Pallas kernels, local(): pl.pallas_call(functools.partial(middle_kernel, margin), out_shape=[field...  2.57 us
    ppermute x6, waiting for transfers between devices, exchange(): lax.ppermute(block, 'ez', [(i, partner(i, step, count)) for i in range(co...  2.36 us
    ppermute x8, waiting for transfers between devices, shift(): lax.ppermute(block, axis, [(i, (i + distance) % count) for i in range(cou...  1.81 us
    unnamed x2, local copies, waits for them, and re-layouts  1.17 us
    pallas_call x1, Pallas kernels, local(): pl.pallas_call(functools.partial(near_kernel, count, margin), out_shape=[...  0.8 us
  transfers between devices with their start and end apart: 14, of which 4 were waited for; matrix products, arithmetic and copies ran while one was open for 2% of the time, Pallas kernels for 15%

profile of v8, /device:TPU:0, one launch (start us, length us, event | category | flops | bytes accessed | tf_op | source)
XLA Modules:
  0.0 33.2 jit_solution(906329324186003311)
XLA Ops:
  0.6 3.0 %collective-permute-start.3 = (f32[8,8,16]{2,1,0:T(8,128)}, f32[8,8,16]{2,1,0:T(8,128)S(1)}, u32[]{:S(2)}, u32[]{:S(2)}) collective-permute-start(f32[8,8,16]{2,1,0:T(8,128)} %bitcast.9), channel_id=1, source_target_pairs={{0,4},{4,8},{8,12},{12,16},{16,20},{20,24},{24,28},{28,0},{1,5},{5... | collective-permute-start | bytes 12296 | tf_op jit(solution)/shard_map/ppermute | solution.py:556
  3.6 0.8 %add_multiply_fusion = f32[8,8,16]{2,1,0:T(8,128)S(1)} fusion(f32[8,16,8]{1,2,0:T(8,128)} %param.2), kind=kLoop, calls=%fused_computation.1 | loop fusion | flops 2048 | bytes 8192 | tf_op jit(solution)/shard_map/mul | solution.py:574
  4.4 3.0 %collective-permute-start = (f32[2,8,16]{2,1,0:T(8,128)S(1)}, f32[2,8,16]{2,1,0:T(8,128)S(1)}, u32[]{:S(2)}, u32[]{:S(2)}) collective-permute-start(f32[2,8,16]{2,1,0:T(8,128)S(1)} %slice.24), channel_id=1, source_target_pairs={{0,28},{4,0},{8,4},{12,8},{16,12},{20,16},{24,20},{28,24},{1,29},{... | collective-permute-start | bytes 3080 | tf_op jit(solution)/shard_map/ppermute | solution.py:556
  7.5 0.0 copy-start
  7.5 1.2 %copy-done = bf16[1,1,2,1728,128]{4,3,2,1,0:T(8,128)(2,1)S(1)} copy-done((bf16[1,1,2,1728,128]{4,3,2,1,0:T(8,128)(2,1)S(1)}, bf16[1,1,2,1728,128]{4,3,2,1,0:T(8,128)(2,1)}, u32[]{:S(2)}) %copy-start) | copy-done | bytes 884760
  8.7 0.5 %first.1 = (f32[2,14,208,128]{3,2,1,0:T(8,128)S(1)}, f32[2,14,208,128]{3,2,1,0:T(8,128)S(1)}) custom-call(bf16[2,1728,128]{2,1,0:T(8,128)(2,1)S(1)} %bitcast.7), custom_call_target="tpu_custom_call" | custom-call | flops 100000 | bytes 10000 | tf_op jit(solution)/shard_map/first/pallas_call | solution.py:581
  9.1 0.0 collective-permute-done.3
  9.2 0.7 %collective-permute-start.5 = (f32[10,2,16]{2,1,0:T(2,128)S(1)}, f32[10,2,16]{2,1,0:T(2,128)S(1)}, u32[]{:S(2)}, u32[]{:S(2)}) collective-permute-start(f32[10,2,16]{2,1,0:T(2,128)S(1)} %get-tuple-element.48), channel_id=1, source_target_pairs={{0,3},{1,0},{2,1},{3,2},{4,7},{5,4},{6,5},{7,6},{8,11},{9,8},{10,9... | collective-permute-start | bytes 3848 | tf_op jit(solution)/shard_map/ppermute | solution.py:556
  9.9 0.0 collective-permute-start.4
  9.9 0.0 collective-permute-done.x_after_ref
  9.9 1.7 %collective-permute-start.2 = (f32[2,2,16]{2,1,0:T(2,128)S(1)}, f32[2,2,16]{2,1,0:T(2,128)S(1)}, u32[]{:S(2)}, u32[]{:S(2)}) collective-permute-start(f32[2,2,16]{2,1,0:T(2,128)S(1)} %get-tuple-element.50), channel_id=1, source_target_pairs={{0,3},{1,0},{2,1},{3,2},{4,7},{5,4},{6,5},{7,6},{8,11},{9,8},{10,9... | collective-permute-start | bytes 776 | tf_op jit(solution)/shard_map/ppermute | solution.py:556
  11.6 0.0 collective-permute-start.1
  11.6 0.0 collective-permute-done.5.z_after_ref
  11.6 1.3 %collective-permute-done.4.z_before_ref = f32[10,2,16]{2,1,0:T(2,128)S(1)} collective-permute-done((f32[10,2,16]{2,1,0:T(2,128)S(1)}, f32[10,2,16]{2,1,0:T(2,128)S(1)}, u32[]{:S(2)}, u32[]{:S(2)}) %collective-permute-start.4) | collective-permute-done | bytes 1312 | tf_op jit(solution)/shard_map/ppermute | solution.py:556
  13.0 2.6 %middle.1 = (f32[2,14,208,128]{3,2,1,0:T(8,128)S(1)}, f32[2,14,208,128]{3,2,1,0:T(8,128)S(1)}, f32[12,16,16,128]{3,2,1,0:T(8,128)S(1)}, bf16[2,2304,256]{2,1,0:T(8,128)(2,1)S(1)}, f32[2,128,256]{2,1,0:T(8,128)S(1)}) custom-call(f32[10,8,16]{2,1,0:T(8,128)S(1)} %pad_maximum_fusion.low_ref, ...), custom_call_target="tpu_custom_call", output_to_operand_aliasing={{0}: (3, {}), {1}: (4, {})} | custom-call | flops 100000000 | bytes 10000000 | tf_op jit(solution)/shard_map/middle/pallas_call | solution.py:599
  15.6 0.0 collective-permute-done.2.z_after_ref
  15.6 0.0 collective-permute-done.1.z_before_ref
  15.6 4.2 %basis.1 = (f32[2,128,128]{2,1,0:T(8,128)S(1)}, f32[2,128,128]{2,1,0:T(8,128)S(1)}, f32[2,128,128]{2,1,0:T(8,128)S(1)}, f32[2,128,128]{2,1,0:T(8,128)S(1)}, f32[...) custom-call(f32[2,8,16]{2,1,0:T(8,128)S(1)} %collective-permute-done, ...), custom_call_target="tpu_custom_call", output_to_operand_aliasing={{4}: (3, {}), {5}: (4, {}), {6}: (5, {}), {7}: (6, {})} | custom-call | tf_op jit(solution)/shard_map/basis/pallas_call | solution.py:613
  19.8 1.8 %collective-permute-start.9 = (f32[2,128,128]{2,1,0:T(8,128)S(1)}, f32[2,128,128]{2,1,0:T(8,128)S(1)}, u32[]{:S(2)}, u32[]{:S(2)}) collective-permute-start(f32[2,128,128]{2,1,0:T(8,128)S(1)} %get-tuple-element.41), channel_id=1, source_target_pairs={{0,28},{4,0},{8,4},{12,8},{16,12},{20,16},{24,20},{28,24},{1,29},{... | collective-permute-start | bytes 393224 | tf_op jit(solution)/shard_map/ppermute | solution.py:556
  21.5 0.6 %collective-permute-start.10 = (f32[2,128,128]{2,1,0:T(8,128)S(1)}, f32[2,128,128]{2,1,0:T(8,128)S(1)}, u32[]{:S(2)}, u32[]{:S(2)}) collective-permute-start(f32[2,128,128]{2,1,0:T(8,128)S(1)} %get-tuple-element.42), channel_id=1, source_target_pairs={{0,3},{1,0},{2,1},{3,2},{4,7},{5,4},{6,5},{7,6},{8,11},{9,8},{10,9... | collective-permute-start | bytes 393224 | tf_op jit(solution)/shard_map/ppermute | solution.py:556
  22.2 0.8 %near.1 = (f32[2,2,128,128]{3,2,1,0:T(8,128)S(1)}, f32[32,2,2,128]{3,2,1,0:T(2,128)S(1)}, f32[32,2,2,128]{3,2,1,0:T(2,128)S(1)}, f32[32,2,2,128]{3,2,1,0:T(2,128)S(1)}, f32[32,2,2,128]{3,2,1,0:T(2,128)S(1)}) custom-call(f32[2,128,128]{2,1,0:T(8,128)S(1)} %get-tuple-element.32.inverse_ref, f32[2,128,128]{2,1,0:T(8,128)S(1)} %get-tuple-element.33.raw_ref, ...), custom_call_target="tpu_custom_call" | custom-call | flops 100000000 | bytes 10000000 | tf_op jit(solution)/shard_map/near/pallas_call | solution.py:635
  23.0 0.1 collective-permute-start.6
  23.1 1.7 %collective-permute-start.7 = (f32[32,2,2,128]{3,2,1,0:T(2,128)S(1)}, f32[32,2,2,128]{3,2,1,0:T(2,128)S(1)}, u32[]{:S(2)}, u32[]{:S(2)}) collective-permute-start(f32[32,2,2,128]{3,2,1,0:T(2,128)S(1)} %get-tuple-element.37), channel_id=1, source_target_pairs={{0,2},{1,3},{2,0},{3,1},{4,6},{5,7},{6,4},{7,5},{8,10},{9,11},{10,... | collective-permute-start | bytes 196616 | tf_op jit(solution)/shard_map/ppermute | solution.py:563
  24.7 0.2 collective-permute-start.8
  24.9 0.5 %collective-permute-done.9.next_x_ref = f32[2,128,128]{2,1,0:T(8,128)S(1)} collective-permute-done((f32[2,128,128]{2,1,0:T(8,128)S(1)}, f32[2,128,128]{2,1,0:T(8,128)S(1)}, u32[]{:S(2)}, u32[]{:S(2)}) %collective-permute-start.9) | collective-permute-done | bytes 131104 | tf_op jit(solution)/shard_map/ppermute | solution.py:556
  25.4 0.0 collective-permute-done.10.next_z_ref
  25.4 0.4 %far.1 = (f32[32,2,2,128]{3,2,1,0:T(2,128)S(1)}, f32[32,2,2,128]{3,2,1,0:T(2,128)S(1)}, f32[32,2,2,128]{3,2,1,0:T(2,128)S(1)}, f32[32,2,2,128]{3,2,1,0:T(2,128)S(1)}) custom-call(f32[2,2,128,128]{3,2,1,0:T(8,128)S(1)} %get-tuple-element.40.plus_ref, f32[2,128,128]{2,1,0:T(8,128)S(1)} %collective-permute-done.9.next_x_ref, ...), custom_call_target="tpu_custom_call" | custom-call | tf_op jit(solution)/shard_map/far/pallas_call | solution.py:647
  25.8 1.2 %collective-permute-start.11 = (f32[32,2,2,128]{3,2,1,0:T(2,128)S(1)}, f32[32,2,2,128]{3,2,1,0:T(2,128)S(1)}, u32[]{:S(2)}, u32[]{:S(2)}) collective-permute-start(f32[32,2,2,128]{3,2,1,0:T(2,128)S(1)} %get-tuple-element.43), channel_id=1, source_target_pairs={{0,3},{1,2},{2,1},{3,0},{4,7},{5,6},{6,5},{7,4},{8,11},{9,10},{10,... | collective-permute-start | bytes 196616 | tf_op jit(solution)/shard_map/ppermute | solution.py:563
  27.0 2.2 %collective-permute-start.12 = (f32[32,2,2,128]{3,2,1,0:T(2,128)S(1)}, f32[32,2,2,128]{3,2,1,0:T(2,128)S(1)}, u32[]{:S(2)}, u32[]{:S(2)}) collective-permute-start(f32[32,2,2,128]{3,2,1,0:T(2,128)S(1)} %get-tuple-element.44), channel_id=1, source_target_pairs={{0,2},{1,3},{2,0},{3,1},{4,6},{5,7},{6,4},{7,5},{8,10},{9,11},{10,... | collective-permute-start | bytes 196616 | tf_op jit(solution)/shard_map/ppermute | solution.py:563
  29.2 0.0 collective-permute-done.6.refs_1_
  29.2 0.0 collective-permute-start.13
  29.2 0.0 collective-permute-done.7.refs_2_
  29.3 0.0 collective-permute-done.8.refs_3_
  29.3 0.8 %place_near.1 = (f32[32,4,2,128]{3,2,1,0:T(2,128)}, f32[32,4,3,2,128]{4,3,2,1,0:T(2,128)}) custom-call(f32[32,2,2,128]{3,2,1,0:T(2,128)S(1)} %get-tuple-element.35.refs_0_, f32[32,2,2,128]{3,2,1,0:T(2,128)S(1)} %collective-permute-done.6.refs_1_, f32[32,2,2,128]{3,2,1,0:T(2,128)S(1)} %collective-permute-done.7.refs_2_, ...), custom_call_target="tpu_custom_call" | custom-call | tf_op jit(solution)/shard_map/place_near/pallas_call | solution.py:661
  30.0 0.2 collective-permute-done.11.refs_0_
  30.3 2.1 %collective-permute-done.12.refs_1_ = f32[32,2,2,128]{3,2,1,0:T(2,128)S(1)} collective-permute-done((f32[32,2,2,128]{3,2,1,0:T(2,128)S(1)}, f32[32,2,2,128]{3,2,1,0:T(2,128)S(1)}, u32[]{:S(2)}, u32[]{:S(2)}) %collective-permute-start.12) | collective-permute-done | bytes 65568 | tf_op jit(solution)/shard_map/ppermute | solution.py:563
  32.4 0.0 collective-permute-done.13.refs_2_
  32.4 0.8 %place_far.1 = f32[32,4,3,2,128]{4,3,2,1,0:T(2,128)} custom-call(f32[32,2,2,128]{3,2,1,0:T(2,128)S(1)} %collective-permute-done.11.refs_0_, f32[32,2,2,128]{3,2,1,0:T(2,128)S(1)} %collective-permute-done.12.refs_1_, f32[32,2,2,128]{3,2,1,0:T(2,128)S(1)} %collective-permute-done.13.refs_2_, ...), custom_call_target="tpu_custom_call", output_to_operand_aliasing={{}: (4, {})} | custom-call | tf_op jit(solution)/shard_map/place_far/pallas_call | solution.py:670
  (5 shorter events, 0.0 us)
Async XLA Ops:
  0.6 8.5 %collective-permute-start.3 = (f32[8,8,16]{2,1,0:T(8,128)}, f32[8,8,16]{2,1,0:T(8,128)S(1)}, u32[]{:S(2)}, u32[]{:S(2)}) collective-permute-start(f32[8,8,16]{2,1,0:T(8,128)} %bitcast.9), channel_id=1, source_target_pairs={{0,4},{4,8},{8,12},{12,16},{16,20},{20,24},{24,28},{28,0},{1,5},{5... | collective-permute-start | bytes 12296 | tf_op jit(solution)/shard_map/ppermute | solution.py:556
  4.4 5.4 %collective-permute-start = (f32[2,8,16]{2,1,0:T(8,128)S(1)}, f32[2,8,16]{2,1,0:T(8,128)S(1)}, u32[]{:S(2)}, u32[]{:S(2)}) collective-permute-start(f32[2,8,16]{2,1,0:T(8,128)S(1)} %slice.24), channel_id=1, source_target_pairs={{0,28},{4,0},{8,4},{12,8},{16,12},{20,16},{24,20},{28,24},{1,29},{... | collective-permute-start | bytes 3080 | tf_op jit(solution)/shard_map/ppermute | solution.py:556
  7.5 1.2 %copy-start = (bf16[1,1,2,1728,128]{4,3,2,1,0:T(8,128)(2,1)S(1)}, bf16[1,1,2,1728,128]{4,3,2,1,0:T(8,128)(2,1)}, u32[]{:S(2)}) copy-start(bf16[1,1,2,1728,128]{4,3,2,1,0:T(8,128)(2,1)} %param.3) | copy-start | bytes 2654212
  9.2 2.5 %collective-permute-start.5 = (f32[10,2,16]{2,1,0:T(2,128)S(1)}, f32[10,2,16]{2,1,0:T(2,128)S(1)}, u32[]{:S(2)}, u32[]{:S(2)}) collective-permute-start(f32[10,2,16]{2,1,0:T(2,128)S(1)} %get-tuple-element.48), channel_id=1, source_target_pairs={{0,3},{1,0},{2,1},{3,2},{4,7},{5,4},{6,5},{7,6},{8,11},{9,8},{10,9... | collective-permute-start | bytes 3848 | tf_op jit(solution)/shard_map/ppermute | solution.py:556
  9.9 3.1 %collective-permute-start.4 = (f32[10,2,16]{2,1,0:T(2,128)S(1)}, f32[10,2,16]{2,1,0:T(2,128)S(1)}, u32[]{:S(2)}, u32[]{:S(2)}) collective-permute-start(f32[10,2,16]{2,1,0:T(2,128)S(1)} %get-tuple-element.49), channel_id=1, source_target_pairs={{0,1},{1,2},{2,3},{3,0},{4,5},{5,6},{6,7},{7,4},{8,9},{9,10},{10,1... | collective-permute-start | bytes 3848 | tf_op jit(solution)/shard_map/ppermute | solution.py:556
  9.9 5.7 %collective-permute-start.2 = (f32[2,2,16]{2,1,0:T(2,128)S(1)}, f32[2,2,16]{2,1,0:T(2,128)S(1)}, u32[]{:S(2)}, u32[]{:S(2)}) collective-permute-start(f32[2,2,16]{2,1,0:T(2,128)S(1)} %get-tuple-element.50), channel_id=1, source_target_pairs={{0,3},{1,0},{2,1},{3,2},{4,7},{5,4},{6,5},{7,6},{8,11},{9,8},{10,9... | collective-permute-start | bytes 776 | tf_op jit(solution)/shard_map/ppermute | solution.py:556
  11.6 3.9 %collective-permute-start.1 = (f32[2,2,16]{2,1,0:T(2,128)S(1)}, f32[2,2,16]{2,1,0:T(2,128)S(1)}, u32[]{:S(2)}, u32[]{:S(2)}) collective-permute-start(f32[2,2,16]{2,1,0:T(2,128)S(1)} %get-tuple-element.51), channel_id=1, source_target_pairs={{0,1},{1,2},{2,3},{3,0},{4,5},{5,6},{6,7},{7,4},{8,9},{9,10},{10,1... | collective-permute-start | bytes 776 | tf_op jit(solution)/shard_map/ppermute | solution.py:556
  19.8 5.6 %collective-permute-start.9 = (f32[2,128,128]{2,1,0:T(8,128)S(1)}, f32[2,128,128]{2,1,0:T(8,128)S(1)}, u32[]{:S(2)}, u32[]{:S(2)}) collective-permute-start(f32[2,128,128]{2,1,0:T(8,128)S(1)} %get-tuple-element.41), channel_id=1, source_target_pairs={{0,28},{4,0},{8,4},{12,8},{16,12},{20,16},{24,20},{28,24},{1,29},{... | collective-permute-start | bytes 393224 | tf_op jit(solution)/shard_map/ppermute | solution.py:556
  21.5 3.8 %collective-permute-start.10 = (f32[2,128,128]{2,1,0:T(8,128)S(1)}, f32[2,128,128]{2,1,0:T(8,128)S(1)}, u32[]{:S(2)}, u32[]{:S(2)}) collective-permute-start(f32[2,128,128]{2,1,0:T(8,128)S(1)} %get-tuple-element.42), channel_id=1, source_target_pairs={{0,3},{1,0},{2,1},{3,2},{4,7},{5,4},{6,5},{7,6},{8,11},{9,8},{10,9... | collective-permute-start | bytes 393224 | tf_op jit(solution)/shard_map/ppermute | solution.py:556
  23.0 6.3 %collective-permute-start.6 = (f32[32,2,2,128]{3,2,1,0:T(2,128)S(1)}, f32[32,2,2,128]{3,2,1,0:T(2,128)S(1)}, u32[]{:S(2)}, u32[]{:S(2)}) collective-permute-start(f32[32,2,2,128]{3,2,1,0:T(2,128)S(1)} %get-tuple-element.36), channel_id=1, source_target_pairs={{0,1},{1,0},{2,3},{3,2},{4,5},{5,4},{6,7},{7,6},{8,9},{9,8},{10,11... | collective-permute-start | bytes 196616 | tf_op jit(solution)/shard_map/ppermute | solution.py:563
  23.1 6.2 %collective-permute-start.7 = (f32[32,2,2,128]{3,2,1,0:T(2,128)S(1)}, f32[32,2,2,128]{3,2,1,0:T(2,128)S(1)}, u32[]{:S(2)}, u32[]{:S(2)}) collective-permute-start(f32[32,2,2,128]{3,2,1,0:T(2,128)S(1)} %get-tuple-element.37), channel_id=1, source_target_pairs={{0,2},{1,3},{2,0},{3,1},{4,6},{5,7},{6,4},{7,5},{8,10},{9,11},{10,... | collective-permute-start | bytes 196616 | tf_op jit(solution)/shard_map/ppermute | solution.py:563
  24.7 4.5 %collective-permute-start.8 = (f32[32,2,2,128]{3,2,1,0:T(2,128)S(1)}, f32[32,2,2,128]{3,2,1,0:T(2,128)S(1)}, u32[]{:S(2)}, u32[]{:S(2)}) collective-permute-start(f32[32,2,2,128]{3,2,1,0:T(2,128)S(1)} %get-tuple-element.38), channel_id=1, source_target_pairs={{0,3},{1,2},{2,1},{3,0},{4,7},{5,6},{6,5},{7,4},{8,11},{9,10},{10,... | collective-permute-start | bytes 196616 | tf_op jit(solution)/shard_map/ppermute | solution.py:563
  25.8 4.5 %collective-permute-start.11 = (f32[32,2,2,128]{3,2,1,0:T(2,128)S(1)}, f32[32,2,2,128]{3,2,1,0:T(2,128)S(1)}, u32[]{:S(2)}, u32[]{:S(2)}) collective-permute-start(f32[32,2,2,128]{3,2,1,0:T(2,128)S(1)} %get-tuple-element.43), channel_id=1, source_target_pairs={{0,3},{1,2},{2,1},{3,0},{4,7},{5,6},{6,5},{7,4},{8,11},{9,10},{10,... | collective-permute-start | bytes 196616 | tf_op jit(solution)/shard_map/ppermute | solution.py:563
  27.0 5.4 %collective-permute-start.12 = (f32[32,2,2,128]{3,2,1,0:T(2,128)S(1)}, f32[32,2,2,128]{3,2,1,0:T(2,128)S(1)}, u32[]{:S(2)}, u32[]{:S(2)}) collective-permute-start(f32[32,2,2,128]{3,2,1,0:T(2,128)S(1)} %get-tuple-element.44), channel_id=1, source_target_pairs={{0,2},{1,3},{2,0},{3,1},{4,6},{5,7},{6,4},{7,5},{8,10},{9,11},{10,... | collective-permute-start | bytes 196616 | tf_op jit(solution)/shard_map/ppermute | solution.py:563
  29.2 3.1 %collective-permute-start.13 = (f32[32,2,2,128]{3,2,1,0:T(2,128)S(1)}, f32[32,2,2,128]{3,2,1,0:T(2,128)S(1)}, u32[]{:S(2)}, u32[]{:S(2)}) collective-permute-start(f32[32,2,2,128]{3,2,1,0:T(2,128)S(1)} %get-tuple-element.45), channel_id=1, source_target_pairs={{0,1},{1,0},{2,3},{3,2},{4,5},{5,4},{6,7},{7,6},{8,9},{9,8},{10,11... | collective-permute-start | bytes 196616 | tf_op jit(solution)/shard_map/ppermute | solution.py:563

commit v9 on v8

--- a/solution.py
+++ b/solution.py
@@ -529,10 +529,14 @@
         copy.wait()
 
 
+def near_order(count):
+    return [*range(2, count), *range(min(2, count))[::-1]]
+
+
 def place_near_kernel(count, *refs):
     diagonal_ref, coupling_ref, semaphores = refs[count:]
     place(
-        refs[:count],
+        [refs[near_order(count).index(step)] for step in range(count)],
         lambda z: (diagonal_ref.at[:, z], coupling_ref.at[:, z, 1]),
         semaphores,
     )
@@ -666,7 +670,7 @@
         scratch_shapes=[semaphores],
         compiler_params=pltpu.CompilerParams(vmem_limit_bytes=16 * 2**20),
         name="place_near",
-    )(*near)
+    )(*[near[step] for step in near_order(count)])
     coupled = pl.pallas_call(
         functools.partial(place_far_kernel, count),
         out_shape=half,

time: 33.4 us -> 33.5 us (level)
  starting transfers between devices: 16.3 us -> 16.7 us
    ppermute x6, starting transfers between devices: 5.41 us -> 5.78 us  [exchange(): lax.ppermute(block, 'ez', [(i, partner(i, step, count)) for i in range(co...]
where the time goes in v9:
time: 33.5 us; the launch traced here: 33.3 us
  starting transfers between devices  16.7 us (50%)
  Pallas kernels  9.9 us (30%)
  waiting for transfers between devices  3.91 us (12%)
  local copies, waits for them, and re-layouts  1.18 us (4%)
  other arithmetic  0.81 us (2%)
  between operations  0.75 us (2%)
    ppermute x8, starting transfers between devices, shift(): lax.ppermute(block, axis, [(i, (i + distance) % count) for i in range(cou...  10.9 us
    ppermute x6, starting transfers between devices, exchange(): lax.ppermute(block, 'ez', [(i, partner(i, step, count)) for i in range(co...  5.78 us
    pallas_call x1, Pallas kernels, local(): pl.pallas_call(functools.partial(basis_kernel, margin), out_shape=[face,...  4.17 us
    pallas_call x1, Pallas kernels, local(): pl.pallas_call(functools.partial(middle_kernel, margin), out_shape=[field...  2.57 us
    ppermute x6, waiting for transfers between devices, exchange(): lax.ppermute(block, 'ez', [(i, partner(i, step, count)) for i in range(co...  2.36 us
    ppermute x8, waiting for transfers between devices, shift(): lax.ppermute(block, axis, [(i, (i + distance) % count) for i in range(cou...  1.55 us
    unnamed x2, local copies, waits for them, and re-layouts  1.17 us
    pallas_call x1, Pallas kernels, local(): pl.pallas_call(functools.partial(near_kernel, count, margin), out_shape=[...  0.8 us
  transfers between devices with their start and end apart: 14, of which 4 were waited for; matrix products, arithmetic and copies ran while one was open for 2% of the time, Pallas kernels for 15%

profile of v9, /device:TPU:0, one launch (start us, length us, event | category | flops | bytes accessed | tf_op | source)
XLA Modules:
  0.0 33.3 jit_solution(11596605995625729318)
XLA Ops:
  0.6 3.0 %collective-permute-start.3 = (f32[8,8,16]{2,1,0:T(8,128)}, f32[8,8,16]{2,1,0:T(8,128)S(1)}, u32[]{:S(2)}, u32[]{:S(2)}) collective-permute-start(f32[8,8,16]{2,1,0:T(8,128)} %bitcast.9), channel_id=1, source_target_pairs={{0,4},{4,8},{8,12},{12,16},{16,20},{20,24},{24,28},{28,0},{1,5},{5... | collective-permute-start | bytes 12296 | tf_op jit(solution)/shard_map/ppermute | solution.py:560
  3.6 0.8 %add_multiply_fusion = f32[8,8,16]{2,1,0:T(8,128)S(1)} fusion(f32[8,16,8]{1,2,0:T(8,128)} %param.2), kind=kLoop, calls=%fused_computation.1 | loop fusion | flops 2048 | bytes 8192 | tf_op jit(solution)/shard_map/mul | solution.py:578
  4.4 3.0 %collective-permute-start = (f32[2,8,16]{2,1,0:T(8,128)S(1)}, f32[2,8,16]{2,1,0:T(8,128)S(1)}, u32[]{:S(2)}, u32[]{:S(2)}) collective-permute-start(f32[2,8,16]{2,1,0:T(8,128)S(1)} %slice.24), channel_id=1, source_target_pairs={{0,28},{4,0},{8,4},{12,8},{16,12},{20,16},{24,20},{28,24},{1,29},{... | collective-permute-start | bytes 3080 | tf_op jit(solution)/shard_map/ppermute | solution.py:560
  7.5 0.0 copy-start
  7.5 1.2 %copy-done = bf16[1,1,2,1728,128]{4,3,2,1,0:T(8,128)(2,1)S(1)} copy-done((bf16[1,1,2,1728,128]{4,3,2,1,0:T(8,128)(2,1)S(1)}, bf16[1,1,2,1728,128]{4,3,2,1,0:T(8,128)(2,1)}, u32[]{:S(2)}) %copy-start) | copy-done | bytes 884760
  8.7 0.5 %first.1 = (f32[2,14,208,128]{3,2,1,0:T(8,128)S(1)}, f32[2,14,208,128]{3,2,1,0:T(8,128)S(1)}) custom-call(bf16[2,1728,128]{2,1,0:T(8,128)(2,1)S(1)} %bitcast.7), custom_call_target="tpu_custom_call" | custom-call | flops 100000 | bytes 10000 | tf_op jit(solution)/shard_map/first/pallas_call | solution.py:585
  9.1 0.0 collective-permute-done.3
  9.2 0.7 %collective-permute-start.5 = (f32[10,2,16]{2,1,0:T(2,128)S(1)}, f32[10,2,16]{2,1,0:T(2,128)S(1)}, u32[]{:S(2)}, u32[]{:S(2)}) collective-permute-start(f32[10,2,16]{2,1,0:T(2,128)S(1)} %get-tuple-element.48), channel_id=1, source_target_pairs={{0,3},{1,0},{2,1},{3,2},{4,7},{5,4},{6,5},{7,6},{8,11},{9,8},{10,9... | collective-permute-start | bytes 3848 | tf_op jit(solution)/shard_map/ppermute | solution.py:560
  9.9 0.0 collective-permute-start.4
  9.9 0.0 collective-permute-done.x_after_ref
  9.9 1.7 %collective-permute-start.2 = (f32[2,2,16]{2,1,0:T(2,128)S(1)}, f32[2,2,16]{2,1,0:T(2,128)S(1)}, u32[]{:S(2)}, u32[]{:S(2)}) collective-permute-start(f32[2,2,16]{2,1,0:T(2,128)S(1)} %get-tuple-element.50), channel_id=1, source_target_pairs={{0,3},{1,0},{2,1},{3,2},{4,7},{5,4},{6,5},{7,6},{8,11},{9,8},{10,9... | collective-permute-start | bytes 776 | tf_op jit(solution)/shard_map/ppermute | solution.py:560
  11.6 0.0 collective-permute-start.1
  11.6 0.0 collective-permute-done.5.z_after_ref
  11.6 1.3 %collective-permute-done.4.z_before_ref = f32[10,2,16]{2,1,0:T(2,128)S(1)} collective-permute-done((f32[10,2,16]{2,1,0:T(2,128)S(1)}, f32[10,2,16]{2,1,0:T(2,128)S(1)}, u32[]{:S(2)}, u32[]{:S(2)}) %collective-permute-start.4) | collective-permute-done | bytes 1312 | tf_op jit(solution)/shard_map/ppermute | solution.py:560
  13.0 2.6 %middle.1 = (f32[2,14,208,128]{3,2,1,0:T(8,128)S(1)}, f32[2,14,208,128]{3,2,1,0:T(8,128)S(1)}, f32[12,16,16,128]{3,2,1,0:T(8,128)S(1)}, bf16[2,2304,256]{2,1,0:T(8,128)(2,1)S(1)}, f32[2,128,256]{2,1,0:T(8,128)S(1)}) custom-call(f32[10,8,16]{2,1,0:T(8,128)S(1)} %pad_maximum_fusion.low_ref, ...), custom_call_target="tpu_custom_call", output_to_operand_aliasing={{0}: (3, {}), {1}: (4, {})} | custom-call | flops 100000000 | bytes 10000000 | tf_op jit(solution)/shard_map/middle/pallas_call | solution.py:603
  15.6 0.0 collective-permute-done.2.z_after_ref
  15.6 0.0 collective-permute-done.1.z_before_ref
  15.6 4.2 %basis.1 = (f32[2,128,128]{2,1,0:T(8,128)S(1)}, f32[2,128,128]{2,1,0:T(8,128)S(1)}, f32[2,128,128]{2,1,0:T(8,128)S(1)}, f32[2,128,128]{2,1,0:T(8,128)S(1)}, f32[...) custom-call(f32[2,8,16]{2,1,0:T(8,128)S(1)} %collective-permute-done, ...), custom_call_target="tpu_custom_call", output_to_operand_aliasing={{4}: (3, {}), {5}: (4, {}), {6}: (5, {}), {7}: (6, {})} | custom-call | tf_op jit(solution)/shard_map/basis/pallas_call | solution.py:617
  19.8 1.8 %collective-permute-start.9 = (f32[2,128,128]{2,1,0:T(8,128)S(1)}, f32[2,128,128]{2,1,0:T(8,128)S(1)}, u32[]{:S(2)}, u32[]{:S(2)}) collective-permute-start(f32[2,128,128]{2,1,0:T(8,128)S(1)} %get-tuple-element.41), channel_id=1, source_target_pairs={{0,28},{4,0},{8,4},{12,8},{16,12},{20,16},{24,20},{28,24},{1,29},{... | collective-permute-start | bytes 393224 | tf_op jit(solution)/shard_map/ppermute | solution.py:560
  21.5 0.6 %collective-permute-start.10 = (f32[2,128,128]{2,1,0:T(8,128)S(1)}, f32[2,128,128]{2,1,0:T(8,128)S(1)}, u32[]{:S(2)}, u32[]{:S(2)}) collective-permute-start(f32[2,128,128]{2,1,0:T(8,128)S(1)} %get-tuple-element.42), channel_id=1, source_target_pairs={{0,3},{1,0},{2,1},{3,2},{4,7},{5,4},{6,5},{7,6},{8,11},{9,8},{10,9... | collective-permute-start | bytes 393224 | tf_op jit(solution)/shard_map/ppermute | solution.py:560
  22.2 0.8 %near.1 = (f32[2,2,128,128]{3,2,1,0:T(8,128)S(1)}, f32[32,2,2,128]{3,2,1,0:T(2,128)S(1)}, f32[32,2,2,128]{3,2,1,0:T(2,128)S(1)}, f32[32,2,2,128]{3,2,1,0:T(2,128)S(1)}, f32[32,2,2,128]{3,2,1,0:T(2,128)S(1)}) custom-call(f32[2,128,128]{2,1,0:T(8,128)S(1)} %get-tuple-element.32.inverse_ref, f32[2,128,128]{2,1,0:T(8,128)S(1)} %get-tuple-element.33.raw_ref, ...), custom_call_target="tpu_custom_call" | custom-call | flops 100000000 | bytes 10000000 | tf_op jit(solution)/shard_map/near/pallas_call | solution.py:639
  23.0 1.7 %collective-permute-start.6 = (f32[32,2,2,128]{3,2,1,0:T(2,128)S(1)}, f32[32,2,2,128]{3,2,1,0:T(2,128)S(1)}, u32[]{:S(2)}, u32[]{:S(2)}) collective-permute-start(f32[32,2,2,128]{3,2,1,0:T(2,128)S(1)} %get-tuple-element.35), channel_id=1, source_target_pairs={{0,2},{1,3},{2,0},{3,1},{4,6},{5,7},{6,4},{7,5},{8,10},{9,11},{10,... | collective-permute-start | bytes 196616 | tf_op jit(solution)/shard_map/ppermute | solution.py:567
  24.7 0.0 collective-permute-start.7
  24.7 0.5 %collective-permute-start.8 = (f32[32,2,2,128]{3,2,1,0:T(2,128)S(1)}, f32[32,2,2,128]{3,2,1,0:T(2,128)S(1)}, u32[]{:S(2)}, u32[]{:S(2)}) collective-permute-start(f32[32,2,2,128]{3,2,1,0:T(2,128)S(1)} %get-tuple-element.37), channel_id=1, source_target_pairs={{0,1},{1,0},{2,3},{3,2},{4,5},{5,4},{6,7},{7,6},{8,9},{9,8},{10,11... | collective-permute-start | bytes 196616 | tf_op jit(solution)/shard_map/ppermute | solution.py:567
  25.2 0.2 collective-permute-done.9.next_x_ref
  25.4 0.0 collective-permute-done.10.next_z_ref
  25.4 0.4 %far.1 = (f32[32,2,2,128]{3,2,1,0:T(2,128)S(1)}, f32[32,2,2,128]{3,2,1,0:T(2,128)S(1)}, f32[32,2,2,128]{3,2,1,0:T(2,128)S(1)}, f32[32,2,2,128]{3,2,1,0:T(2,128)S(1)}) custom-call(f32[2,2,128,128]{3,2,1,0:T(8,128)S(1)} %get-tuple-element.40.plus_ref, f32[2,128,128]{2,1,0:T(8,128)S(1)} %collective-permute-done.9.next_x_ref, ...), custom_call_target="tpu_custom_call" | custom-call | tf_op jit(solution)/shard_map/far/pallas_call | solution.py:651
  25.8 1.6 %collective-permute-start.11 = (f32[32,2,2,128]{3,2,1,0:T(2,128)S(1)}, f32[32,2,2,128]{3,2,1,0:T(2,128)S(1)}, u32[]{:S(2)}, u32[]{:S(2)}) collective-permute-start(f32[32,2,2,128]{3,2,1,0:T(2,128)S(1)} %get-tuple-element.43), channel_id=1, source_target_pairs={{0,3},{1,2},{2,1},{3,0},{4,7},{5,6},{6,5},{7,4},{8,11},{9,10},{10,... | collective-permute-start | bytes 196616 | tf_op jit(solution)/shard_map/ppermute | solution.py:567
  27.3 2.0 %collective-permute-start.12 = (f32[32,2,2,128]{3,2,1,0:T(2,128)S(1)}, f32[32,2,2,128]{3,2,1,0:T(2,128)S(1)}, u32[]{:S(2)}, u32[]{:S(2)}) collective-permute-start(f32[32,2,2,128]{3,2,1,0:T(2,128)S(1)} %get-tuple-element.44), channel_id=1, source_target_pairs={{0,2},{1,3},{2,0},{3,1},{4,6},{5,7},{6,4},{7,5},{8,10},{9,11},{10,... | collective-permute-start | bytes 196616 | tf_op jit(solution)/shard_map/ppermute | solution.py:567
  29.3 0.0 collective-permute-done.6.refs_0_
  29.3 0.0 collective-permute-start.13
  29.3 0.0 collective-permute-done.7.refs_1_
  29.4 0.0 collective-permute-done.8.refs_2_
  29.4 0.8 %place_near.1 = (f32[32,4,2,128]{3,2,1,0:T(2,128)}, f32[32,4,3,2,128]{4,3,2,1,0:T(2,128)}) custom-call(f32[32,2,2,128]{3,2,1,0:T(2,128)S(1)} %collective-permute-done.6.refs_0_, f32[32,2,2,128]{3,2,1,0:T(2,128)S(1)} %collective-permute-done.7.refs_1_, f32[32,2,2,128]{3,2,1,0:T(2,128)S(1)} %collective-permute-done.8.refs_2_, ...), custom_call_target="tpu_custom_call" | custom-call | tf_op jit(solution)/shard_map/place_near/pallas_call | solution.py:665
  30.1 0.1 collective-permute-done.11.refs_0_
  30.3 2.2 %collective-permute-done.12.refs_1_ = f32[32,2,2,128]{3,2,1,0:T(2,128)S(1)} collective-permute-done((f32[32,2,2,128]{3,2,1,0:T(2,128)S(1)}, f32[32,2,2,128]{3,2,1,0:T(2,128)S(1)}, u32[]{:S(2)}, u32[]{:S(2)}) %collective-permute-start.12) | collective-permute-done | bytes 65568 | tf_op jit(solution)/shard_map/ppermute | solution.py:567
  32.5 0.0 collective-permute-done.13.refs_2_
  32.5 0.8 %place_far.1 = f32[32,4,3,2,128]{4,3,2,1,0:T(2,128)} custom-call(f32[32,2,2,128]{3,2,1,0:T(2,128)S(1)} %collective-permute-done.11.refs_0_, f32[32,2,2,128]{3,2,1,0:T(2,128)S(1)} %collective-permute-done.12.refs_1_, f32[32,2,2,128]{3,2,1,0:T(2,128)S(1)} %collective-permute-done.13.refs_2_, ...), custom_call_target="tpu_custom_call", output_to_operand_aliasing={{}: (4, {})} | custom-call | tf_op jit(solution)/shard_map/place_far/pallas_call | solution.py:674
  (5 shorter events, 0.0 us)
Async XLA Ops:
  0.6 8.5 %collective-permute-start.3 = (f32[8,8,16]{2,1,0:T(8,128)}, f32[8,8,16]{2,1,0:T(8,128)S(1)}, u32[]{:S(2)}, u32[]{:S(2)}) collective-permute-start(f32[8,8,16]{2,1,0:T(8,128)} %bitcast.9), channel_id=1, source_target_pairs={{0,4},{4,8},{8,12},{12,16},{16,20},{20,24},{24,28},{28,0},{1,5},{5... | collective-permute-start | bytes 12296 | tf_op jit(solution)/shard_map/ppermute | solution.py:560
  4.4 5.4 %collective-permute-start = (f32[2,8,16]{2,1,0:T(8,128)S(1)}, f32[2,8,16]{2,1,0:T(8,128)S(1)}, u32[]{:S(2)}, u32[]{:S(2)}) collective-permute-start(f32[2,8,16]{2,1,0:T(8,128)S(1)} %slice.24), channel_id=1, source_target_pairs={{0,28},{4,0},{8,4},{12,8},{16,12},{20,16},{24,20},{28,24},{1,29},{... | collective-permute-start | bytes 3080 | tf_op jit(solution)/shard_map/ppermute | solution.py:560
  7.5 1.2 %copy-start = (bf16[1,1,2,1728,128]{4,3,2,1,0:T(8,128)(2,1)S(1)}, bf16[1,1,2,1728,128]{4,3,2,1,0:T(8,128)(2,1)}, u32[]{:S(2)}) copy-start(bf16[1,1,2,1728,128]{4,3,2,1,0:T(8,128)(2,1)} %param.3) | copy-start | bytes 2654212
  9.2 2.5 %collective-permute-start.5 = (f32[10,2,16]{2,1,0:T(2,128)S(1)}, f32[10,2,16]{2,1,0:T(2,128)S(1)}, u32[]{:S(2)}, u32[]{:S(2)}) collective-permute-start(f32[10,2,16]{2,1,0:T(2,128)S(1)} %get-tuple-element.48), channel_id=1, source_target_pairs={{0,3},{1,0},{2,1},{3,2},{4,7},{5,4},{6,5},{7,6},{8,11},{9,8},{10,9... | collective-permute-start | bytes 3848 | tf_op jit(solution)/shard_map/ppermute | solution.py:560
  9.9 3.1 %collective-permute-start.4 = (f32[10,2,16]{2,1,0:T(2,128)S(1)}, f32[10,2,16]{2,1,0:T(2,128)S(1)}, u32[]{:S(2)}, u32[]{:S(2)}) collective-permute-start(f32[10,2,16]{2,1,0:T(2,128)S(1)} %get-tuple-element.49), channel_id=1, source_target_pairs={{0,1},{1,2},{2,3},{3,0},{4,5},{5,6},{6,7},{7,4},{8,9},{9,10},{10,1... | collective-permute-start | bytes 3848 | tf_op jit(solution)/shard_map/ppermute | solution.py:560
  9.9 5.7 %collective-permute-start.2 = (f32[2,2,16]{2,1,0:T(2,128)S(1)}, f32[2,2,16]{2,1,0:T(2,128)S(1)}, u32[]{:S(2)}, u32[]{:S(2)}) collective-permute-start(f32[2,2,16]{2,1,0:T(2,128)S(1)} %get-tuple-element.50), channel_id=1, source_target_pairs={{0,3},{1,0},{2,1},{3,2},{4,7},{5,4},{6,5},{7,6},{8,11},{9,8},{10,9... | collective-permute-start | bytes 776 | tf_op jit(solution)/shard_map/ppermute | solution.py:560
  11.6 3.9 %collective-permute-start.1 = (f32[2,2,16]{2,1,0:T(2,128)S(1)}, f32[2,2,16]{2,1,0:T(2,128)S(1)}, u32[]{:S(2)}, u32[]{:S(2)}) collective-permute-start(f32[2,2,16]{2,1,0:T(2,128)S(1)} %get-tuple-element.51), channel_id=1, source_target_pairs={{0,1},{1,2},{2,3},{3,0},{4,5},{5,6},{6,7},{7,4},{8,9},{9,10},{10,1... | collective-permute-start | bytes 776 | tf_op jit(solution)/shard_map/ppermute | solution.py:560
  19.8 5.6 %collective-permute-start.9 = (f32[2,128,128]{2,1,0:T(8,128)S(1)}, f32[2,128,128]{2,1,0:T(8,128)S(1)}, u32[]{:S(2)}, u32[]{:S(2)}) collective-permute-start(f32[2,128,128]{2,1,0:T(8,128)S(1)} %get-tuple-element.41), channel_id=1, source_target_pairs={{0,28},{4,0},{8,4},{12,8},{16,12},{20,16},{24,20},{28,24},{1,29},{... | collective-permute-start | bytes 393224 | tf_op jit(solution)/shard_map/ppermute | solution.py:560
  21.5 3.8 %collective-permute-start.10 = (f32[2,128,128]{2,1,0:T(8,128)S(1)}, f32[2,128,128]{2,1,0:T(8,128)S(1)}, u32[]{:S(2)}, u32[]{:S(2)}) collective-permute-start(f32[2,128,128]{2,1,0:T(8,128)S(1)} %get-tuple-element.42), channel_id=1, source_target_pairs={{0,3},{1,0},{2,1},{3,2},{4,7},{5,4},{6,5},{7,6},{8,11},{9,8},{10,9... | collective-permute-start | bytes 393224 | tf_op jit(solution)/shard_map/ppermute | solution.py:560
  23.0 6.4 %collective-permute-start.6 = (f32[32,2,2,128]{3,2,1,0:T(2,128)S(1)}, f32[32,2,2,128]{3,2,1,0:T(2,128)S(1)}, u32[]{:S(2)}, u32[]{:S(2)}) collective-permute-start(f32[32,2,2,128]{3,2,1,0:T(2,128)S(1)} %get-tuple-element.35), channel_id=1, source_target_pairs={{0,2},{1,3},{2,0},{3,1},{4,6},{5,7},{6,4},{7,5},{8,10},{9,11},{10,... | collective-permute-start | bytes 196616 | tf_op jit(solution)/shard_map/ppermute | solution.py:567
  24.7 4.7 %collective-permute-start.7 = (f32[32,2,2,128]{3,2,1,0:T(2,128)S(1)}, f32[32,2,2,128]{3,2,1,0:T(2,128)S(1)}, u32[]{:S(2)}, u32[]{:S(2)}) collective-permute-start(f32[32,2,2,128]{3,2,1,0:T(2,128)S(1)} %get-tuple-element.36), channel_id=1, source_target_pairs={{0,3},{1,2},{2,1},{3,0},{4,7},{5,6},{6,5},{7,4},{8,11},{9,10},{10,... | collective-permute-start | bytes 196616 | tf_op jit(solution)/shard_map/ppermute | solution.py:567
  24.7 4.7 %collective-permute-start.8 = (f32[32,2,2,128]{3,2,1,0:T(2,128)S(1)}, f32[32,2,2,128]{3,2,1,0:T(2,128)S(1)}, u32[]{:S(2)}, u32[]{:S(2)}) collective-permute-start(f32[32,2,2,128]{3,2,1,0:T(2,128)S(1)} %get-tuple-element.37), channel_id=1, source_target_pairs={{0,1},{1,0},{2,3},{3,2},{4,5},{5,4},{6,7},{7,6},{8,9},{9,8},{10,11... | collective-permute-start | bytes 196616 | tf_op jit(solution)/shard_map/ppermute | solution.py:567
  25.8 4.5 %collective-permute-start.11 = (f32[32,2,2,128]{3,2,1,0:T(2,128)S(1)}, f32[32,2,2,128]{3,2,1,0:T(2,128)S(1)}, u32[]{:S(2)}, u32[]{:S(2)}) collective-permute-start(f32[32,2,2,128]{3,2,1,0:T(2,128)S(1)} %get-tuple-element.43), channel_id=1, source_target_pairs={{0,3},{1,2},{2,1},{3,0},{4,7},{5,6},{6,5},{7,4},{8,11},{9,10},{10,... | collective-permute-start | bytes 196616 | tf_op jit(solution)/shard_map/ppermute | solution.py:567
  27.3 5.2 %collective-permute-start.12 = (f32[32,2,2,128]{3,2,1,0:T(2,128)S(1)}, f32[32,2,2,128]{3,2,1,0:T(2,128)S(1)}, u32[]{:S(2)}, u32[]{:S(2)}) collective-permute-start(f32[32,2,2,128]{3,2,1,0:T(2,128)S(1)} %get-tuple-element.44), channel_id=1, source_target_pairs={{0,2},{1,3},{2,0},{3,1},{4,6},{5,7},{6,4},{7,5},{8,10},{9,11},{10,... | collective-permute-start | bytes 196616 | tf_op jit(solution)/shard_map/ppermute | solution.py:567
  29.3 3.1 %collective-permute-start.13 = (f32[32,2,2,128]{3,2,1,0:T(2,128)S(1)}, f32[32,2,2,128]{3,2,1,0:T(2,128)S(1)}, u32[]{:S(2)}, u32[]{:S(2)}) collective-permute-start(f32[32,2,2,128]{3,2,1,0:T(2,128)S(1)} %get-tuple-element.45), channel_id=1, source_target_pairs={{0,1},{1,0},{2,3},{3,2},{4,5},{5,4},{6,7},{7,6},{8,9},{9,8},{10,11... | collective-permute-start | bytes 196616 | tf_op jit(solution)/shard_map/ppermute | solution.py:567
